TPU v7x, 128 devices: a whole 4x4x4 slice. The times are simulated.
128 devices in a mesh: ctx: 32 (over z, y, core), head: 4 (over x).
Axes of the slice: x: 4, y: 4, z: 4, core: 2. Of those that a mesh axis runs over, the one named last changes fastest.
Arguments:
- span_order: int32 [32, 2], replicated, may hold values from 0 to 63, as said below
- queries: bfloat16 [16384, 512], P('ctx', 'head'), may hold values from -8 to 8
- key_rows: bfloat16 [16384, 128], P('ctx'), may hold values from -8 to 8
- value_rows: bfloat16 [16384, 128], P('ctx'), may hold values from -6 to 6
- out_grads: bfloat16 [16384, 512], P('ctx', 'head'), may hold values from -6 to 6
Outputs:
- query_grad: bfloat16 [16384, 512], P('ctx', 'head')
- key_grad: bfloat16 [16384, 128], P('ctx')
- value_grad: bfloat16 [16384, 128], P('ctx')
Inputs may be any that keep to these rules, and one draw needn't show every extreme that they name: `span_order`: every span 0 to 63 stands in exactly one slot, and the two slots of a row hold spans c and 63 - c.
All inputs are finite; a program needn't handle non-finite values.
Results may differ from a plain program's by a relative error of at most 0.0079.
Values may be sent and summed in bfloat16 or wider, within the bound.
No kernel may reach another device: no remote copies, remote signals or barrier semaphores. Data moves between devices by JAX's collectives and lax.ppermute only.
A program may use at most 64 MiB of HBM per device.

v0:
```python
import jax
import jax.numpy as jnp
from jax import lax
from jax.sharding import PartitionSpec as P

DH = 128
SPAN = 256


sub_rows_most = 1024
neg_large = -1e30


def positions(flat_order, begin_at, row_count):
    row_ids = begin_at + jnp.arange(row_count, dtype=jnp.int32)
    slot_ids = row_ids // SPAN
    slot_table = jnp.arange(flat_order.shape[0], dtype=jnp.int32)
    span_id = jnp.sum(
        jnp.where(slot_ids[:, None] == slot_table[None, :], flat_order[None, :], 0), axis=1
    )
    return span_id * SPAN + row_ids % SPAN


def blockwise(step_fn, running, pieces, begin_at):
    row_count = pieces[0].shape[0]
    sub_rows = min(row_count, sub_rows_most)

    def one_turn(step_idx, inner):
        offset = step_idx * sub_rows
        sliced = tuple((lax.dynamic_slice_in_dim(member, offset, sub_rows, 0) for member in pieces))
        return step_fn(inner, sliced, begin_at + offset)

    return lax.fori_loop(0, row_count // sub_rows, one_turn, running)


def local(span_order, queries, key_rows, value_rows, out_grads):
    score_scale = DH ** (-0.5)
    head_count = queries.shape[1] // DH
    local_rows = queries.shape[0]
    total_rows = local_rows * lax.axis_size("ctx")
    flat_order = span_order.reshape(-1)
    my_pos = positions(flat_order, lax.axis_index("ctx") * local_rows, local_rows)

    def stats_step(running, pieces, begin_at):
        maxima, totals, weighted = running
        key_block, value_block = pieces
        visible = my_pos[:, None] >= positions(flat_order, begin_at, key_block.shape[0])[None, :]
        new_max, new_tot, new_wt = ([], [], [])
        scores = (
            jnp.einsum("qd,kd->qk", queries, key_block, preferred_element_type=jnp.float32)
            * score_scale
        )
        dprobs = jnp.einsum("qd,kd->qk", out_grads, value_block, preferred_element_type=jnp.float32)
        row_top = jnp.maximum(maxima[0], jnp.max(jnp.where(visible, scores, neg_large), axis=1))
        expon = jnp.where(visible, jnp.exp(scores - row_top[:, None]), 0.0)
        shrink = jnp.exp(maxima[0] - row_top)
        new_max.append(row_top)
        new_tot.append(totals[0] * shrink + jnp.sum(expon, axis=1))
        new_wt.append(weighted[0] * shrink + jnp.sum(expon * dprobs, axis=1))
        return (jnp.stack(new_max), jnp.stack(new_tot), jnp.stack(new_wt))

    stats_init = (
        jnp.full((head_count, local_rows), neg_large, jnp.float32),
        jnp.zeros((head_count, local_rows), jnp.float32),
        jnp.zeros((head_count, local_rows), jnp.float32),
    )
    gathered = None
    gathered = (
        lax.all_gather(key_rows, "ctx", axis=0, tiled=True),
        lax.all_gather(value_rows, "ctx", axis=0, tiled=True),
    )
    maxima, totals, weighted = blockwise(stats_step, stats_init, gathered, 0)
    log_norm = maxima + jnp.log(totals)
    row_delta = weighted / totals
    dq_zero = jnp.zeros((head_count, local_rows, DH), jnp.float32)

    def block_grads(key_block, value_block, begin_at):
        visible = my_pos[:, None] >= positions(flat_order, begin_at, key_block.shape[0])[None, :]
        scores = (
            jnp.einsum("qd,kd->qk", queries, key_block, preferred_element_type=jnp.float32)
            * score_scale
        )
        dprobs = jnp.einsum("qd,kd->qk", out_grads, value_block, preferred_element_type=jnp.float32)
        attn_probs = jnp.where(visible, jnp.exp(scores - log_norm[0][:, None]), 0.0)
        dscores = (attn_probs * (dprobs - row_delta[0][:, None])).astype(jnp.bfloat16)
        dq_terms = [jnp.dot(dscores, key_block, preferred_element_type=jnp.float32)]
        dscore_list = [(dscores, attn_probs.astype(jnp.bfloat16))]
        return (jnp.stack(dq_terms), dscore_list)

    def grad_step(running, pieces, begin_at):
        dq_run, term_rows = running
        key_block, value_block = pieces
        dq_terms, dscore_list = block_grads(key_block, value_block, begin_at)
        key_part = jnp.zeros((key_block.shape[0], DH), jnp.float32)
        value_part = jnp.zeros((key_block.shape[0], DH), jnp.float32)
        dscores, probs_low = dscore_list[0]
        key_part = key_part + jnp.einsum(
            "qk,qd->kd", dscores, queries, preferred_element_type=jnp.float32
        )
        value_part = value_part + jnp.einsum(
            "qk,qd->kd", probs_low, out_grads, preferred_element_type=jnp.float32
        )
        placed = lax.dynamic_update_slice_in_dim(
            term_rows, jnp.concatenate([key_part, value_part], axis=1), begin_at, 0
        )
        return (dq_run + dq_terms, placed)

    grad_init = (dq_zero, jnp.zeros((total_rows, 2 * DH), jnp.float32))
    grad_result = blockwise(grad_step, grad_init, gathered, 0)
    dq_acc, all_terms = grad_result
    summed = lax.psum_scatter(all_terms, "ctx", scatter_dimension=0, tiled=True)
    key_acc = summed[:, :DH]
    value_acc = summed[:, DH:]
    query_grad = (dq_acc[0] * score_scale).astype(jnp.bfloat16)
    key_sum, value_sum = lax.psum((key_acc, value_acc), "head")
    key_grad = (key_sum * score_scale).astype(jnp.bfloat16)
    value_grad = value_sum.astype(jnp.bfloat16)
    return (query_grad, key_grad, value_grad)


def solution(mesh):
    return jax.shard_map(
        local,
        mesh=mesh,
        in_specs=(P(), P("ctx", "head"), P("ctx", None), P("ctx", None), P("ctx", "head")),
        out_specs=(P("ctx", "head"), P("ctx", None), P("ctx", None)),
        check_vma=False,
    )
```

profile of v0, /device:TPU:0, one launch (start us, length us, event | category | flops | bytes accessed | tf_op | source)
XLA Modules:
  0.0 453.5 jit_solution(17598513300461769368)
XLA Ops:
  10.0 49.2 %all-gather.3.cloned.1.call-done = bf16[16384,128]{1,0:T(8,128)(2,1)} async-done(((bf16[512,128]{1,0:T(8,128)(2,1)}), bf16[16384,128]{1,0:T(8,128)(2,1)}) %all-gather.3.cloned.1.call-update) | async-done | bytes 4194320 | tf_op jit(solution)/shard_map/all_gather | solution.py:69
  59.2 48.0 %all-gather.5.cloned.1.call-done = bf16[16384,128]{1,0:T(8,128)(2,1)} async-done(((bf16[512,128]{1,0:T(8,128)(2,1)}), bf16[16384,128]{1,0:T(8,128)(2,1)}) %all-gather.5.cloned.1.call-update) | async-done | bytes 4194320 | tf_op jit(solution)/shard_map/all_gather | solution.py:70
  107.2 61.5 %while.40 = (s32[]{:T(128)}, f32[1,512]{1,0:T(1,128)S(1)}, f32[1,512]{1,0:T(1,128)S(1)}, f32[1,512]{1,0:T(1,128)S(1)}, s32[512]{0:T(512)S(1)}, /*index=5*/s32[32...) while((s32[]{:T(128)}, f32[1,512]{1,0:T(1,128)S(1)}, ...), condition=%wide.wide.region_6.7_spmd.clone, body=%wide.wide.region_1.6_spmd.clone.sunk | while | flops 276531200 | bytes 7688699 | solution.py:33
  108.8 1.6 fusion.104
  112.6 1.6 fusion.104
  116.5 1.6 fusion.104
  120.3 1.6 fusion.104
  124.2 1.6 fusion.104
  128.0 1.6 fusion.104
  131.9 1.6 fusion.104
  135.7 1.6 fusion.104
  139.6 1.6 fusion.104
  143.4 1.6 fusion.104
  147.3 1.6 fusion.104
  151.1 1.6 fusion.104
  155.0 1.6 fusion.104
  158.8 1.6 fusion.104
  168.7 6.0 %broadcast_in_dim.154.clone = f32[16384,256]{1,0:T(8,128)} broadcast(f32[]{:T(128)} %constant.272.clone.1), dimensions={} | broadcast | bytes 16777220 | tf_op jit(solution)/shard_map/broadcast_in_dim | solution.py:108
  174.7 112.7 %while.41 = (s32[]{:T(128)}, f32[1,512,128]{2,1,0:T(8,128)S(1)}, f32[16384,256]{1,0:T(8,128)}, s32[512]{0:T(512)S(1)}, s32[32,2]{1,0:T(8,128)}, /*index=5*/bf16[...) while((s32[]{:T(128)}, f32[1,512,128]{2,1,0:T(8,128)S(1)}, ...), condition=%wide.wide.region_9.10_spmd.clone, body=%wide.wide.region_7.9_spmd.clone.sunk | while | flops 675902464 | bytes 18643436 | solution.py:33
  288.2 114.0 %reduce-scatter.2.cloned.1.call-done = f32[512,256]{1,0:T(8,128)} async-done(((f32[16384,256]{1,0:T(8,128)}), f32[512,256]{1,0:T(8,128)}) %reduce-scatter.2.cloned.1.call-update) | async-done | bytes 524304 | tf_op jit(solution)/shard_map/reduce_scatter | solution.py:111
  402.2 1.8 fusion.40
  404.0 20.6 %all-reduce.4 = bf16[512,128]{1,0:T(8,128)(2,1)} all-reduce(f32[512,128]{1,0:T(8,128)S(1)} %get-tuple-element.701), channel_id=1, replica_groups=mesh['ctx'=32,'head'=4] {'head'}, use_global_device_ids=true, to_apply=%region_12.13 | all-reduce | flops 65536 | bytes 393216 | tf_op jit(solution)/shard_map/psum | solution.py:115
  424.6 20.7 %all-reduce.3.cloned.1.call-done = f32[512,128]{1,0:T(8,128)} async-done(((f32[512,128]{1,0:T(8,128)}), f32[512,128]{1,0:T(8,128)}) %all-reduce.3.cloned.1.call-update) | async-done | bytes 262160 | tf_op jit(solution)/shard_map/psum | solution.py:115
  445.3 1.6 multiply_convert_fusion
  (397 shorter events, 152.8 us)
Async XLA Ops:
  7.2 52.0 %all-gather.3.cloned.1.call-start = ((), (), s32[]{:S(2)}) async-start(), calls=%async_computation.1 | async-start | bytes 4325376 | tf_op jit(solution)/shard_map/all_gather | solution.py:69
  7.9 99.3 %all-gather.5.cloned.1.call-start = ((), (), s32[]{:S(2)}) async-start(), calls=%async_computation.2 | async-start | bytes 4325376 | tf_op jit(solution)/shard_map/all_gather | solution.py:70
  8.6 393.6 %reduce-scatter.2.cloned.1.call-start = ((), (), s32[]{:S(2)}) async-start(), calls=%async_computation.3 | async-start | bytes 17301504 | tf_op jit(solution)/shard_map/reduce_scatter | solution.py:111
  9.5 97.7 %copy-start.3 = (s32[32,2]{1,0:T(8,128)}, s32[32,2]{1,0:T(8,128)S(1)}, u32[]{:S(2)}) copy-start(s32[32,2]{1,0:T(8,128)S(1)} %copy.16) | copy-start | bytes 772
  107.2 1.6 copy-start
  111.0 1.6 copy-start
  114.8 1.6 copy-start
  118.7 1.6 copy-start
  122.5 1.6 copy-start
  126.4 1.6 copy-start
  130.2 1.6 copy-start
  134.1 1.6 copy-start
  137.9 1.6 copy-start
  141.8 1.6 copy-start
  145.6 1.6 copy-start
  149.5 1.6 copy-start
  153.3 1.6 copy-start
  157.2 1.6 copy-start
  161.0 1.6 copy-start
  164.9 1.6 copy-start
  168.7 6.0 %copy-start.1 = (bf16[512,128]{1,0:T(8,128)(2,1)S(1)}, bf16[512,128]{1,0:T(8,128)(2,1)}, u32[]{:S(2)}) copy-start(bf16[512,128]{1,0:T(8,128)(2,1)} %get-tuple-element.1040) | copy-start | bytes 393220
  168.7 6.0 %copy-start.2 = (bf16[512,128]{1,0:T(8,128)(2,1)S(1)}, bf16[512,128]{1,0:T(8,128)(2,1)}, u32[]{:S(2)}) copy-start(bf16[512,128]{1,0:T(8,128)(2,1)} %get-tuple-element.1041) | copy-start | bytes 393220
  287.5 157.8 %all-reduce.3.cloned.1.call-start = ((), (), s32[]{:S(2)}) async-start(), calls=%async_computation.4 | async-start | bytes 524288 | tf_op jit(solution)/shard_map/psum | solution.py:115
Sparse Core Ops, SparseCore 0:
  10.3 48.8 all-gather.2
  61.4 45.6 all-gather.4
  287.6 114.5 reduce-scatter.1
  404.4 40.8 all-reduce.2
where the time goes:
time: 456 us; the launch traced here: 453 us
  waiting for transfers between devices  233 us (51%)
  matrix products  135 us (30%)
  local copies, waits for them, and re-layouts  31.5 us (7%)
  blocking collectives  20.6 us (5%)
  other arithmetic  17.1 us (4%)
  between operations  13.9 us (3%)
    reduce_scatter x1, waiting for transfers between devices, local(): summed = lax.psum_scatter(all_terms, 'ctx', scatter_dimension=0, tiled=True)  114 us
    all_gather x1, waiting for transfers between devices, local(): lax.all_gather(key_rows, 'ctx', axis=0, tiled=True)  49.2 us
    all_gather x1, waiting for transfers between devices, local(): lax.all_gather(value_rows, 'ctx', axis=0, tiled=True)  48 us
    dot_general x16, matrix products, stats_step(): jnp.einsum('qd,kd->qk', out_grads, value_block, preferred_element_type=jn...  25.9 us
    dot_general x16, matrix products, block_grads(): jnp.einsum('qd,kd->qk', queries, key_block, preferred_element_type=jnp.fl...  24.7 us
    dot_general x16, matrix products, block_grads(): dq_terms = [jnp.dot(dscores, key_block, preferred_element_type=jnp.float32)]  23.4 us
    dot_general x16, matrix products, stats_step(): jnp.einsum('qd,kd->qk', queries, key_block, preferred_element_type=jnp.fl...  23.2 us
    dynamic_update_slice x32, local copies, waits for them, and re-layouts, grad_step(): lax.dynamic_update_slice_in_dim(term_rows, jnp.concatenate([key_part, val...  22.5 us
  transfers between devices with their start and end apart: 4, of which 4 were waited for; matrix products, arithmetic and copies ran while one was open for 0% of the time, Pallas kernels for 0%

commit v1 on v0

v1 whole, which is shorter than its diff:
```python
import functools

import jax
import jax.numpy as jnp
from jax import lax
from jax.experimental import pallas as pl
from jax.experimental.pallas import tpu as pltpu
from jax.sharding import Mesh, PartitionSpec as P

DH = 128
SPAN = 256
HALF = 32
SCALE = DH ** (-0.5)
LOG2E = 1.4426950408889634
SCALE2 = SCALE * LOG2E
NEG = -1e30
NT = (((1,), (1,)), ((), ()))
NN = (((1,), (0,)), ((), ()))
F32 = jnp.float32
BF16 = jnp.bfloat16


def low_span(order_ref, z, y, c):
    row = (z * 4 + y) * 2 + c
    return jnp.minimum(order_ref[row, 0], order_ref[row, 1])


def pair_picks(order_ref, a):
    z, y, c = lax.axis_index("z"), lax.axis_index("y"), lax.axis_index("c")
    mine = low_span(order_ref, z, (y + 4 - a % 4) % 4, (c + a // 4) % 2)
    return [
        jnp.where(mine > low_span(order_ref, (z + 4 - b) % 4, y, c), 0, 1) for b in range(4)
    ]


def half(ref, piece, which, second):
    begin = which * SPAN + second * 2 * SPAN
    if not isinstance(begin, int):
        begin = pl.multiple_of(begin, SPAN)
    return ref[piece, pl.ds(begin, SPAN), :]


def products(q_ref, kv_ref, a, q_which, b, k_which):
    scores = lax.dot_general(
        half(kv_ref, b, k_which, 0), half(q_ref, a, q_which, 0), NT, preferred_element_type=F32
    )
    dprobs = lax.dot_general(
        half(kv_ref, b, k_which, 1), half(q_ref, a, q_which, 1), NT, preferred_element_type=F32
    )
    return scores * SCALE2, dprobs


def diagonal_visible():
    key_row = lax.broadcasted_iota(jnp.int32, (SPAN, SPAN), 0)
    query_row = lax.broadcasted_iota(jnp.int32, (SPAN, SPAN), 1)
    return key_row <= query_row


def for_each_pair(order_ref, tile):
    picks = pair_picks(order_ref, 0)
    tile(0, 1, [(b, 0) for b in range(4)], False)
    for b in range(1, 4):
        tile(0, picks[b], [(b, picks[b])], False)
    tile(0, 0, [(0, 0)], True)
    tile(0, 1, [(0, 1)], True)

    def one_piece(a, carry):
        picks = pair_picks(order_ref, a)
        tile(a, 1, [(b, 0) for b in range(4)], False)
        for b in range(4):
            tile(a, picks[b], [(b, picks[b])], False)
        return carry

    lax.fori_loop(1, 8, one_piece, 0)


def stats_kernel(order_ref, q_ref, kv_ref, own_ref, swapped_ref, top_ref, total_ref, weighted_ref):
    top_ref[...] = jnp.full(top_ref.shape, NEG, F32)
    total_ref[...] = jnp.zeros(total_ref.shape, F32)
    weighted_ref[...] = jnp.zeros(weighted_ref.shape, F32)

    def tile(a, q_which, keys, masked):
        slot = a * 2 + q_which
        old = top_ref[slot]
        top = old
        parts = []
        for b, k_which in keys:
            scores, dprobs = products(q_ref, kv_ref, a, q_which, b, k_which)
            if masked:
                scores = jnp.where(diagonal_visible(), scores, NEG)
            parts.append((scores.reshape(32, 8, SPAN), dprobs.reshape(32, 8, SPAN)))
            top = jnp.maximum(top, jnp.max(parts[-1][0], axis=0))
        shrink = jnp.exp2(old - top)
        total = total_ref[slot] * shrink
        weighted = weighted_ref[slot] * shrink
        for scores, dprobs in parts:
            expon = jnp.exp2(scores - top[None])
            if masked:
                expon = jnp.where(diagonal_visible().reshape(32, 8, SPAN), expon, 0.0)
            total = total + jnp.sum(expon, axis=0)
            weighted = weighted + jnp.sum(expon * dprobs, axis=0)
        top_ref[slot] = top
        total_ref[slot] = total
        weighted_ref[slot] = weighted

    for_each_pair(order_ref, tile)
    for slot in range(16):
        tops = top_ref[slot]
        top = jnp.max(tops, axis=0, keepdims=True)
        factor = jnp.exp2(tops - top)
        rows = (
            top,
            jnp.sum(total_ref[slot] * factor, axis=0, keepdims=True),
            jnp.sum(weighted_ref[slot] * factor, axis=0, keepdims=True),
        )
        other = (slot + 8) % 16
        for kind, row in enumerate(rows):
            own_ref[kind, pl.ds(slot, 1), :] = row
            swapped_ref[kind, pl.ds(other, 1), :] = row


def grads_kernel(
    order_ref, s0_ref, s1_ref, s2_ref, s3_ref, q_ref, kv_ref,
    dkv0_ref, dkv1_ref, dkv2_ref, dkv3_ref, dq_keep_ref, dq_send_ref,
    norm_ref, delta_ref, dk_ref, dv_ref, dqt_ref, kt_ref,
):
    for a in range(8):
        dc, dy = a // 4, a % 4
        found = []
        for k, ref in enumerate((s0_ref, s1_ref, s2_ref, s3_ref)):
            begin = 2 * (4 * dc + (dy - k) % 4)
            found.append([ref[kind, pl.ds(begin, 2), :] for kind in range(3)])
        top = functools.reduce(jnp.maximum, [f[0] for f in found])
        factors = [jnp.exp2(f[0] - top) for f in found]
        total = sum(f[1] * g for f, g in zip(found, factors))
        weighted = sum(f[2] * g for f, g in zip(found, factors))
        norm = top + jnp.log2(total)
        delta = weighted / total
        for which in range(2):
            norm_ref[2 * a + which] = jnp.broadcast_to(norm[which : which + 1], (8, SPAN))
            delta_ref[2 * a + which] = jnp.broadcast_to(delta[which : which + 1], (8, SPAN))
    for b in range(4):
        for which in range(2):
            kt_ref[2 * b + which] = half(kv_ref, b, which, 0).T
    dk_ref[...] = jnp.zeros(dk_ref.shape, F32)
    dv_ref[...] = jnp.zeros(dv_ref.shape, F32)
    dqt_ref[...] = jnp.zeros(dqt_ref.shape, F32)

    def tile(a, q_which, keys, masked):
        slot = a * 2 + q_which
        norm = norm_ref[slot][None]
        delta = delta_ref[slot][None]
        queries = half(q_ref, a, q_which, 0)
        out_grads = half(q_ref, a, q_which, 1)
        dqt = None
        for b, k_which in keys:
            scores, dprobs = products(q_ref, kv_ref, a, q_which, b, k_which)
            probs = jnp.exp2(scores.reshape(32, 8, SPAN) - norm)
            if masked:
                probs = jnp.where(diagonal_visible().reshape(32, 8, SPAN), probs, 0.0)
            dscores = probs * (dprobs.reshape(32, 8, SPAN) - delta)
            probs = probs.reshape(SPAN, SPAN).astype(BF16)
            dscores = dscores.reshape(SPAN, SPAN).astype(BF16)
            key_slot = 2 * b + k_which
            dv_ref[key_slot] += lax.dot_general(probs, out_grads, NN, preferred_element_type=F32)
            dk_ref[key_slot] += lax.dot_general(dscores, queries, NN, preferred_element_type=F32)
            term = lax.dot_general(kt_ref[key_slot], dscores, NN, preferred_element_type=F32)
            dqt = term if dqt is None else dqt + term
        dqt_ref[slot] += dqt

    for_each_pair(order_ref, tile)
    for b, ref in enumerate((dkv0_ref, dkv1_ref, dkv2_ref, dkv3_ref)):
        for which in range(2):
            ref[pl.ds(which * SPAN, SPAN), :] = dk_ref[2 * b + which].astype(ref.dtype)
            ref[pl.ds((2 + which) * SPAN, SPAN), :] = dv_ref[2 * b + which].astype(ref.dtype)
    for slot in range(8):
        dq_keep_ref[pl.ds(slot * SPAN, SPAN), :] = dqt_ref[slot].T.astype(dq_keep_ref.dtype)
        dq_send_ref[pl.ds(slot * SPAN, SPAN), :] = dqt_ref[slot + 8].T.astype(dq_send_ref.dtype)


SMEM = pl.BlockSpec(memory_space=pltpu.SMEM)
VMEM = pl.BlockSpec(memory_space=pltpu.VMEM)
PIECE = 4 * SPAN


def call_stats(span_order, q_all, kv_all):
    shape = jax.ShapeDtypeStruct((3, 16, SPAN), F32)
    return pl.pallas_call(
        stats_kernel,
        out_shape=(shape, shape),
        in_specs=[SMEM, VMEM, VMEM],
        out_specs=(VMEM, VMEM),
        scratch_shapes=[pltpu.VMEM((16, 8, SPAN), F32)] * 3,
        compiler_params=pltpu.CompilerParams(vmem_limit_bytes=32 * 2**20),
        cost_estimate=pl.CostEstimate(
            flops=65 * 2 * 2 * SPAN * SPAN * DH, bytes_accessed=3 * 2**20, transcendentals=65 * SPAN * SPAN
        ),
        name="stats",
    )(span_order, q_all, kv_all)


def call_grads(span_order, stats, q_all, kv_all):
    piece = jax.ShapeDtypeStruct((PIECE, DH), BF16)
    return pl.pallas_call(
        grads_kernel,
        out_shape=(
            jax.ShapeDtypeStruct((PIECE, DH), F32), piece, piece, piece,
            jax.ShapeDtypeStruct((8 * SPAN, DH), F32),
            jax.ShapeDtypeStruct((8 * SPAN, DH), BF16),
        ),
        in_specs=[SMEM] + [VMEM] * 6,
        out_specs=(VMEM,) * 6,
        scratch_shapes=[
            pltpu.VMEM((16, 8, SPAN), F32),
            pltpu.VMEM((16, 8, SPAN), F32),
            pltpu.VMEM((8, SPAN, DH), F32),
            pltpu.VMEM((8, SPAN, DH), F32),
            pltpu.VMEM((16, DH, SPAN), F32),
            pltpu.VMEM((8, DH, SPAN), BF16),
        ],
        compiler_params=pltpu.CompilerParams(vmem_limit_bytes=40 * 2**20),
        cost_estimate=pl.CostEstimate(
            flops=65 * 5 * 2 * SPAN * SPAN * DH, bytes_accessed=6 * 2**20, transcendentals=65 * SPAN * SPAN
        ),
        name="grads",
    )(span_order, *stats, q_all, kv_all)


def back(value, axis, k):
    return lax.ppermute(value, axis, [(i, (i + k) % 4) for i in range(4)])


def ahead(value, axis, k):
    return lax.ppermute(value, axis, [(i, (i - k) % 4) for i in range(4)])


def swap_core(value):
    return lax.ppermute(value, "c", [(0, 1), (1, 0)])


def local(span_order, queries, key_rows, value_rows, out_grads):
    z, y, c = lax.axis_index("z"), lax.axis_index("y"), lax.axis_index("c")
    row = (z * 4 + y) * 2 + c
    flipped = lax.dynamic_slice(span_order, (row, 0), (1, 1))[0, 0] >= HALF

    def in_order(value):
        low, high = value[:SPAN], value[SPAN:]
        return [jnp.where(flipped, high, low), jnp.where(flipped, low, high)]

    q_own = jnp.concatenate(in_order(queries) + in_order(out_grads), axis=0)
    kv_own = jnp.concatenate(in_order(key_rows) + in_order(value_rows), axis=0)
    q_near = jnp.concatenate([q_own] + [back(q_own, "y", k) for k in (1, 2, 3)], axis=0)
    kv_all = jnp.stack([kv_own] + [back(kv_own, "z", k) for k in (1, 2, 3)])
    q_all = jnp.concatenate([q_near, swap_core(q_near)], axis=0).reshape(8, PIECE, DH)

    mine, for_other = call_stats(span_order, q_all, kv_all)
    theirs = swap_core(for_other)
    top = jnp.maximum(mine[0], theirs[0])
    mine_by, theirs_by = jnp.exp2(mine[0] - top), jnp.exp2(theirs[0] - top)
    both = jnp.stack([top, mine[1] * mine_by + theirs[1] * theirs_by, mine[2] * mine_by + theirs[2] * theirs_by])
    stats = [both] + [back(both, "y", k) for k in (1, 2, 3)]

    dkv0, dkv1, dkv2, dkv3, dq_keep, dq_send = call_grads(span_order, stats, q_all, kv_all)
    zs = [ahead(part, "z", k) for k, part in ((1, dkv1), (2, dkv2), (3, dkv3))]
    dq_other = swap_core(dq_send)

    def dq_piece(k):
        rows = slice(k * 2 * SPAN, (k + 1) * 2 * SPAN)
        return dq_keep[rows] + dq_other[rows].astype(F32)

    ys = [ahead(dq_piece(k).astype(BF16), "y", k) for k in (1, 2, 3)]
    summed = (dkv0 + sum(part.astype(F32) for part in zs)).astype(BF16)
    x1, x2, x3 = [back(summed, "x", k).astype(F32) for k in (1, 2, 3)]
    total = (summed.astype(F32) + x2) + (x1 + x3)
    dq = dq_piece(0) + sum(part.astype(F32) for part in ys)

    def out_order(value):
        return jnp.concatenate(in_order(value), axis=0).astype(BF16)

    return (
        out_order(dq * SCALE),
        out_order(total[: 2 * SPAN] * SCALE),
        out_order(total[2 * SPAN :]),
    )


def solution(mesh):
    fine = Mesh(mesh.devices.reshape(4, 4, 2, 4), ("z", "y", "c", "x"))
    ctx = ("z", "y", "c")
    return jax.shard_map(
        local,
        mesh=fine,
        in_specs=(P(), P(ctx, "x"), P(ctx, None), P(ctx, None), P(ctx, "x")),
        out_specs=(P(ctx, "x"), P(ctx, None), P(ctx, None)),
        check_vma=False,
    )
```

time: 456 us -> 133 us (0.29)
  waiting for transfers between devices: 233 us -> 54 us
  matrix products: 135 us -> 0 us
  starting transfers between devices: 0.16 us -> 29.6 us
  local copies, waits for them, and re-layouts: 31.5 us -> 2.49 us
  Pallas kernels: 0 us -> 27.8 us
  blocking collectives: 20.6 us -> 0 us
  between operations: 13.9 us -> 0.82 us
    dot_general x112 -> x0, matrix products: 135 us -> none  [the longest x16 25.9 us: stats_step(): jnp.einsum('qd,kd->qk', out_grads, value_block, preferred_element_type=jn...]
    reduce_scatter x1 -> x0, waiting for transfers between devices: 114 us -> none  [local(): summed = lax.psum_scatter(all_terms, 'ctx', scatter_dimension=0, tiled=True)]
    all_gather x2 -> x0, waiting for transfers between devices: 97.2 us -> none  [the longest x1 49.2 us: local(): lax.all_gather(key_rows, 'ctx', axis=0, tiled=True)]
    ppermute x0 -> x21, waiting for transfers between devices: none -> 54 us  [the longest x12 33.9 us: back(): return lax.ppermute(value, axis, [(i, (i + k) % 4) for i in range(4)])]
    ppermute x0 -> x21, starting transfers between devices: none -> 29.6 us  [the longest x12 22.8 us: back(): return lax.ppermute(value, axis, [(i, (i + k) % 4) for i in range(4)])]
    pallas_call x0 -> x2, Pallas kernels: none -> 27.8 us  [the longest x1 18.1 us: call_grads(): pl.pallas_call(grads_kernel, out_shape=(jax.ShapeDtypeStruct((PIECE, DH),...]
    dynamic_update_slice x32 -> x0, local copies, waits for them, and re-layouts: 22.5 us -> none  [grad_step(): lax.dynamic_update_slice_in_dim(term_rows, jnp.concatenate([key_part, val...]
    psum x1 -> x0, waiting for transfers between devices: 20.7 us -> none  [local(): key_sum, value_sum = lax.psum((key_acc, value_acc), 'head')]
  transfers between devices with their start and end apart: 4 -> 21, of which waited for: 4 -> 17; matrix products, arithmetic and copies ran while one was open for 0% -> 5% of each run, Pallas kernels for 0% -> 0%
where the time goes in v1:
time: 133 us; the launch traced here: 132 us
  waiting for transfers between devices  54 us (41%)
  starting transfers between devices  29.6 us (22%)
  Pallas kernels  27.8 us (21%)
  other arithmetic  17.1 us (13%)
  local copies, waits for them, and re-layouts  2.49 us (2%)
    ppermute x12, waiting for transfers between devices, back(): return lax.ppermute(value, axis, [(i, (i + k) % 4) for i in range(4)])  33.9 us
    ppermute x12, starting transfers between devices, back(): return lax.ppermute(value, axis, [(i, (i + k) % 4) for i in range(4)])  22.8 us
    ppermute x6, waiting for transfers between devices, ahead(): return lax.ppermute(value, axis, [(i, (i - k) % 4) for i in range(4)])  18.9 us
    pallas_call x1, Pallas kernels, call_grads(): pl.pallas_call(grads_kernel, out_shape=(jax.ShapeDtypeStruct((PIECE, DH),...  18.1 us
    pallas_call x1, Pallas kernels, call_stats(): pl.pallas_call(stats_kernel, out_shape=(shape, shape), in_specs=[SMEM, VM...  9.76 us
    unnamed x4, other arithmetic  8.69 us
    ppermute x6, starting transfers between devices, ahead(): return lax.ppermute(value, axis, [(i, (i - k) % 4) for i in range(4)])  6.78 us
  transfers between devices with their start and end apart: 21, of which 17 were waited for; matrix products, arithmetic and copies ran while one was open for 5% of the time, Pallas kernels for 0%

profile of v1, /device:TPU:0, one launch (start us, length us, event | category | flops | bytes accessed | tf_op | source)
XLA Modules:
  0.0 131.9 jit_solution(7561928641822713179)
XLA Ops:
  1.9 2.2 %constant_dynamic-update-slice_fusion.6 = (bf16[4096,128]{1,0:T(8,128)(2,1)}, bf16[256,128]{1,0:T(8,128)(2,1)S(1)}) fusion(bf16[512,128]{1,0:T(8,128)(2,1)} %param.6, pred[]{:T(512)} %bitcast), kind=kLoop, calls=%fused_computation.34 | loop fusion | flops 32767 | bytes 262145
  4.1 2.2 %constant_dynamic-update-slice_fusion.5 = (bf16[4096,128]{1,0:T(8,128)(2,1)}, bf16[256,128]{1,0:T(8,128)(2,1)S(1)}) fusion(bf16[4096,128]{1,0:T(8,128)(2,1)} %get-tuple-element.27, bf16[512,128]{1,0:T(8,128)(2,1)} %param.6, pred[]{:T(512)} %bitcast), kind=kLoop, calls=%fused_computation.33 | loop fusion | flops 32768 | bytes 262656
  6.3 2.2 %constant_dynamic-update-slice_fusion.4 = (bf16[4096,128]{1,0:T(8,128)(2,1)}, bf16[256,128]{1,0:T(8,128)(2,1)S(1)}) fusion(bf16[4096,128]{1,0:T(8,128)(2,1)} %get-tuple-element.25, bf16[512,128]{1,0:T(8,128)(2,1)} %param.9, pred[]{:T(512)} %bitcast), kind=kLoop, calls=%fused_computation.32 | loop fusion | flops 32768 | bytes 262656
  8.4 2.2 %constant_dynamic-update-slice_fusion.3 = (bf16[4096,128]{1,0:T(8,128)(2,1)}, bf16[256,128]{1,0:T(8,128)(2,1)S(1)}) fusion(bf16[4096,128]{1,0:T(8,128)(2,1)} %get-tuple-element.23, bf16[512,128]{1,0:T(8,128)(2,1)} %param.9, pred[]{:T(512)} %bitcast), kind=kLoop, calls=%fused_computation.31 | loop fusion | flops 32768 | bytes 262656
  12.4 2.9 %collective-permute-start.1 = (bf16[1024,128]{1,0:T(8,128)(2,1)S(1)}, bf16[1024,128]{1,0:T(8,128)(2,1)S(1)}, u32[]{:S(2)}, u32[]{:S(2)}) collective-permute-start(bf16[1024,128]{1,0:T(8,128)(2,1)S(1)} %pad_maximum_fusion.1), channel_id=1, source_target_pairs={{0,16},{8,24},{16,0},{24,8},{1,17},{9,25},{17,1},{25,9},{2,18},{10... | collective-permute-start | bytes 786440 | tf_op jit(solution)/shard_map/ppermute | solution.py:230
  16.7 3.4 %collective-permute-done = bf16[1024,128]{1,0:T(8,128)(2,1)S(1)} collective-permute-done((bf16[1024,128]{1,0:T(8,128)(2,1)S(1)}, bf16[1024,128]{1,0:T(8,128)(2,1)S(1)}, u32[]{:S(2)}, u32[]{:S(2)}) %collective-permute-start) | collective-permute-done | bytes 262176 | tf_op jit(solution)/shard_map/ppermute | solution.py:230
  20.8 6.1 %collective-permute-done.1 = bf16[1024,128]{1,0:T(8,128)(2,1)S(1)} collective-permute-done((bf16[1024,128]{1,0:T(8,128)(2,1)S(1)}, bf16[1024,128]{1,0:T(8,128)(2,1)S(1)}, u32[]{:S(2)}, u32[]{:S(2)}) %collective-permute-start.1) | collective-permute-done | bytes 262176 | tf_op jit(solution)/shard_map/ppermute | solution.py:230
  30.5 1.9 %collective-permute-start.4 = (bf16[1024,128]{1,0:T(8,128)(2,1)}, bf16[1024,128]{1,0:T(8,128)(2,1)}, u32[]{:S(2)}, u32[]{:S(2)}) collective-permute-start(bf16[1024,128]{1,0:T(8,128)(2,1)} %get-tuple-element.35), channel_id=1, source_target_pairs={{0,32},{32,64},{64,96},{96,0},{1,33},{33,65},{65,97},{97,1},{2,34}... | collective-permute-start | bytes 786440 | tf_op jit(solution)/shard_map/ppermute | solution.py:230
  32.4 3.6 %collective-permute-start.5 = (bf16[1024,128]{1,0:T(8,128)(2,1)}, bf16[1024,128]{1,0:T(8,128)(2,1)}, u32[]{:S(2)}, u32[]{:S(2)}) collective-permute-start(bf16[1024,128]{1,0:T(8,128)(2,1)} %get-tuple-element.35), channel_id=1, source_target_pairs={{0,64},{32,96},{64,0},{96,32},{1,65},{33,97},{65,1},{97,33},{2,66}... | collective-permute-start | bytes 786440 | tf_op jit(solution)/shard_map/ppermute | solution.py:230
  37.1 4.7 %collective-permute-done.4 = bf16[1024,128]{1,0:T(8,128)(2,1)} collective-permute-done((bf16[1024,128]{1,0:T(8,128)(2,1)}, bf16[1024,128]{1,0:T(8,128)(2,1)}, u32[]{:S(2)}, u32[]{:S(2)}) %collective-permute-start.4) | collective-permute-done | bytes 262176 | tf_op jit(solution)/shard_map/ppermute | solution.py:230
  41.8 6.8 %collective-permute-done.5 = bf16[1024,128]{1,0:T(8,128)(2,1)} collective-permute-done((bf16[1024,128]{1,0:T(8,128)(2,1)}, bf16[1024,128]{1,0:T(8,128)(2,1)}, u32[]{:S(2)}, u32[]{:S(2)}) %collective-permute-start.5) | collective-permute-done | bytes 262176 | tf_op jit(solution)/shard_map/ppermute | solution.py:230
  50.0 9.8 %stats.1 = (f32[3,16,256]{2,1,0:T(8,128)S(1)}, f32[3,16,256]{2,1,0:T(8,128)S(1)}) custom-call(s32[32,2]{1,0:T(8,128)S(1)} %copy.9.order_ref, bf16[8,1024,128]{2,1,0:T(8,128)(2,1)S(1)} %bitcast.7, bf16[4,1024,128]{2,1,0:T(8,128)(2,1)S(1)} %pad_maximum_fusion.kv_ref), custom_call_target="tpu_custom_call" | custom-call | flops 2181038080 | bytes 3145728 | tf_op jit(solution)/shard_map/stats/pallas_call | solution.py:188
  65.3 2.9 %collective-permute-done.8.s1_ref = f32[3,16,256]{2,1,0:T(8,128)S(1)} collective-permute-done((f32[3,16,256]{2,1,0:T(8,128)S(1)}, f32[3,16,256]{2,1,0:T(8,128)S(1)}, u32[]{:S(2)}, u32[]{:S(2)}) %collective-permute-start.8) | collective-permute-done | bytes 49184 | tf_op jit(solution)/shard_map/ppermute | solution.py:230
  68.8 18.1 %grads.1 = (f32[1024,128]{1,0:T(8,128)S(1)}, bf16[1024,128]{1,0:T(8,128)(2,1)S(1)}, bf16[1024,128]{1,0:T(8,128)(2,1)S(1)}, bf16[1024,128]{1,0:T(8,128)(2,1)S(1)}...) custom-call(s32[32,2]{1,0:T(8,128)S(1)} %copy.9.order_ref, f32[3,16,256]{2,1,0:T(8,128)S(1)} %pad_maximum_fusion.6.s0_ref, ...), custom_call_target="tpu_custom_call" | custom-call | flops 5452595200 | bytes 6291456 | tf_op jit(solution)/shard_map/grads/pallas_call | solution.py:204
  86.9 2.1 %collective-permute-start.15 = (bf16[1024,128]{1,0:T(8,128)(2,1)S(1)}, bf16[1024,128]{1,0:T(8,128)(2,1)S(1)}, u32[]{:S(2)}, u32[]{:S(2)}) collective-permute-start(bf16[1024,128]{1,0:T(8,128)(2,1)S(1)} %get-tuple-element.16), channel_id=1, source_target_pairs={{0,96},{32,0},{64,32},{96,64},{1,97},{33,1},{65,33},{97,65},{2,98}... | collective-permute-start | bytes 786440 | tf_op jit(solution)/shard_map/ppermute | solution.py:234
  90.6 8.5 %collective-permute-done.15 = bf16[1024,128]{1,0:T(8,128)(2,1)S(1)} collective-permute-done((bf16[1024,128]{1,0:T(8,128)(2,1)S(1)}, bf16[1024,128]{1,0:T(8,128)(2,1)S(1)}, u32[]{:S(2)}, u32[]{:S(2)}) %collective-permute-start.15) | collective-permute-done | bytes 262176 | tf_op jit(solution)/shard_map/ppermute | solution.py:234
  99.8 3.0 %collective-permute-done.17 = bf16[1024,128]{1,0:T(8,128)(2,1)S(1)} collective-permute-done((bf16[1024,128]{1,0:T(8,128)(2,1)S(1)}, bf16[1024,128]{1,0:T(8,128)(2,1)S(1)}, u32[]{:S(2)}, u32[]{:S(2)}) %collective-permute-start.17) | collective-permute-done | bytes 262176 | tf_op jit(solution)/shard_map/ppermute | solution.py:234
  102.9 3.1 %collective-permute-start.18 = (bf16[1024,128]{1,0:T(8,128)(2,1)S(1)}, bf16[1024,128]{1,0:T(8,128)(2,1)S(1)}, u32[]{:S(2)}, u32[]{:S(2)}) collective-permute-start(bf16[1024,128]{1,0:T(8,128)(2,1)S(1)} %add_convert_fusion), channel_id=1, source_target_pairs={{0,2},{1,3},{2,0},{3,1},{4,6},{5,7},{6,4},{7,5},{8,10},{9,11},{10,... | collective-permute-start | bytes 786440 | tf_op jit(solution)/shard_map/ppermute | solution.py:230
  106.6 2.6 %collective-permute-start.20 = (bf16[1024,128]{1,0:T(8,128)(2,1)S(1)}, bf16[1024,128]{1,0:T(8,128)(2,1)S(1)}, u32[]{:S(2)}, u32[]{:S(2)}) collective-permute-start(bf16[1024,128]{1,0:T(8,128)(2,1)S(1)} %add_convert_fusion), channel_id=1, source_target_pairs={{0,3},{1,0},{2,1},{3,2},{4,7},{5,4},{6,5},{7,6},{8,11},{9,8},{10,9... | collective-permute-start | bytes 786440 | tf_op jit(solution)/shard_map/ppermute | solution.py:230
  109.2 4.5 %collective-permute-done.18 = bf16[1024,128]{1,0:T(8,128)(2,1)S(1)} collective-permute-done((bf16[1024,128]{1,0:T(8,128)(2,1)S(1)}, bf16[1024,128]{1,0:T(8,128)(2,1)S(1)}, u32[]{:S(2)}, u32[]{:S(2)}) %collective-permute-start.18) | collective-permute-done | bytes 262176 | tf_op jit(solution)/shard_map/ppermute | solution.py:230
  113.7 4.5 %collective-permute-done.19 = bf16[1024,128]{1,0:T(8,128)(2,1)S(1)} collective-permute-done((bf16[1024,128]{1,0:T(8,128)(2,1)S(1)}, bf16[1024,128]{1,0:T(8,128)(2,1)S(1)}, u32[]{:S(2)}, u32[]{:S(2)}) %collective-permute-start.19) | collective-permute-done | bytes 262176 | tf_op jit(solution)/shard_map/ppermute | solution.py:230
  119.3 2.1 %collective-permute-start.12 = (bf16[512,128]{1,0:T(8,128)(2,1)S(1)}, bf16[512,128]{1,0:T(8,128)(2,1)S(1)}, u32[]{:S(2)}, u32[]{:S(2)}) collective-permute-start(bf16[512,128]{1,0:T(8,128)(2,1)S(1)} %get-tuple-element.29), channel_id=1, source_target_pairs={{0,24},{8,0},{16,8},{24,16},{1,25},{9,1},{17,9},{25,17},{2,26},{10... | collective-permute-start | bytes 393224 | tf_op jit(solution)/shard_map/ppermute | solution.py:234
  123.7 3.4 %collective-permute-done.12 = bf16[512,128]{1,0:T(8,128)(2,1)S(1)} collective-permute-done((bf16[512,128]{1,0:T(8,128)(2,1)S(1)}, bf16[512,128]{1,0:T(8,128)(2,1)S(1)}, u32[]{:S(2)}, u32[]{:S(2)}) %collective-permute-start.12) | collective-permute-done | bytes 131104 | tf_op jit(solution)/shard_map/ppermute | solution.py:234
  127.1 2.2 %collective-permute-done.13 = bf16[512,128]{1,0:T(8,128)(2,1)S(1)} collective-permute-done((bf16[512,128]{1,0:T(8,128)(2,1)S(1)}, bf16[512,128]{1,0:T(8,128)(2,1)S(1)}, u32[]{:S(2)}, u32[]{:S(2)}) %collective-permute-start.13) | collective-permute-done | bytes 131104 | tf_op jit(solution)/shard_map/ppermute | solution.py:234
  (58 shorter events, 26.2 us)
Async XLA Ops:
  4.1 24.3 %copy-start = (bf16[512,128]{1,0:T(8,128)(2,1)S(1)}, bf16[512,128]{1,0:T(8,128)(2,1)}, u32[]{:S(2)}) copy-start(bf16[512,128]{1,0:T(8,128)(2,1)} %param.7) | copy-start | bytes 393220
  6.3 22.8 %copy-start.1 = (bf16[512,128]{1,0:T(8,128)(2,1)S(1)}, bf16[512,128]{1,0:T(8,128)(2,1)}, u32[]{:S(2)}) copy-start(bf16[512,128]{1,0:T(8,128)(2,1)} %param.8) | copy-start | bytes 393220
  10.6 26.3 %copy-start.2 = (s32[32,2]{0,1:T(2,128)S(1)}, s32[32,2]{0,1:T(2,128)}, u32[]{:S(2)}) copy-start(s32[32,2]{0,1:T(2,128)} %param.5) | copy-start | bytes 772
  10.6 9.5 %collective-permute-start = (bf16[1024,128]{1,0:T(8,128)(2,1)S(1)}, bf16[1024,128]{1,0:T(8,128)(2,1)S(1)}, u32[]{:S(2)}, u32[]{:S(2)}) collective-permute-start(bf16[1024,128]{1,0:T(8,128)(2,1)S(1)} %pad_maximum_fusion.1), channel_id=1, source_target_pairs={{0,8},{8,16},{16,24},{24,0},{1,9},{9,17},{17,25},{25,1},{2,10},{10... | collective-permute-start | bytes 786440 | tf_op jit(solution)/shard_map/ppermute | solution.py:230
  12.4 14.5 %collective-permute-start.1 = (bf16[1024,128]{1,0:T(8,128)(2,1)S(1)}, bf16[1024,128]{1,0:T(8,128)(2,1)S(1)}, u32[]{:S(2)}, u32[]{:S(2)}) collective-permute-start(bf16[1024,128]{1,0:T(8,128)(2,1)S(1)} %pad_maximum_fusion.1), channel_id=1, source_target_pairs={{0,16},{8,24},{16,0},{24,8},{1,17},{9,25},{17,1},{25,9},{2,18},{10... | collective-permute-start | bytes 786440 | tf_op jit(solution)/shard_map/ppermute | solution.py:230
  15.3 12.4 %collective-permute-start.2 = (bf16[1024,128]{1,0:T(8,128)(2,1)S(1)}, bf16[1024,128]{1,0:T(8,128)(2,1)S(1)}, u32[]{:S(2)}, u32[]{:S(2)}) collective-permute-start(bf16[1024,128]{1,0:T(8,128)(2,1)S(1)} %pad_maximum_fusion.1), channel_id=1, source_target_pairs={{0,24},{8,0},{16,8},{24,16},{1,25},{9,1},{17,9},{25,17},{2,26},{10... | collective-permute-start | bytes 786440 | tf_op jit(solution)/shard_map/ppermute | solution.py:230
  28.4 21.5 %collective-permute-start.3 = (bf16[4096,128]{1,0:T(8,128)(2,1)}, bf16[4096,128]{1,0:T(8,128)(2,1)S(1)}, u32[]{:S(2)}, u32[]{:S(2)}) collective-permute-start(bf16[4096,128]{1,0:T(8,128)(2,1)} %get-tuple-element.36), channel_id=1, source_target_pairs={{0,4},{4,0},{1,5},{5,1},{2,6},{6,2},{3,7},{7,3},{8,12},{12,8},{9,1... | collective-permute-start | bytes 3145736 | tf_op jit(solution)/shard_map/ppermute | solution.py:238
  30.5 11.3 %collective-permute-start.4 = (bf16[1024,128]{1,0:T(8,128)(2,1)}, bf16[1024,128]{1,0:T(8,128)(2,1)}, u32[]{:S(2)}, u32[]{:S(2)}) collective-permute-start(bf16[1024,128]{1,0:T(8,128)(2,1)} %get-tuple-element.35), channel_id=1, source_target_pairs={{0,32},{32,64},{64,96},{96,0},{1,33},{33,65},{65,97},{97,1},{2,34}... | collective-permute-start | bytes 786440 | tf_op jit(solution)/shard_map/ppermute | solution.py:230
  32.4 16.2 %collective-permute-start.5 = (bf16[1024,128]{1,0:T(8,128)(2,1)}, bf16[1024,128]{1,0:T(8,128)(2,1)}, u32[]{:S(2)}, u32[]{:S(2)}) collective-permute-start(bf16[1024,128]{1,0:T(8,128)(2,1)} %get-tuple-element.35), channel_id=1, source_target_pairs={{0,64},{32,96},{64,0},{96,32},{1,65},{33,97},{65,1},{97,33},{2,66}... | collective-permute-start | bytes 786440 | tf_op jit(solution)/shard_map/ppermute | solution.py:230
  36.0 12.6 %collective-permute-start.6 = (bf16[1024,128]{1,0:T(8,128)(2,1)}, bf16[1024,128]{1,0:T(8,128)(2,1)}, u32[]{:S(2)}, u32[]{:S(2)}) collective-permute-start(bf16[1024,128]{1,0:T(8,128)(2,1)} %get-tuple-element.35), channel_id=1, source_target_pairs={{0,96},{32,0},{64,32},{96,64},{1,97},{33,1},{65,33},{97,65},{2,98}... | collective-permute-start | bytes 786440 | tf_op jit(solution)/shard_map/ppermute | solution.py:230
  59.7 1.3 collective-permute-start.7
  61.1 4.2 %collective-permute-start.10 = (f32[3,16,256]{2,1,0:T(8,128)S(1)}, f32[3,16,256]{2,1,0:T(8,128)S(1)}, u32[]{:S(2)}, u32[]{:S(2)}) collective-permute-start(f32[3,16,256]{2,1,0:T(8,128)S(1)} %pad_maximum_fusion.6.s0_ref), channel_id=1, source_target_pairs={{0,24},{8,0},{16,8},{24,16},{1,25},{9,1},{17,9},{25,17},{2,26},{10... | collective-permute-start | bytes 147464 | tf_op jit(solution)/shard_map/ppermute | solution.py:230
  62.6 5.6 %collective-permute-start.8 = (f32[3,16,256]{2,1,0:T(8,128)S(1)}, f32[3,16,256]{2,1,0:T(8,128)S(1)}, u32[]{:S(2)}, u32[]{:S(2)}) collective-permute-start(f32[3,16,256]{2,1,0:T(8,128)S(1)} %pad_maximum_fusion.6.s0_ref), channel_id=1, source_target_pairs={{0,8},{8,16},{16,24},{24,0},{1,9},{9,17},{17,25},{25,1},{2,10},{10... | collective-permute-start | bytes 147464 | tf_op jit(solution)/shard_map/ppermute | solution.py:230
  63.2 5.6 %collective-permute-start.9 = (f32[3,16,256]{2,1,0:T(8,128)S(1)}, f32[3,16,256]{2,1,0:T(8,128)S(1)}, u32[]{:S(2)}, u32[]{:S(2)}) collective-permute-start(f32[3,16,256]{2,1,0:T(8,128)S(1)} %pad_maximum_fusion.6.s0_ref), channel_id=1, source_target_pairs={{0,16},{8,24},{16,0},{24,8},{1,17},{9,25},{17,1},{25,9},{2,18},{10... | collective-permute-start | bytes 147464 | tf_op jit(solution)/shard_map/ppermute | solution.py:230
  86.9 12.2 %collective-permute-start.15 = (bf16[1024,128]{1,0:T(8,128)(2,1)S(1)}, bf16[1024,128]{1,0:T(8,128)(2,1)S(1)}, u32[]{:S(2)}, u32[]{:S(2)}) collective-permute-start(bf16[1024,128]{1,0:T(8,128)(2,1)S(1)} %get-tuple-element.16), channel_id=1, source_target_pairs={{0,96},{32,0},{64,32},{96,64},{1,97},{33,1},{65,33},{97,65},{2,98}... | collective-permute-start | bytes 786440 | tf_op jit(solution)/shard_map/ppermute | solution.py:234
  89.0 10.8 %collective-permute-start.16 = (bf16[1024,128]{1,0:T(8,128)(2,1)S(1)}, bf16[1024,128]{1,0:T(8,128)(2,1)S(1)}, u32[]{:S(2)}, u32[]{:S(2)}) collective-permute-start(bf16[1024,128]{1,0:T(8,128)(2,1)S(1)} %get-tuple-element.17), channel_id=1, source_target_pairs={{0,64},{32,96},{64,0},{96,32},{1,65},{33,97},{65,1},{97,33},{2,66}... | collective-permute-start | bytes 786440 | tf_op jit(solution)/shard_map/ppermute | solution.py:234
  90.2 12.6 %collective-permute-start.17 = (bf16[1024,128]{1,0:T(8,128)(2,1)S(1)}, bf16[1024,128]{1,0:T(8,128)(2,1)S(1)}, u32[]{:S(2)}, u32[]{:S(2)}) collective-permute-start(bf16[1024,128]{1,0:T(8,128)(2,1)S(1)} %get-tuple-element.18), channel_id=1, source_target_pairs={{0,32},{32,64},{64,96},{96,0},{1,33},{33,65},{65,97},{97,1},{2,34}... | collective-permute-start | bytes 786440 | tf_op jit(solution)/shard_map/ppermute | solution.py:234
  102.9 10.8 %collective-permute-start.18 = (bf16[1024,128]{1,0:T(8,128)(2,1)S(1)}, bf16[1024,128]{1,0:T(8,128)(2,1)S(1)}, u32[]{:S(2)}, u32[]{:S(2)}) collective-permute-start(bf16[1024,128]{1,0:T(8,128)(2,1)S(1)} %add_convert_fusion), channel_id=1, source_target_pairs={{0,2},{1,3},{2,0},{3,1},{4,6},{5,7},{6,4},{7,5},{8,10},{9,11},{10,... | collective-permute-start | bytes 786440 | tf_op jit(solution)/shard_map/ppermute | solution.py:230
  106.0 12.2 %collective-permute-start.19 = (bf16[1024,128]{1,0:T(8,128)(2,1)S(1)}, bf16[1024,128]{1,0:T(8,128)(2,1)S(1)}, u32[]{:S(2)}, u32[]{:S(2)}) collective-permute-start(bf16[1024,128]{1,0:T(8,128)(2,1)S(1)} %add_convert_fusion), channel_id=1, source_target_pairs={{0,1},{1,2},{2,3},{3,0},{4,5},{5,6},{6,7},{7,4},{8,9},{9,10},{10,1... | collective-permute-start | bytes 786440 | tf_op jit(solution)/shard_map/ppermute | solution.py:230
  106.6 11.7 %collective-permute-start.20 = (bf16[1024,128]{1,0:T(8,128)(2,1)S(1)}, bf16[1024,128]{1,0:T(8,128)(2,1)S(1)}, u32[]{:S(2)}, u32[]{:S(2)}) collective-permute-start(bf16[1024,128]{1,0:T(8,128)(2,1)S(1)} %add_convert_fusion), channel_id=1, source_target_pairs={{0,3},{1,0},{2,1},{3,2},{4,7},{5,4},{6,5},{7,6},{8,11},{9,8},{10,9... | collective-permute-start | bytes 786440 | tf_op jit(solution)/shard_map/ppermute | solution.py:230
  109.2 9.9 %collective-permute-start.11 = (bf16[2048,128]{1,0:T(8,128)(2,1)S(1)}, bf16[2048,128]{1,0:T(8,128)(2,1)S(1)}, u32[]{:S(2)}, u32[]{:S(2)}) collective-permute-start(bf16[2048,128]{1,0:T(8,128)(2,1)S(1)} %get-tuple-element.14), channel_id=1, source_target_pairs={{0,4},{4,0},{1,5},{5,1},{2,6},{6,2},{3,7},{7,3},{8,12},{12,8},{9,1... | collective-permute-start | bytes 1572872 | tf_op jit(solution)/shard_map/ppermute | solution.py:238
  119.3 7.8 %collective-permute-start.12 = (bf16[512,128]{1,0:T(8,128)(2,1)S(1)}, bf16[512,128]{1,0:T(8,128)(2,1)S(1)}, u32[]{:S(2)}, u32[]{:S(2)}) collective-permute-start(bf16[512,128]{1,0:T(8,128)(2,1)S(1)} %get-tuple-element.29), channel_id=1, source_target_pairs={{0,24},{8,0},{16,8},{24,16},{1,25},{9,1},{17,9},{25,17},{2,26},{10... | collective-permute-start | bytes 393224 | tf_op jit(solution)/shard_map/ppermute | solution.py:234
  121.4 7.9 %collective-permute-start.13 = (bf16[512,128]{1,0:T(8,128)(2,1)S(1)}, bf16[512,128]{1,0:T(8,128)(2,1)S(1)}, u32[]{:S(2)}, u32[]{:S(2)}) collective-permute-start(bf16[512,128]{1,0:T(8,128)(2,1)S(1)} %get-tuple-element.31), channel_id=1, source_target_pairs={{0,16},{8,24},{16,0},{24,8},{1,17},{9,25},{17,1},{25,9},{2,18},{10... | collective-permute-start | bytes 393224 | tf_op jit(solution)/shard_map/ppermute | solution.py:234
  121.4 9.1 %collective-permute-start.14 = (bf16[512,128]{1,0:T(8,128)(2,1)S(1)}, bf16[512,128]{1,0:T(8,128)(2,1)S(1)}, u32[]{:S(2)}, u32[]{:S(2)}) collective-permute-start(bf16[512,128]{1,0:T(8,128)(2,1)S(1)} %get-tuple-element.30), channel_id=1, source_target_pairs={{0,8},{8,16},{16,24},{24,0},{1,9},{9,17},{17,25},{25,1},{2,10},{10... | collective-permute-start | bytes 393224 | tf_op jit(solution)/shard_map/ppermute | solution.py:234

commit v2 on v1

v2 whole, which is shorter than its diff:
```python
import functools

import jax
import jax.numpy as jnp
from jax import lax
from jax.experimental import pallas as pl
from jax.experimental.pallas import tpu as pltpu
from jax.sharding import Mesh, PartitionSpec as P

DH = 128
SPAN = 256
SCALE = DH ** (-0.5)
LOG2E = 1.4426950408889634
SCALE2 = SCALE * LOG2E
NEG = -1e30
NT = (((1,), (1,)), ((), ()))
NN = (((1,), (0,)), ((), ()))
F32 = jnp.float32
BF16 = jnp.bfloat16


def spans_of(order_ref, z, y, c):
    row = (z * 4 + y) * 2 + c
    first, second = order_ref[row, 0], order_ref[row, 1]
    return jnp.minimum(first, second), jnp.where(first < second, 0, 1)


def query_spans(order_ref, a):
    z, y, c = lax.axis_index("z"), lax.axis_index("y"), lax.axis_index("c")
    return spans_of(order_ref, z, (y + 4 - a % 4) % 4, (c + a // 4) % 2)


def key_spans(order_ref, b):
    z, y, c = lax.axis_index("z"), lax.axis_index("y"), lax.axis_index("c")
    return spans_of(order_ref, (z + 4 - b) % 4, y, c)


def one_query_piece(order_ref, tile, a, pieces, own):
    low, low_slot = query_spans(order_ref, a)
    found = [key_spans(order_ref, b) for b in pieces]
    tile(a, 1 - low_slot, [(b, slot) for b, (_, slot) in zip(pieces, found)], False)
    for b, (key_low, key_slot) in zip(pieces, found):
        if own and b == 0:
            tile(0, 0, [(0, 0)], True)
            tile(0, 1, [(0, 1)], True)
        else:
            lows = low > key_low
            tile(a, jnp.where(lows, low_slot, 1 - low_slot), [(b, jnp.where(lows, key_slot, 1 - key_slot))], False)


def half(ref, piece, which, second):
    begin = which * SPAN + second * 2 * SPAN
    if not isinstance(begin, int):
        begin = pl.multiple_of(begin, SPAN)
    return ref[piece, pl.ds(begin, SPAN), :]


def products(q_ref, kv_ref, a, q_which, b, k_which):
    scores = lax.dot_general(
        half(kv_ref, b, k_which, 0), half(q_ref, a, q_which, 0), NT, preferred_element_type=F32
    )
    dprobs = lax.dot_general(
        half(kv_ref, b, k_which, 1), half(q_ref, a, q_which, 1), NT, preferred_element_type=F32
    )
    return scores * SCALE2, dprobs


def diagonal_visible():
    key_row = lax.broadcasted_iota(jnp.int32, (SPAN, SPAN), 0)
    query_row = lax.broadcasted_iota(jnp.int32, (SPAN, SPAN), 1)
    return key_row <= query_row


def stats_kernel(
    order_ref, near_ref, far_ref, kv0_ref, kv1_ref, kv2_ref, kv3_ref, own_ref, swapped_ref,
    q_ref, kv_ref, top_ref, total_ref, weighted_ref,
):
    q_ref[0:4] = near_ref[...].reshape(4, PIECE, DH)
    q_ref[4:8] = far_ref[...].reshape(4, PIECE, DH)
    for b, ref in enumerate((kv0_ref, kv1_ref, kv2_ref, kv3_ref)):
        kv_ref[b] = ref[...]
    top_ref[...] = jnp.full(top_ref.shape, NEG, F32)
    total_ref[...] = jnp.zeros(total_ref.shape, F32)
    weighted_ref[...] = jnp.zeros(weighted_ref.shape, F32)

    def tile(a, q_which, keys, masked):
        slot = a * 2 + q_which
        old = top_ref[slot]
        top = old
        parts = []
        for b, k_which in keys:
            scores, dprobs = products(q_ref, kv_ref, a, q_which, b, k_which)
            if masked:
                scores = jnp.where(diagonal_visible(), scores, NEG)
            parts.append((scores.reshape(32, 8, SPAN), dprobs.reshape(32, 8, SPAN)))
            top = jnp.maximum(top, jnp.max(parts[-1][0], axis=0))
        shrink = jnp.exp2(old - top)
        total = total_ref[slot] * shrink
        weighted = weighted_ref[slot] * shrink
        for scores, dprobs in parts:
            expon = jnp.exp2(scores - top[None])
            if masked:
                expon = jnp.where(diagonal_visible().reshape(32, 8, SPAN), expon, 0.0)
            total = total + jnp.sum(expon, axis=0)
            weighted = weighted + jnp.sum(expon * dprobs, axis=0)
        top_ref[slot] = top
        total_ref[slot] = total
        weighted_ref[slot] = weighted

    pieces = (0, 1, 2, 3)
    one_query_piece(order_ref, tile, 0, pieces, True)

    def one(a, carry):
        one_query_piece(order_ref, tile, a, pieces, False)
        return carry

    lax.fori_loop(1, 8, one, 0)
    for slot in range(16):
        tops = top_ref[slot]
        top = jnp.max(tops, axis=0, keepdims=True)
        factor = jnp.exp2(tops - top)
        rows = (
            top,
            jnp.sum(total_ref[slot] * factor, axis=0, keepdims=True),
            jnp.sum(weighted_ref[slot] * factor, axis=0, keepdims=True),
        )
        other = (slot + 8) % 16
        for kind, row in enumerate(rows):
            own_ref[kind, pl.ds(slot, 1), :] = row
            swapped_ref[kind, pl.ds(other, 1), :] = row


def norm_and_delta(stat_refs, norm_ref, delta_ref):
    for a in range(8):
        dc, dy = a // 4, a % 4
        found = []
        for k, ref in enumerate(stat_refs):
            begin = 2 * (4 * dc + (dy - k) % 4)
            found.append([ref[kind, pl.ds(begin, 2), :] for kind in range(3)])
        top = functools.reduce(jnp.maximum, [f[0] for f in found])
        factors = [jnp.exp2(f[0] - top) for f in found]
        total = sum(f[1] * g for f, g in zip(found, factors))
        weighted = sum(f[2] * g for f, g in zip(found, factors))
        norm = top + jnp.log2(total)
        delta = weighted / total
        for which in range(2):
            norm_ref[2 * a + which] = jnp.broadcast_to(norm[which : which + 1], (8, SPAN))
            delta_ref[2 * a + which] = jnp.broadcast_to(delta[which : which + 1], (8, SPAN))


def grads_kernel(pieces, first, last, *refs):
    refs = list(refs)
    order_ref, stat_refs, near_ref, far_ref = refs[0], refs[1:5], refs[5], refs[6]
    del refs[:7]
    kv_refs = refs[: len(pieces)]
    del refs[: len(pieces)]
    dqt_in = None if first else refs.pop(0)
    dkv_refs = dict(zip(pieces, refs[: len(pieces)]))
    del refs[: len(pieces)]
    dq_outs = [refs.pop(0), refs.pop(0)] if last else [refs.pop(0)]
    q_ref, kv_ref, norm_ref, delta_ref, dk_ref, dv_ref, kt_ref = refs[:7]
    dqt_ref = refs[7] if last else dq_outs[0]

    norm_and_delta(stat_refs, norm_ref, delta_ref)
    q_ref[0:4] = near_ref[...].reshape(4, PIECE, DH)
    q_ref[4:8] = far_ref[...].reshape(4, PIECE, DH)
    for i, b in enumerate(pieces):
        kv_ref[i] = kv_refs[i][...]
        for which in range(2):
            kt_ref[2 * i + which] = kv_ref[i, pl.ds(which * SPAN, SPAN), :].T
    dk_ref[...] = jnp.zeros(dk_ref.shape, F32)
    dv_ref[...] = jnp.zeros(dv_ref.shape, F32)
    if first:
        dqt_ref[...] = jnp.zeros(dqt_ref.shape, F32)
    else:
        dqt_ref[...] = dqt_in[...]

    def tile(a, q_which, keys, masked):
        slot = a * 2 + q_which
        norm = norm_ref[slot][None]
        delta = delta_ref[slot][None]
        queries = half(q_ref, a, q_which, 0)
        out_grads = half(q_ref, a, q_which, 1)
        dqt = None
        for b, k_which in keys:
            i = pieces.index(b)
            key_slot = 2 * i + k_which
            scores = lax.dot_general(
                half(kv_ref, i, k_which, 0), queries, NT, preferred_element_type=F32
            ) * SCALE2
            dprobs = lax.dot_general(
                half(kv_ref, i, k_which, 1), out_grads, NT, preferred_element_type=F32
            )
            probs = jnp.exp2(scores.reshape(32, 8, SPAN) - norm)
            if masked:
                probs = jnp.where(diagonal_visible().reshape(32, 8, SPAN), probs, 0.0)
            dscores = probs * (dprobs.reshape(32, 8, SPAN) - delta)
            probs = probs.reshape(SPAN, SPAN).astype(BF16)
            dscores = dscores.reshape(SPAN, SPAN).astype(BF16)
            dv_ref[key_slot] += lax.dot_general(probs, out_grads, NN, preferred_element_type=F32)
            dk_ref[key_slot] += lax.dot_general(dscores, queries, NN, preferred_element_type=F32)
            term = lax.dot_general(kt_ref[key_slot], dscores, NN, preferred_element_type=F32)
            dqt = term if dqt is None else dqt + term
        dqt_ref[slot] += dqt

    start, step = 0, max(1, 4 // len(pieces))
    if 0 in pieces:
        one_query_piece(order_ref, tile, 0, pieces, True)
        one_query_piece(order_ref, tile, 1, pieces, False)
        start, step = 2, 3

    def some(i, carry):
        for j in range(step):
            one_query_piece(order_ref, tile, start + i * step + j, pieces, False)
        return carry

    lax.fori_loop(0, (8 - start) // step, some, 0)
    for i, b in enumerate(pieces):
        ref = dkv_refs[b]
        for which in range(2):
            ref[pl.ds(which * SPAN, SPAN), :] = dk_ref[2 * i + which].astype(ref.dtype)
            ref[pl.ds((2 + which) * SPAN, SPAN), :] = dv_ref[2 * i + which].astype(ref.dtype)
    if last:
        for out, begin in zip(dq_outs, (0, 8)):
            for slot in range(8):
                out[pl.ds(slot * SPAN, SPAN), :] = dqt_ref[begin + slot].T.astype(out.dtype)


def pack_kernel(queries_ref, keys_ref, values_ref, grads_ref, q_ref, kv_ref, sems):
    rows = 2 * SPAN
    copies = []
    for i, (source, target) in enumerate(
        ((queries_ref, q_ref), (grads_ref, q_ref), (keys_ref, kv_ref), (values_ref, kv_ref))
    ):
        place = target.at[pl.ds((i % 2) * rows, rows), :]
        copies.append(pltpu.make_async_copy(source, place, sems.at[i]))
    for copy in copies:
        copy.start()
    for copy in copies:
        copy.wait()


def middle_kernel(dkv_ref, z1_ref, z2_ref, z3_ref, sum_ref):
    total = dkv_ref[...] + z1_ref[...].astype(F32) + z2_ref[...].astype(F32) + z3_ref[...].astype(F32)
    sum_ref[...] = total.astype(BF16)


def query_kernel(keep_ref, other_ref, dq_ref, r1_ref, r2_ref, r3_ref):
    for k, ref in enumerate((dq_ref, r1_ref, r2_ref, r3_ref)):
        rows = pl.ds(k * 2 * SPAN, 2 * SPAN)
        ref[...] = (keep_ref[rows, :] + other_ref[rows, :].astype(F32)).astype(ref.dtype)


def last_kernel(sum_ref, x1_ref, x2_ref, x3_ref, dq_ref, y1_ref, y2_ref, y3_ref, q_out, k_out, v_out):
    own, x1, x2, x3 = [ref[...].astype(F32) for ref in (sum_ref, x1_ref, x2_ref, x3_ref)]
    total = (own + x2) + (x1 + x3)
    k_out[...] = (total[: 2 * SPAN] * SCALE).astype(BF16)
    v_out[...] = total[2 * SPAN :].astype(BF16)
    dq = dq_ref[...]
    for ref in (y1_ref, y2_ref, y3_ref):
        dq = dq + ref[...].astype(F32)
    q_out[...] = (dq * SCALE).astype(BF16)


SMEM = pl.BlockSpec(memory_space=pltpu.SMEM)
VMEM = pl.BlockSpec(memory_space=pltpu.VMEM)
PIECE = 4 * SPAN


def call_stats(span_order, q_near, q_far, kvs):
    shape = jax.ShapeDtypeStruct((3, 16, SPAN), F32)
    return pl.pallas_call(
        stats_kernel,
        out_shape=(shape, shape),
        in_specs=[SMEM] + [VMEM] * 6,
        out_specs=(VMEM, VMEM),
        scratch_shapes=[pltpu.VMEM((8, PIECE, DH), BF16), pltpu.VMEM((4, PIECE, DH), BF16)]
        + [pltpu.VMEM((16, 8, SPAN), F32)] * 3,
        compiler_params=pltpu.CompilerParams(vmem_limit_bytes=32 * 2**20),
        cost_estimate=pl.CostEstimate(
            flops=65 * 2 * 2 * SPAN * SPAN * DH, bytes_accessed=3 * 2**20, transcendentals=65 * SPAN * SPAN
        ),
        name="stats",
    )(span_order, q_near, q_far, *kvs)


def call_grads(pieces, first, last, span_order, stats, q_near, q_far, kvs, dqt):
    tiles = 16 * len(pieces)
    dkv_shapes = tuple(jax.ShapeDtypeStruct((PIECE, DH), BF16 if b else F32) for b in pieces)
    if last:
        dq_shapes = tuple(jax.ShapeDtypeStruct((8 * SPAN, DH), dtype) for dtype in (F32, BF16))
    else:
        dq_shapes = (jax.ShapeDtypeStruct((16, DH, SPAN), F32),)
    args = [span_order, *stats, q_near, q_far, *[kvs[b] for b in pieces]] + ([] if first else [dqt])
    out = pl.pallas_call(
        functools.partial(grads_kernel, pieces, first, last),
        out_shape=dkv_shapes + dq_shapes,
        in_specs=[SMEM] + [VMEM] * (len(args) - 1),
        out_specs=(VMEM,) * (len(pieces) + len(dq_shapes)),
        scratch_shapes=[
            pltpu.VMEM((8, PIECE, DH), BF16),
            pltpu.VMEM((len(pieces), PIECE, DH), BF16),
            pltpu.VMEM((16, 8, SPAN), F32),
            pltpu.VMEM((16, 8, SPAN), F32),
            pltpu.VMEM((2 * len(pieces), SPAN, DH), F32),
            pltpu.VMEM((2 * len(pieces), SPAN, DH), F32),
            pltpu.VMEM((2 * len(pieces), DH, SPAN), BF16),
        ]
        + ([pltpu.VMEM((16, DH, SPAN), F32)] if last else []),
        compiler_params=pltpu.CompilerParams(vmem_limit_bytes=32 * 2**20),
        cost_estimate=pl.CostEstimate(
            flops=tiles * 5 * 2 * SPAN * SPAN * DH, bytes_accessed=4 * 2**20, transcendentals=tiles * SPAN * SPAN
        ),
        name="grads",
    )(*args)
    return out[: len(pieces)], out[len(pieces) :]


def plain_call(kernel, name, out_shapes, *args):
    return pl.pallas_call(
        kernel,
        out_shape=tuple(jax.ShapeDtypeStruct(shape, dtype) for shape, dtype in out_shapes),
        in_specs=[VMEM] * len(args),
        out_specs=(VMEM,) * len(out_shapes),
        compiler_params=pltpu.CompilerParams(vmem_limit_bytes=16 * 2**20),
        cost_estimate=pl.CostEstimate(flops=2**20, bytes_accessed=2**21, transcendentals=0),
        name=name,
    )(*args)


def call_pack(*args):
    return pl.pallas_call(
        pack_kernel,
        out_shape=(jax.ShapeDtypeStruct((PIECE, DH), BF16),) * 2,
        in_specs=[pl.BlockSpec(memory_space=pl.ANY)] * 4,
        out_specs=(VMEM, VMEM),
        scratch_shapes=[pltpu.SemaphoreType.DMA((4,))],
        compiler_params=pltpu.CompilerParams(vmem_limit_bytes=56 * 2**20),
        name="pack",
    )(*args)


def back(value, axis, k):
    return lax.ppermute(value, axis, [(i, (i + k) % 4) for i in range(4)])


def ahead(value, axis, k):
    return lax.ppermute(value, axis, [(i, (i - k) % 4) for i in range(4)])


def swap_core(value):
    return lax.ppermute(value, "c", [(0, 1), (1, 0)])


def local(span_order, queries, key_rows, value_rows, out_grads):
    q_own, kv_own = call_pack(queries, key_rows, value_rows, out_grads)
    q_got = [back(q_own, "y", k) for k in (1, 2, 3)]
    kv_got = [back(kv_own, "z", k) for k in (1, 2, 3)]
    q_got, kv_got = lax.optimization_barrier((q_got, kv_got))
    q_near = jnp.concatenate([q_own] + q_got, axis=0)
    q_far = swap_core(q_near)
    kvs = [kv_own] + kv_got

    mine, for_other = call_stats(span_order, q_near, q_far, kvs)
    theirs = swap_core(for_other)
    top = jnp.maximum(mine[0], theirs[0])
    mine_by, theirs_by = jnp.exp2(mine[0] - top), jnp.exp2(theirs[0] - top)
    both = jnp.stack([top, mine[1] * mine_by + theirs[1] * theirs_by, mine[2] * mine_by + theirs[2] * theirs_by])
    stats = [both] + [back(both, "y", k) for k in (1, 2, 3)]

    common = (span_order, stats, q_near, q_far, kvs)
    (dkv1, dkv2, dkv3), (dqt,) = call_grads((1, 2, 3), True, False, *common, None)
    (dkv0,), (dq_keep, dq_send) = call_grads((0,), False, True, *common, dqt)
    z1, z2, z3 = ahead(dkv1, "z", 1), ahead(dkv2, "z", 2), ahead(dkv3, "z", 3)
    (summed,) = plain_call(middle_kernel, "middle", [((PIECE, DH), BF16)], dkv0, z1, z2, z3)
    dq_send, summed = lax.optimization_barrier((dq_send, summed))
    dq_other = swap_core(dq_send)
    rows = (2 * SPAN, DH)
    dq, r1, r2, r3 = plain_call(
        query_kernel, "query", [(rows, F32), (rows, BF16), (rows, BF16), (rows, BF16)], dq_keep, dq_other
    )
    xs = [back(summed, "x", k) for k in (1, 2, 3)]
    ys = [ahead(part, "y", k) for k, part in ((1, r1), (2, r2), (3, r3))]
    return plain_call(last_kernel, "last", [(rows, BF16)] * 3, summed, *xs, dq, *ys)


def solution(mesh):
    fine = Mesh(mesh.devices.reshape(4, 4, 2, 4), ("z", "y", "c", "x"))
    ctx = ("z", "y", "c")
    return jax.shard_map(
        local,
        mesh=fine,
        in_specs=(P(), P(ctx, "x"), P(ctx, None), P(ctx, None), P(ctx, "x")),
        out_specs=(P(ctx, "x"), P(ctx, None), P(ctx, None)),
        check_vma=False,
    )
```

time: 133 us -> 103 us (0.77)
  other arithmetic: 17.1 us -> 0.04 us
  waiting for transfers between devices: 54 us -> 41.4 us
  Pallas kernels: 27.8 us -> 33.4 us
  starting transfers between devices: 29.6 us -> 25.4 us
    ppermute x6, waiting for transfers between devices: 18.9 us -> 8.59 us  [ahead(): return lax.ppermute(value, axis, [(i, (i - k) % 4) for i in range(4)])]
    unnamed x4 -> x0, other arithmetic: 8.69 us -> none
    pallas_call x2 -> x7, Pallas kernels: 27.8 us -> 33.4 us  [the longest x2 20.3 us: call_grads(): pl.pallas_call(functools.partial(grads_kernel, pieces, first, last), out_...]
    ppermute x12, waiting for transfers between devices: 33.9 us -> 29.2 us  [back(): return lax.ppermute(value, axis, [(i, (i + k) % 4) for i in range(4)])]
    another operation x4 -> x0, other arithmetic: 3.3 us -> none  [the longest x2 1.96 us: local(): kv_all = jnp.stack([kv_own] + [back(kv_own, 'z', k) for k in (1, 2, 3)])]
    ppermute x12, starting transfers between devices: 22.8 us -> 20 us  [back(): return lax.ppermute(value, axis, [(i, (i + k) % 4) for i in range(4)])]
    ppermute x3, waiting for transfers between devices: 1.22 us -> 3.65 us  [swap_core(): return lax.ppermute(value, 'c', [(0, 1), (1, 0)])]
    concatenate x4 -> x0, other arithmetic: 2.01 us -> none  [the longest x3 1.99 us: out_order(): return jnp.concatenate(in_order(value), axis=0).astype(BF16)]
  transfers between devices with their start and end apart: 21 -> 21, of which waited for: 17 -> 16; matrix products, arithmetic and copies ran while one was open for 5% -> 1% of each run, Pallas kernels for 0% -> 6%
where the time goes in v2:
time: 103 us; the launch traced here: 102 us
  waiting for transfers between devices  41.4 us (40%)
  Pallas kernels  33.4 us (32%)
  starting transfers between devices  25.4 us (25%)
  local copies, waits for them, and re-layouts  1.17 us (1%)
    ppermute x12, waiting for transfers between devices, back(): return lax.ppermute(value, axis, [(i, (i + k) % 4) for i in range(4)])  29.2 us
    pallas_call x2, Pallas kernels, call_grads(): pl.pallas_call(functools.partial(grads_kernel, pieces, first, last), out_...  20.3 us
    ppermute x12, starting transfers between devices, back(): return lax.ppermute(value, axis, [(i, (i + k) % 4) for i in range(4)])  20 us
    pallas_call x1, Pallas kernels, call_stats(): pl.pallas_call(stats_kernel, out_shape=(shape, shape), in_specs=[SMEM] +...  10.1 us
    ppermute x6, waiting for transfers between devices, ahead(): return lax.ppermute(value, axis, [(i, (i - k) % 4) for i in range(4)])  8.59 us
    ppermute x6, starting transfers between devices, ahead(): return lax.ppermute(value, axis, [(i, (i - k) % 4) for i in range(4)])  4.94 us
    ppermute x3, waiting for transfers between devices, swap_core(): return lax.ppermute(value, 'c', [(0, 1), (1, 0)])  3.65 us
  transfers between devices with their start and end apart: 21, of which 16 were waited for; matrix products, arithmetic and copies ran while one was open for 1% of the time, Pallas kernels for 6%

profile of v2, /device:TPU:0, one launch (start us, length us, event | category | flops | bytes accessed | tf_op | source)
XLA Modules:
  0.0 102.2 jit_solution(14295514522602721924)
XLA Ops:
  0.6 1.9 %pack.1 = (bf16[1024,128]{1,0:T(8,128)(2,1)}, bf16[1024,128]{1,0:T(8,128)(2,1)}) custom-call(bf16[512,128]{1,0:T(8,128)(2,1)} %queries_ref.1, bf16[512,128]{1,0:T(8,128)(2,1)} %keys_ref.1, bf16[512,128]{1,0:T(8,128)(2,1)} %values_ref.1, bf16[512,128]{1,0:T(8,128)(2,1)} %grads_ref.1), custom_call_target="tpu_custom_call" | custom-call | tf_op jit(solution)/shard_map/pack/pallas_call | solution.py:332
  2.6 3.2 %collective-permute-start.2 = (bf16[1024,128]{1,0:T(8,128)(2,1)}, bf16[1024,128]{1,0:T(8,128)(2,1)S(1)}, u32[]{:S(2)}, u32[]{:S(2)}) collective-permute-start(bf16[1024,128]{1,0:T(8,128)(2,1)} %get-tuple-element.26), channel_id=1, source_target_pairs={{0,24},{8,0},{16,8},{24,16},{1,25},{9,1},{17,9},{25,17},{2,26},{10... | collective-permute-start | bytes 786440 | tf_op jit(solution)/shard_map/ppermute | solution.py:344
  7.4 4.0 %collective-permute-start.5 = (bf16[1024,128]{1,0:T(8,128)(2,1)}, bf16[1024,128]{1,0:T(8,128)(2,1)S(1)}, u32[]{:S(2)}, u32[]{:S(2)}) collective-permute-start(bf16[1024,128]{1,0:T(8,128)(2,1)} %get-tuple-element.27.kv0_ref.refs_7_), channel_id=1, source_target_pairs={{0,96},{32,0},{64,32},{96,64},{1,97},{33,1},{65,33},{97,65},{2,98}... | collective-permute-start | bytes 786440 | tf_op jit(solution)/shard_map/ppermute | solution.py:344
  11.4 5.9 %collective-permute-done.2 = bf16[1024,128]{1,0:T(8,128)(2,1)S(1)} collective-permute-done((bf16[1024,128]{1,0:T(8,128)(2,1)}, bf16[1024,128]{1,0:T(8,128)(2,1)S(1)}, u32[]{:S(2)}, u32[]{:S(2)}) %collective-permute-start.2) | collective-permute-done | bytes 262176 | tf_op jit(solution)/shard_map/ppermute | solution.py:344
  17.3 1.9 %collective-permute-start.3 = (bf16[1024,128]{1,0:T(8,128)(2,1)}, bf16[1024,128]{1,0:T(8,128)(2,1)S(1)}, u32[]{:S(2)}, u32[]{:S(2)}) collective-permute-start(bf16[1024,128]{1,0:T(8,128)(2,1)} %get-tuple-element.27.kv0_ref.refs_7_), channel_id=1, source_target_pairs={{0,32},{32,64},{64,96},{96,0},{1,33},{33,65},{65,97},{97,1},{2,34}... | collective-permute-start | bytes 786440 | tf_op jit(solution)/shard_map/ppermute | solution.py:344
  20.9 1.2 %collective-permute-done.5.kv3_ref.refs_9_ = bf16[1024,128]{1,0:T(8,128)(2,1)S(1)} collective-permute-done((bf16[1024,128]{1,0:T(8,128)(2,1)}, bf16[1024,128]{1,0:T(8,128)(2,1)S(1)}, u32[]{:S(2)}, u32[]{:S(2)}) %collective-permute-start.5) | collective-permute-done | bytes 262176 | tf_op jit(solution)/shard_map/ppermute | solution.py:344
  22.2 4.6 %collective-permute-done.3.kv1_ref.refs_7_ = bf16[1024,128]{1,0:T(8,128)(2,1)S(1)} collective-permute-done((bf16[1024,128]{1,0:T(8,128)(2,1)}, bf16[1024,128]{1,0:T(8,128)(2,1)S(1)}, u32[]{:S(2)}, u32[]{:S(2)}) %collective-permute-start.3) | collective-permute-done | bytes 262176 | tf_op jit(solution)/shard_map/ppermute | solution.py:344
  27.1 2.5 %collective-permute-done.6.far_ref.refs_6_ = bf16[4096,128]{1,0:T(8,128)(2,1)S(1)} collective-permute-done((bf16[4096,128]{1,0:T(8,128)(2,1)S(1)}, bf16[4096,128]{1,0:T(8,128)(2,1)S(1)}, u32[]{:S(2)}, u32[]{:S(2)}) %collective-permute-start.6) | collective-permute-done | bytes 1048608 | tf_op jit(solution)/shard_map/ppermute | solution.py:352
  29.6 10.1 %stats.1 = (f32[3,16,256]{2,1,0:T(8,128)S(1)}, f32[3,16,256]{2,1,0:T(8,128)S(1)}) custom-call(s32[32,2]{1,0:T(8,128)S(1)} %copy.10.order_ref.refs_0_, bf16[4096,128]{1,0:T(8,128)(2,1)S(1)} %constant_dynamic-update-slice_fusion.near_ref.refs_5_, bf16[4096,128]{1,0:T(8,128)(2,1)S(1)} %collective-permute-done.6.far_ref.refs_6_, bf16[1024,128]{1,0:T(8,128)(2,1)S(1)} %copy-done, ...), custom_call_target="tpu_custom_call" | custom-call | flops 2181038080 | bytes 3145728 | tf_op jit(solution)/shard_map/stats/pallas_call | solution.py:272
  39.9 1.1 %collective-permute-done.7 = f32[3,16,256]{2,1,0:T(8,128)S(1)} collective-permute-done((f32[3,16,256]{2,1,0:T(8,128)S(1)}, f32[3,16,256]{2,1,0:T(8,128)S(1)}, u32[]{:S(2)}, u32[]{:S(2)}) %collective-permute-start.7) | collective-permute-done | bytes 49184 | tf_op jit(solution)/shard_map/ppermute | solution.py:352
  41.0 3.8 %collective-permute-start.10 = (f32[3,16,256]{2,1,0:T(8,128)S(1)}, f32[3,16,256]{2,1,0:T(8,128)S(1)}, u32[]{:S(2)}, u32[]{:S(2)}) collective-permute-start(f32[3,16,256]{2,1,0:T(8,128)S(1)} %pad_maximum_fusion.refs_1_), channel_id=1, source_target_pairs={{0,24},{8,0},{16,8},{24,16},{1,25},{9,1},{17,9},{25,17},{2,26},{10... | collective-permute-start | bytes 147464 | tf_op jit(solution)/shard_map/ppermute | solution.py:344
  45.8 1.5 %collective-permute-done.10.refs_4_ = f32[3,16,256]{2,1,0:T(8,128)S(1)} collective-permute-done((f32[3,16,256]{2,1,0:T(8,128)S(1)}, f32[3,16,256]{2,1,0:T(8,128)S(1)}, u32[]{:S(2)}, u32[]{:S(2)}) %collective-permute-start.10) | collective-permute-done | bytes 49184 | tf_op jit(solution)/shard_map/ppermute | solution.py:344
  47.3 3.2 %collective-permute-done.9.refs_3_ = f32[3,16,256]{2,1,0:T(8,128)S(1)} collective-permute-done((f32[3,16,256]{2,1,0:T(8,128)S(1)}, f32[3,16,256]{2,1,0:T(8,128)S(1)}, u32[]{:S(2)}, u32[]{:S(2)}) %collective-permute-start.9) | collective-permute-done | bytes 49184 | tf_op jit(solution)/shard_map/ppermute | solution.py:344
  50.7 14.2 %grads.2 = (bf16[1024,128]{1,0:T(8,128)(2,1)S(1)}, bf16[1024,128]{1,0:T(8,128)(2,1)S(1)}, bf16[1024,128]{1,0:T(8,128)(2,1)S(1)}, f32[16,128,256]{2,1,0:T(8,128)S(1)}) custom-call(s32[32,2]{1,0:T(8,128)S(1)} %copy.10.order_ref.refs_0_, f32[3,16,256]{2,1,0:T(8,128)S(1)} %pad_maximum_fusion.refs_1_, f32[3,16,256]{2,1,0:T(8,128)S(1)} %collective-permute-done.8.refs_2_, ...), custom_call_target="tpu_custom_call" | custom-call | flops 4026531840 | bytes 4194304 | tf_op jit(solution)/shard_map/grads/pallas_call | solution.py:295
  64.9 1.8 %collective-permute-start.11 = (bf16[1024,128]{1,0:T(8,128)(2,1)S(1)}, bf16[1024,128]{1,0:T(8,128)(2,1)S(1)}, u32[]{:S(2)}, u32[]{:S(2)}) collective-permute-start(bf16[1024,128]{1,0:T(8,128)(2,1)S(1)} %get-tuple-element.39), channel_id=1, source_target_pairs={{0,96},{32,0},{64,32},{96,64},{1,97},{33,1},{65,33},{97,65},{2,98}... | collective-permute-start | bytes 786440 | tf_op jit(solution)/shard_map/ppermute | solution.py:348
  66.8 1.3 %collective-permute-start.13 = (bf16[1024,128]{1,0:T(8,128)(2,1)S(1)}, bf16[1024,128]{1,0:T(8,128)(2,1)S(1)}, u32[]{:S(2)}, u32[]{:S(2)}) collective-permute-start(bf16[1024,128]{1,0:T(8,128)(2,1)S(1)} %get-tuple-element.41), channel_id=1, source_target_pairs={{0,32},{32,64},{64,96},{96,0},{1,33},{33,65},{65,97},{97,1},{2,34}... | collective-permute-start | bytes 786440 | tf_op jit(solution)/shard_map/ppermute | solution.py:348
  68.0 6.1 %grads.3 = (f32[1024,128]{1,0:T(8,128)S(1)}, f32[2048,128]{1,0:T(8,128)S(1)}, bf16[2048,128]{1,0:T(8,128)(2,1)S(1)}) custom-call(s32[32,2]{1,0:T(8,128)S(1)} %copy.10.order_ref.refs_0_, f32[3,16,256]{2,1,0:T(8,128)S(1)} %pad_maximum_fusion.refs_1_, f32[3,16,256]{2,1,0:T(8,128)S(1)} %collective-permute-done.8.refs_2_, ...), custom_call_target="tpu_custom_call" | custom-call | flops 1342177280 | bytes 4194304 | tf_op jit(solution)/shard_map/grads/pallas_call | solution.py:295
  74.2 2.7 %collective-permute-done.11.z1_ref = bf16[1024,128]{1,0:T(8,128)(2,1)S(1)} collective-permute-done((bf16[1024,128]{1,0:T(8,128)(2,1)S(1)}, bf16[1024,128]{1,0:T(8,128)(2,1)S(1)}, u32[]{:S(2)}, u32[]{:S(2)}) %collective-permute-start.11) | collective-permute-done | bytes 262176 | tf_op jit(solution)/shard_map/ppermute | solution.py:348
  77.5 2.8 %collective-permute-done.13.z3_ref = bf16[1024,128]{1,0:T(8,128)(2,1)S(1)} collective-permute-done((bf16[1024,128]{1,0:T(8,128)(2,1)S(1)}, bf16[1024,128]{1,0:T(8,128)(2,1)S(1)}, u32[]{:S(2)}, u32[]{:S(2)}) %collective-permute-start.13) | collective-permute-done | bytes 262176 | tf_op jit(solution)/shard_map/ppermute | solution.py:348
  80.5 2.8 %collective-permute-start.16 = (bf16[1024,128]{1,0:T(8,128)(2,1)S(1)}, bf16[1024,128]{1,0:T(8,128)(2,1)S(1)}, u32[]{:S(2)}, u32[]{:S(2)}) collective-permute-start(bf16[1024,128]{1,0:T(8,128)(2,1)S(1)} %middle.1.sum_ref), channel_id=1, source_target_pairs={{0,3},{1,0},{2,1},{3,2},{4,7},{5,4},{6,5},{7,6},{8,11},{9,8},{10,9... | collective-permute-start | bytes 786440 | tf_op jit(solution)/shard_map/ppermute | solution.py:344
  85.1 1.2 %collective-permute-start.18 = (bf16[512,128]{1,0:T(8,128)(2,1)S(1)}, bf16[512,128]{1,0:T(8,128)(2,1)S(1)}, u32[]{:S(2)}, u32[]{:S(2)}) collective-permute-start(bf16[512,128]{1,0:T(8,128)(2,1)S(1)} %get-tuple-element.46), channel_id=1, source_target_pairs={{0,24},{8,0},{16,8},{24,16},{1,25},{9,1},{17,9},{25,17},{2,26},{10... | collective-permute-start | bytes 393224 | tf_op jit(solution)/shard_map/ppermute | solution.py:348
  86.9 8.2 %collective-permute-done.16.x3_ref = bf16[1024,128]{1,0:T(8,128)(2,1)S(1)} collective-permute-done((bf16[1024,128]{1,0:T(8,128)(2,1)S(1)}, bf16[1024,128]{1,0:T(8,128)(2,1)S(1)}, u32[]{:S(2)}, u32[]{:S(2)}) %collective-permute-start.16) | collective-permute-done | bytes 262176 | tf_op jit(solution)/shard_map/ppermute | solution.py:344
  95.1 3.7 %collective-permute-done.14.x1_ref = bf16[1024,128]{1,0:T(8,128)(2,1)S(1)} collective-permute-done((bf16[1024,128]{1,0:T(8,128)(2,1)S(1)}, bf16[1024,128]{1,0:T(8,128)(2,1)S(1)}, u32[]{:S(2)}, u32[]{:S(2)}) %collective-permute-start.14) | collective-permute-done | bytes 262176 | tf_op jit(solution)/shard_map/ppermute | solution.py:344
  98.8 2.5 %collective-permute-done.20.y3_ref = bf16[512,128]{1,0:T(8,128)(2,1)S(1)} collective-permute-done((bf16[512,128]{1,0:T(8,128)(2,1)S(1)}, bf16[512,128]{1,0:T(8,128)(2,1)S(1)}, u32[]{:S(2)}, u32[]{:S(2)}) %collective-permute-start.20) | collective-permute-done | bytes 131104 | tf_op jit(solution)/shard_map/ppermute | solution.py:348
  (37 shorter events, 9.2 us)
Async XLA Ops:
  0.6 26.3 %copy-start.1 = (s32[32,2]{0,1:T(2,128)S(1)}, s32[32,2]{0,1:T(2,128)}, u32[]{:S(2)}) copy-start(s32[32,2]{0,1:T(2,128)} %param.5) | copy-start | bytes 772
  2.6 27.0 %copy-start = (bf16[1024,128]{1,0:T(8,128)(2,1)S(1)}, bf16[1024,128]{1,0:T(8,128)(2,1)}, u32[]{:S(2)}) copy-start(bf16[1024,128]{1,0:T(8,128)(2,1)} %get-tuple-element.27.kv0_ref.refs_7_) | copy-start | bytes 786436
  2.6 14.7 %collective-permute-start.2 = (bf16[1024,128]{1,0:T(8,128)(2,1)}, bf16[1024,128]{1,0:T(8,128)(2,1)S(1)}, u32[]{:S(2)}, u32[]{:S(2)}) collective-permute-start(bf16[1024,128]{1,0:T(8,128)(2,1)} %get-tuple-element.26), channel_id=1, source_target_pairs={{0,24},{8,0},{16,8},{24,16},{1,25},{9,1},{17,9},{25,17},{2,26},{10... | collective-permute-start | bytes 786440 | tf_op jit(solution)/shard_map/ppermute | solution.py:344
  5.8 14.4 %collective-permute-start.1 = (bf16[1024,128]{1,0:T(8,128)(2,1)}, bf16[1024,128]{1,0:T(8,128)(2,1)S(1)}, u32[]{:S(2)}, u32[]{:S(2)}) collective-permute-start(bf16[1024,128]{1,0:T(8,128)(2,1)} %get-tuple-element.26), channel_id=1, source_target_pairs={{0,16},{8,24},{16,0},{24,8},{1,17},{9,25},{17,1},{25,9},{2,18},{10... | collective-permute-start | bytes 786440 | tf_op jit(solution)/shard_map/ppermute | solution.py:344
  6.4 14.5 %collective-permute-start = (bf16[1024,128]{1,0:T(8,128)(2,1)}, bf16[1024,128]{1,0:T(8,128)(2,1)S(1)}, u32[]{:S(2)}, u32[]{:S(2)}) collective-permute-start(bf16[1024,128]{1,0:T(8,128)(2,1)} %get-tuple-element.26), channel_id=1, source_target_pairs={{0,8},{8,16},{16,24},{24,0},{1,9},{9,17},{17,25},{25,1},{2,10},{10... | collective-permute-start | bytes 786440 | tf_op jit(solution)/shard_map/ppermute | solution.py:344
  7.4 14.7 %collective-permute-start.5 = (bf16[1024,128]{1,0:T(8,128)(2,1)}, bf16[1024,128]{1,0:T(8,128)(2,1)S(1)}, u32[]{:S(2)}, u32[]{:S(2)}) collective-permute-start(bf16[1024,128]{1,0:T(8,128)(2,1)} %get-tuple-element.27.kv0_ref.refs_7_), channel_id=1, source_target_pairs={{0,96},{32,0},{64,32},{96,64},{1,97},{33,1},{65,33},{97,65},{2,98}... | collective-permute-start | bytes 786440 | tf_op jit(solution)/shard_map/ppermute | solution.py:344
  11.4 10.8 %collective-permute-start.4 = (bf16[1024,128]{1,0:T(8,128)(2,1)}, bf16[1024,128]{1,0:T(8,128)(2,1)S(1)}, u32[]{:S(2)}, u32[]{:S(2)}) collective-permute-start(bf16[1024,128]{1,0:T(8,128)(2,1)} %get-tuple-element.27.kv0_ref.refs_7_), channel_id=1, source_target_pairs={{0,64},{32,96},{64,0},{96,32},{1,65},{33,97},{65,1},{97,33},{2,66}... | collective-permute-start | bytes 786440 | tf_op jit(solution)/shard_map/ppermute | solution.py:344
  17.3 9.5 %collective-permute-start.3 = (bf16[1024,128]{1,0:T(8,128)(2,1)}, bf16[1024,128]{1,0:T(8,128)(2,1)S(1)}, u32[]{:S(2)}, u32[]{:S(2)}) collective-permute-start(bf16[1024,128]{1,0:T(8,128)(2,1)} %get-tuple-element.27.kv0_ref.refs_7_), channel_id=1, source_target_pairs={{0,32},{32,64},{64,96},{96,0},{1,33},{33,65},{65,97},{97,1},{2,34}... | collective-permute-start | bytes 786440 | tf_op jit(solution)/shard_map/ppermute | solution.py:344
  26.9 2.7 %collective-permute-start.6 = (bf16[4096,128]{1,0:T(8,128)(2,1)S(1)}, bf16[4096,128]{1,0:T(8,128)(2,1)S(1)}, u32[]{:S(2)}, u32[]{:S(2)}) collective-permute-start(bf16[4096,128]{1,0:T(8,128)(2,1)S(1)} %constant_dynamic-update-slice_fusion.near_ref.refs_5_), channel_id=1, source_target_pairs={{0,4},{4,0},{1,5},{5,1},{2,6},{6,2},{3,7},{7,3},{8,12},{12,8},{9,1... | collective-permute-start | bytes 3145736 | tf_op jit(solution)/shard_map/ppermute | solution.py:352
  39.7 1.3 %collective-permute-start.7 = (f32[3,16,256]{2,1,0:T(8,128)S(1)}, f32[3,16,256]{2,1,0:T(8,128)S(1)}, u32[]{:S(2)}, u32[]{:S(2)}) collective-permute-start(f32[3,16,256]{2,1,0:T(8,128)S(1)} %get-tuple-element.35), channel_id=1, source_target_pairs={{0,4},{4,0},{1,5},{5,1},{2,6},{6,2},{3,7},{7,3},{8,12},{12,8},{9,1... | collective-permute-start | bytes 147464 | tf_op jit(solution)/shard_map/ppermute | solution.py:352
  41.0 6.3 %collective-permute-start.10 = (f32[3,16,256]{2,1,0:T(8,128)S(1)}, f32[3,16,256]{2,1,0:T(8,128)S(1)}, u32[]{:S(2)}, u32[]{:S(2)}) collective-permute-start(f32[3,16,256]{2,1,0:T(8,128)S(1)} %pad_maximum_fusion.refs_1_), channel_id=1, source_target_pairs={{0,24},{8,0},{16,8},{24,16},{1,25},{9,1},{17,9},{25,17},{2,26},{10... | collective-permute-start | bytes 147464 | tf_op jit(solution)/shard_map/ppermute | solution.py:344
  44.9 5.6 %collective-permute-start.9 = (f32[3,16,256]{2,1,0:T(8,128)S(1)}, f32[3,16,256]{2,1,0:T(8,128)S(1)}, u32[]{:S(2)}, u32[]{:S(2)}) collective-permute-start(f32[3,16,256]{2,1,0:T(8,128)S(1)} %pad_maximum_fusion.refs_1_), channel_id=1, source_target_pairs={{0,16},{8,24},{16,0},{24,8},{1,17},{9,25},{17,1},{25,9},{2,18},{10... | collective-permute-start | bytes 147464 | tf_op jit(solution)/shard_map/ppermute | solution.py:344
  44.9 5.8 %collective-permute-start.8 = (f32[3,16,256]{2,1,0:T(8,128)S(1)}, f32[3,16,256]{2,1,0:T(8,128)S(1)}, u32[]{:S(2)}, u32[]{:S(2)}) collective-permute-start(f32[3,16,256]{2,1,0:T(8,128)S(1)} %pad_maximum_fusion.refs_1_), channel_id=1, source_target_pairs={{0,8},{8,16},{16,24},{24,0},{1,9},{9,17},{17,25},{25,1},{2,10},{10... | collective-permute-start | bytes 147464 | tf_op jit(solution)/shard_map/ppermute | solution.py:344
  64.9 11.9 %collective-permute-start.11 = (bf16[1024,128]{1,0:T(8,128)(2,1)S(1)}, bf16[1024,128]{1,0:T(8,128)(2,1)S(1)}, u32[]{:S(2)}, u32[]{:S(2)}) collective-permute-start(bf16[1024,128]{1,0:T(8,128)(2,1)S(1)} %get-tuple-element.39), channel_id=1, source_target_pairs={{0,96},{32,0},{64,32},{96,64},{1,97},{33,1},{65,33},{97,65},{2,98}... | collective-permute-start | bytes 786440 | tf_op jit(solution)/shard_map/ppermute | solution.py:348
  66.8 10.8 %collective-permute-start.12 = (bf16[1024,128]{1,0:T(8,128)(2,1)S(1)}, bf16[1024,128]{1,0:T(8,128)(2,1)S(1)}, u32[]{:S(2)}, u32[]{:S(2)}) collective-permute-start(bf16[1024,128]{1,0:T(8,128)(2,1)S(1)} %get-tuple-element.40), channel_id=1, source_target_pairs={{0,64},{32,96},{64,0},{96,32},{1,65},{33,97},{65,1},{97,33},{2,66}... | collective-permute-start | bytes 786440 | tf_op jit(solution)/shard_map/ppermute | solution.py:348
  66.8 13.5 %collective-permute-start.13 = (bf16[1024,128]{1,0:T(8,128)(2,1)S(1)}, bf16[1024,128]{1,0:T(8,128)(2,1)S(1)}, u32[]{:S(2)}, u32[]{:S(2)}) collective-permute-start(bf16[1024,128]{1,0:T(8,128)(2,1)S(1)} %get-tuple-element.41), channel_id=1, source_target_pairs={{0,32},{32,64},{64,96},{96,0},{1,33},{33,65},{65,97},{97,1},{2,34}... | collective-permute-start | bytes 786440 | tf_op jit(solution)/shard_map/ppermute | solution.py:348
  80.4 4.6 %collective-permute-start.17 = (bf16[2048,128]{1,0:T(8,128)(2,1)S(1)}, bf16[2048,128]{1,0:T(8,128)(2,1)S(1)}, u32[]{:S(2)}, u32[]{:S(2)}) collective-permute-start(bf16[2048,128]{1,0:T(8,128)(2,1)S(1)} %get-tuple-element.44), channel_id=1, source_target_pairs={{0,4},{4,0},{1,5},{5,1},{2,6},{6,2},{3,7},{7,3},{8,12},{12,8},{9,1... | collective-permute-start | bytes 1572872 | tf_op jit(solution)/shard_map/ppermute | solution.py:352
  80.5 14.7 %collective-permute-start.16 = (bf16[1024,128]{1,0:T(8,128)(2,1)S(1)}, bf16[1024,128]{1,0:T(8,128)(2,1)S(1)}, u32[]{:S(2)}, u32[]{:S(2)}) collective-permute-start(bf16[1024,128]{1,0:T(8,128)(2,1)S(1)} %middle.1.sum_ref), channel_id=1, source_target_pairs={{0,3},{1,0},{2,1},{3,2},{4,7},{5,4},{6,5},{7,6},{8,11},{9,8},{10,9... | collective-permute-start | bytes 786440 | tf_op jit(solution)/shard_map/ppermute | solution.py:344
  83.3 11.8 %collective-permute-start.15 = (bf16[1024,128]{1,0:T(8,128)(2,1)S(1)}, bf16[1024,128]{1,0:T(8,128)(2,1)S(1)}, u32[]{:S(2)}, u32[]{:S(2)}) collective-permute-start(bf16[1024,128]{1,0:T(8,128)(2,1)S(1)} %middle.1.sum_ref), channel_id=1, source_target_pairs={{0,2},{1,3},{2,0},{3,1},{4,6},{5,7},{6,4},{7,5},{8,10},{9,11},{10,... | collective-permute-start | bytes 786440 | tf_op jit(solution)/shard_map/ppermute | solution.py:344
  84.1 14.7 %collective-permute-start.14 = (bf16[1024,128]{1,0:T(8,128)(2,1)S(1)}, bf16[1024,128]{1,0:T(8,128)(2,1)S(1)}, u32[]{:S(2)}, u32[]{:S(2)}) collective-permute-start(bf16[1024,128]{1,0:T(8,128)(2,1)S(1)} %middle.1.sum_ref), channel_id=1, source_target_pairs={{0,1},{1,2},{2,3},{3,0},{4,5},{5,6},{6,7},{7,4},{8,9},{9,10},{10,1... | collective-permute-start | bytes 786440 | tf_op jit(solution)/shard_map/ppermute | solution.py:344
  85.1 13.7 %collective-permute-start.18 = (bf16[512,128]{1,0:T(8,128)(2,1)S(1)}, bf16[512,128]{1,0:T(8,128)(2,1)S(1)}, u32[]{:S(2)}, u32[]{:S(2)}) collective-permute-start(bf16[512,128]{1,0:T(8,128)(2,1)S(1)} %get-tuple-element.46), channel_id=1, source_target_pairs={{0,24},{8,0},{16,8},{24,16},{1,25},{9,1},{17,9},{25,17},{2,26},{10... | collective-permute-start | bytes 393224 | tf_op jit(solution)/shard_map/ppermute | solution.py:348
  86.3 12.5 %collective-permute-start.19 = (bf16[512,128]{1,0:T(8,128)(2,1)S(1)}, bf16[512,128]{1,0:T(8,128)(2,1)S(1)}, u32[]{:S(2)}, u32[]{:S(2)}) collective-permute-start(bf16[512,128]{1,0:T(8,128)(2,1)S(1)} %get-tuple-element.47), channel_id=1, source_target_pairs={{0,16},{8,24},{16,0},{24,8},{1,17},{9,25},{17,1},{25,9},{2,18},{10... | collective-permute-start | bytes 393224 | tf_op jit(solution)/shard_map/ppermute | solution.py:348
  95.1 6.2 %collective-permute-start.20 = (bf16[512,128]{1,0:T(8,128)(2,1)S(1)}, bf16[512,128]{1,0:T(8,128)(2,1)S(1)}, u32[]{:S(2)}, u32[]{:S(2)}) collective-permute-start(bf16[512,128]{1,0:T(8,128)(2,1)S(1)} %get-tuple-element.48), channel_id=1, source_target_pairs={{0,8},{8,16},{16,24},{24,0},{1,9},{9,17},{17,25},{25,1},{2,10},{10... | collective-permute-start | bytes 393224 | tf_op jit(solution)/shard_map/ppermute | solution.py:348

commit v3 on v2

--- a/solution.py
+++ b/solution.py
@@ -71,50 +71,90 @@
     return key_row <= query_row
 
 
-def stats_kernel(
-    order_ref, near_ref, far_ref, kv0_ref, kv1_ref, kv2_ref, kv3_ref, own_ref, swapped_ref,
-    q_ref, kv_ref, top_ref, total_ref, weighted_ref,
-):
+def query_place(a):
+    y, c = lax.axis_index("y"), lax.axis_index("c")
+    return 2 * (((y + 4 - a % 4) % 4) * 2 + (c + a // 4) % 2)
+
+
+def in_flight(begin, finish, depth):
+    waiting = []
+
+    def tile(a, q_which, keys, masked):
+        for b, k_which in keys:
+            waiting.append(begin(a, q_which, b, k_which, masked))
+            if len(waiting) > depth:
+                finish(waiting.pop(0))
+
+    def drain():
+        while waiting:
+            finish(waiting.pop(0))
+
+    return tile, drain
+
+
+def run_tiles(order_ref, tile, drain, pieces):
+    start, step = 0, max(2, 4 // len(pieces))
+    if 0 in pieces:
+        one_query_piece(order_ref, tile, 0, pieces, True)
+        one_query_piece(order_ref, tile, 1, pieces, False)
+        start, step = 2, 3 if len(pieces) == 1 else 2
+        drain()
+
+    def some(i, carry):
+        for j in range(step):
+            one_query_piece(order_ref, tile, start + i * step + j, pieces, False)
+        drain()
+        return carry
+
+    lax.fori_loop(0, (8 - start) // step, some, 0)
+
+
+def stats_kernel(pieces, first, last, *refs):
+    refs = list(refs)
+    order_ref, near_ref, far_ref = refs[:3]
+    del refs[:3]
+    kv_refs = refs[: len(pieces)]
+    del refs[: len(pieces)]
+    before = [] if first else refs[:3]
+    del refs[: len(before)]
+    if last:
+        out_ref = refs.pop(0)
+        q_ref, kv_ref, top_ref, total_ref, weighted_ref = refs
+    else:
+        top_ref, total_ref, weighted_ref, q_ref, kv_ref = refs
     q_ref[0:4] = near_ref[...].reshape(4, PIECE, DH)
     q_ref[4:8] = far_ref[...].reshape(4, PIECE, DH)
-    for b, ref in enumerate((kv0_ref, kv1_ref, kv2_ref, kv3_ref)):
-        kv_ref[b] = ref[...]
-    top_ref[...] = jnp.full(top_ref.shape, NEG, F32)
-    total_ref[...] = jnp.zeros(total_ref.shape, F32)
-    weighted_ref[...] = jnp.zeros(weighted_ref.shape, F32)
-
-    def tile(a, q_which, keys, masked):
-        slot = a * 2 + q_which
+    for i, ref in enumerate(kv_refs):
+        kv_ref[i] = ref[...]
+    if first:
+        top_ref[...] = jnp.full(top_ref.shape, NEG, F32)
+        total_ref[...] = jnp.zeros(total_ref.shape, F32)
+        weighted_ref[...] = jnp.zeros(weighted_ref.shape, F32)
+    else:
+        for ref, source in zip((top_ref, total_ref, weighted_ref), before):
+            ref[...] = source[...]
+
+    def begin(a, q_which, b, k_which, masked):
+        scores, dprobs = products(q_ref, kv_ref, a, q_which, pieces.index(b), k_which)
+        if masked:
+            scores = jnp.where(diagonal_visible(), scores, NEG)
+        return a * 2 + q_which, masked, scores.reshape(32, 8, SPAN), dprobs.reshape(32, 8, SPAN)
+
+    def finish(state):
+        slot, masked, scores, dprobs = state
         old = top_ref[slot]
-        top = old
-        parts = []
-        for b, k_which in keys:
-            scores, dprobs = products(q_ref, kv_ref, a, q_which, b, k_which)
-            if masked:
-                scores = jnp.where(diagonal_visible(), scores, NEG)
-            parts.append((scores.reshape(32, 8, SPAN), dprobs.reshape(32, 8, SPAN)))
-            top = jnp.maximum(top, jnp.max(parts[-1][0], axis=0))
+        top = jnp.maximum(old, jnp.max(scores, axis=0))
         shrink = jnp.exp2(old - top)
-        total = total_ref[slot] * shrink
-        weighted = weighted_ref[slot] * shrink
-        for scores, dprobs in parts:
-            expon = jnp.exp2(scores - top[None])
-            if masked:
-                expon = jnp.where(diagonal_visible().reshape(32, 8, SPAN), expon, 0.0)
-            total = total + jnp.sum(expon, axis=0)
-            weighted = weighted + jnp.sum(expon * dprobs, axis=0)
+        expon = jnp.exp2(scores - top[None])
+        if masked:
+            expon = jnp.where(diagonal_visible().reshape(32, 8, SPAN), expon, 0.0)
         top_ref[slot] = top
-        total_ref[slot] = total
-        weighted_ref[slot] = weighted
-
-    pieces = (0, 1, 2, 3)
-    one_query_piece(order_ref, tile, 0, pieces, True)
-
-    def one(a, carry):
-        one_query_piece(order_ref, tile, a, pieces, False)
-        return carry
-
-    lax.fori_loop(1, 8, one, 0)
+        total_ref[slot] = total_ref[slot] * shrink + jnp.sum(expon, axis=0)
+        weighted_ref[slot] = weighted_ref[slot] * shrink + jnp.sum(expon * dprobs, axis=0)
+
+    run_tiles(order_ref, *in_flight(begin, finish, 2), pieces)
+    if not last:
+        return
     for slot in range(16):
         tops = top_ref[slot]
         top = jnp.max(tops, axis=0, keepdims=True)
@@ -124,28 +164,22 @@
             jnp.sum(total_ref[slot] * factor, axis=0, keepdims=True),
             jnp.sum(weighted_ref[slot] * factor, axis=0, keepdims=True),
         )
-        other = (slot + 8) % 16
+        place = query_place(slot // 2) + slot % 2
         for kind, row in enumerate(rows):
-            own_ref[kind, pl.ds(slot, 1), :] = row
-            swapped_ref[kind, pl.ds(other, 1), :] = row
-
-
-def norm_and_delta(stat_refs, norm_ref, delta_ref):
-    for a in range(8):
-        dc, dy = a // 4, a % 4
-        found = []
-        for k, ref in enumerate(stat_refs):
-            begin = 2 * (4 * dc + (dy - k) % 4)
-            found.append([ref[kind, pl.ds(begin, 2), :] for kind in range(3)])
-        top = functools.reduce(jnp.maximum, [f[0] for f in found])
-        factors = [jnp.exp2(f[0] - top) for f in found]
-        total = sum(f[1] * g for f, g in zip(found, factors))
-        weighted = sum(f[2] * g for f, g in zip(found, factors))
-        norm = top + jnp.log2(total)
-        delta = weighted / total
-        for which in range(2):
-            norm_ref[2 * a + which] = jnp.broadcast_to(norm[which : which + 1], (8, SPAN))
-            delta_ref[2 * a + which] = jnp.broadcast_to(delta[which : which + 1], (8, SPAN))
+            out_ref[kind, pl.ds(place, 1), :] = row
+
+
+def norm_and_delta(stat_refs, sum_ref, norm_ref, delta_ref):
+    found = [[ref[kind] for kind in range(3)] for ref in stat_refs]
+    top = functools.reduce(jnp.maximum, [f[0] for f in found])
+    factors = [jnp.exp2(f[0] - top) for f in found]
+    total = sum(f[1] * g for f, g in zip(found, factors))
+    sum_ref[0] = top + jnp.log2(total)
+    sum_ref[1] = sum(f[2] * g for f, g in zip(found, factors)) / total
+    for slot in range(16):
+        place = query_place(slot // 2) + slot % 2
+        norm_ref[slot] = jnp.broadcast_to(sum_ref[0, pl.ds(place, 1), :], (8, SPAN))
+        delta_ref[slot] = jnp.broadcast_to(sum_ref[1, pl.ds(place, 1), :], (8, SPAN))
 
 
 def grads_kernel(pieces, first, last, *refs):
@@ -158,10 +192,10 @@
     dkv_refs = dict(zip(pieces, refs[: len(pieces)]))
     del refs[: len(pieces)]
     dq_outs = [refs.pop(0), refs.pop(0)] if last else [refs.pop(0)]
-    q_ref, kv_ref, norm_ref, delta_ref, dk_ref, dv_ref, kt_ref = refs[:7]
-    dqt_ref = refs[7] if last else dq_outs[0]
-
-    norm_and_delta(stat_refs, norm_ref, delta_ref)
+    q_ref, kv_ref, sum_ref, norm_ref, delta_ref, dk_ref, dv_ref, kt_ref = refs[:8]
+    dqt_ref = refs[8] if last else dq_outs[0]
+
+    norm_and_delta(stat_refs, sum_ref, norm_ref, delta_ref)
     q_ref[0:4] = near_ref[...].reshape(4, PIECE, DH)
     q_ref[4:8] = far_ref[...].reshape(4, PIECE, DH)
     for i, b in enumerate(pieces):
@@ -175,46 +209,32 @@
     else:
         dqt_ref[...] = dqt_in[...]
 
-    def tile(a, q_which, keys, masked):
+    def begin(a, q_which, b, k_which, masked):
         slot = a * 2 + q_which
-        norm = norm_ref[slot][None]
-        delta = delta_ref[slot][None]
         queries = half(q_ref, a, q_which, 0)
         out_grads = half(q_ref, a, q_which, 1)
-        dqt = None
-        for b, k_which in keys:
-            i = pieces.index(b)
-            key_slot = 2 * i + k_which
-            scores = lax.dot_general(
-                half(kv_ref, i, k_which, 0), queries, NT, preferred_element_type=F32
-            ) * SCALE2
-            dprobs = lax.dot_general(
-                half(kv_ref, i, k_which, 1), out_grads, NT, preferred_element_type=F32
-            )
-            probs = jnp.exp2(scores.reshape(32, 8, SPAN) - norm)
-            if masked:
-                probs = jnp.where(diagonal_visible().reshape(32, 8, SPAN), probs, 0.0)
-            dscores = probs * (dprobs.reshape(32, 8, SPAN) - delta)
-            probs = probs.reshape(SPAN, SPAN).astype(BF16)
-            dscores = dscores.reshape(SPAN, SPAN).astype(BF16)
-            dv_ref[key_slot] += lax.dot_general(probs, out_grads, NN, preferred_element_type=F32)
-            dk_ref[key_slot] += lax.dot_general(dscores, queries, NN, preferred_element_type=F32)
-            term = lax.dot_general(kt_ref[key_slot], dscores, NN, preferred_element_type=F32)
-            dqt = term if dqt is None else dqt + term
-        dqt_ref[slot] += dqt
-
-    start, step = 0, max(1, 4 // len(pieces))
-    if 0 in pieces:
-        one_query_piece(order_ref, tile, 0, pieces, True)
-        one_query_piece(order_ref, tile, 1, pieces, False)
-        start, step = 2, 3
-
-    def some(i, carry):
-        for j in range(step):
-            one_query_piece(order_ref, tile, start + i * step + j, pieces, False)
-        return carry
-
-    lax.fori_loop(0, (8 - start) // step, some, 0)
+        i = pieces.index(b)
+        scores = lax.dot_general(
+            half(kv_ref, i, k_which, 0), queries, NT, preferred_element_type=F32
+        ) * SCALE2
+        dprobs = lax.dot_general(
+            half(kv_ref, i, k_which, 1), out_grads, NT, preferred_element_type=F32
+        )
+        return slot, 2 * i + k_which, masked, queries, out_grads, scores, dprobs
+
+    def finish(state):
+        slot, key_slot, masked, queries, out_grads, scores, dprobs = state
+        probs = jnp.exp2(scores.reshape(32, 8, SPAN) - norm_ref[slot][None])
+        if masked:
+            probs = jnp.where(diagonal_visible().reshape(32, 8, SPAN), probs, 0.0)
+        dscores = probs * (dprobs.reshape(32, 8, SPAN) - delta_ref[slot][None])
+        probs = probs.reshape(SPAN, SPAN).astype(BF16)
+        dscores = dscores.reshape(SPAN, SPAN).astype(BF16)
+        dv_ref[key_slot] += lax.dot_general(probs, out_grads, NN, preferred_element_type=F32)
+        dk_ref[key_slot] += lax.dot_general(dscores, queries, NN, preferred_element_type=F32)
+        dqt_ref[slot] += lax.dot_general(kt_ref[key_slot], dscores, NN, preferred_element_type=F32)
+
+    run_tiles(order_ref, *in_flight(begin, finish, 1), pieces)
     for i, b in enumerate(pieces):
         ref = dkv_refs[b]
         for which in range(2):
@@ -267,21 +287,24 @@
 PIECE = 4 * SPAN
 
 
-def call_stats(span_order, q_near, q_far, kvs):
-    shape = jax.ShapeDtypeStruct((3, 16, SPAN), F32)
+def call_stats(pieces, first, last, span_order, q_near, q_far, kvs, before):
+    shape = (3, 16, SPAN) if last else (16, 8, SPAN)
+    running = [pltpu.VMEM((16, 8, SPAN), F32)] * 3 if last else []
+    args = [span_order, q_near, q_far, *[kvs[b] for b in pieces], *before]
     return pl.pallas_call(
-        stats_kernel,
-        out_shape=(shape, shape),
-        in_specs=[SMEM] + [VMEM] * 6,
-        out_specs=(VMEM, VMEM),
-        scratch_shapes=[pltpu.VMEM((8, PIECE, DH), BF16), pltpu.VMEM((4, PIECE, DH), BF16)]
-        + [pltpu.VMEM((16, 8, SPAN), F32)] * 3,
+        functools.partial(stats_kernel, pieces, first, last),
+        out_shape=(jax.ShapeDtypeStruct(shape, F32),) * (1 if last else 3),
+        in_specs=[SMEM] + [VMEM] * (len(args) - 1),
+        out_specs=(VMEM,) * (1 if last else 3),
+        scratch_shapes=[pltpu.VMEM((8, PIECE, DH), BF16), pltpu.VMEM((len(pieces), PIECE, DH), BF16)] + running,
         compiler_params=pltpu.CompilerParams(vmem_limit_bytes=32 * 2**20),
         cost_estimate=pl.CostEstimate(
-            flops=65 * 2 * 2 * SPAN * SPAN * DH, bytes_accessed=3 * 2**20, transcendentals=65 * SPAN * SPAN
+            flops=16 * len(pieces) * 2 * 2 * SPAN * SPAN * DH,
+            bytes_accessed=3 * 2**20,
+            transcendentals=16 * len(pieces) * SPAN * SPAN,
         ),
         name="stats",
-    )(span_order, q_near, q_far, *kvs)
+    )(*args)
 
 
 def call_grads(pieces, first, last, span_order, stats, q_near, q_far, kvs, dqt):
@@ -300,6 +323,7 @@
         scratch_shapes=[
             pltpu.VMEM((8, PIECE, DH), BF16),
             pltpu.VMEM((len(pieces), PIECE, DH), BF16),
+            pltpu.VMEM((2, 16, SPAN), F32),
             pltpu.VMEM((16, 8, SPAN), F32),
             pltpu.VMEM((16, 8, SPAN), F32),
             pltpu.VMEM((2 * len(pieces), SPAN, DH), F32),
@@ -352,21 +376,25 @@
     return lax.ppermute(value, "c", [(0, 1), (1, 0)])
 
 
+def merged(mine, theirs):
+    top = jnp.maximum(mine[0], theirs[0])
+    mine_by, theirs_by = jnp.exp2(mine[0] - top), jnp.exp2(theirs[0] - top)
+    return jnp.stack([top, mine[1] * mine_by + theirs[1] * theirs_by, mine[2] * mine_by + theirs[2] * theirs_by])
+
+
 def local(span_order, queries, key_rows, value_rows, out_grads):
     q_own, kv_own = call_pack(queries, key_rows, value_rows, out_grads)
     q_got = [back(q_own, "y", k) for k in (1, 2, 3)]
     kv_got = [back(kv_own, "z", k) for k in (1, 2, 3)]
-    q_got, kv_got = lax.optimization_barrier((q_got, kv_got))
+    q_got, kv_got[0], kv_got[2] = lax.optimization_barrier((q_got, kv_got[0], kv_got[2]))
     q_near = jnp.concatenate([q_own] + q_got, axis=0)
     q_far = swap_core(q_near)
     kvs = [kv_own] + kv_got
 
-    mine, for_other = call_stats(span_order, q_near, q_far, kvs)
-    theirs = swap_core(for_other)
-    top = jnp.maximum(mine[0], theirs[0])
-    mine_by, theirs_by = jnp.exp2(mine[0] - top), jnp.exp2(theirs[0] - top)
-    both = jnp.stack([top, mine[1] * mine_by + theirs[1] * theirs_by, mine[2] * mine_by + theirs[2] * theirs_by])
-    stats = [both] + [back(both, "y", k) for k in (1, 2, 3)]
+    running = call_stats((0, 1, 3), True, False, span_order, q_near, q_far, kvs, ())
+    (stats,) = call_stats((2,), False, True, span_order, q_near, q_far, kvs, running)
+    stats = merged(stats, swap_core(stats))
+    stats = [stats] + [back(stats, "y", k) for k in (1, 2, 3)]
 
     common = (span_order, stats, q_near, q_far, kvs)
     (dkv1, dkv2, dkv3), (dqt,) = call_grads((1, 2, 3), True, False, *common, None)

time: 103 us -> 92.8 us (0.901)
  Pallas kernels: 33.4 us -> 26.2 us
  waiting for transfers between devices: 41.4 us -> 36.5 us
  starting transfers between devices: 25.4 us -> 27.1 us
    pallas_call x2, Pallas kernels: 20.3 us -> 14.3 us  [call_grads(): pl.pallas_call(functools.partial(grads_kernel, pieces, first, last), out_...]
    ppermute x12, waiting for transfers between devices: 29.2 us -> 25 us  [back(): return lax.ppermute(value, axis, [(i, (i + k) % 4) for i in range(4)])]
    ppermute x3, waiting for transfers between devices: 3.65 us -> 1.22 us  [swap_core(): return lax.ppermute(value, 'c', [(0, 1), (1, 0)])]
    ppermute x6, starting transfers between devices: 4.94 us -> 7.24 us  [ahead(): return lax.ppermute(value, axis, [(i, (i - k) % 4) for i in range(4)])]
    ppermute x6, waiting for transfers between devices: 8.59 us -> 10.3 us  [ahead(): return lax.ppermute(value, axis, [(i, (i - k) % 4) for i in range(4)])]
    pallas_call x1 -> x2, Pallas kernels: 10.1 us -> 8.88 us  [call_stats(): pl.pallas_call(functools.partial(stats_kernel, pieces, first, last), out_...]
  transfers between devices with their start and end apart: 21 -> 21, of which waited for: 16 -> 13; matrix products, arithmetic and copies ran while one was open for 1% -> 1% of each run, Pallas kernels for 6% -> 12%
where the time goes in v3:
time: 92.8 us; the launch traced here: 91.8 us
  waiting for transfers between devices  36.5 us (39%)
  starting transfers between devices  27.1 us (29%)
  Pallas kernels  26.2 us (28%)
  local copies, waits for them, and re-layouts  1.17 us (1%)
    ppermute x12, waiting for transfers between devices, back(): return lax.ppermute(value, axis, [(i, (i + k) % 4) for i in range(4)])  25 us
    ppermute x12, starting transfers between devices, back(): return lax.ppermute(value, axis, [(i, (i + k) % 4) for i in range(4)])  19.6 us
    pallas_call x2, Pallas kernels, call_grads(): pl.pallas_call(functools.partial(grads_kernel, pieces, first, last), out_...  14.3 us
    ppermute x6, waiting for transfers between devices, ahead(): return lax.ppermute(value, axis, [(i, (i - k) % 4) for i in range(4)])  10.3 us
    pallas_call x2, Pallas kernels, call_stats(): pl.pallas_call(functools.partial(stats_kernel, pieces, first, last), out_...  8.88 us
    ppermute x6, starting transfers between devices, ahead(): return lax.ppermute(value, axis, [(i, (i - k) % 4) for i in range(4)])  7.24 us
    pallas_call x1, Pallas kernels, call_pack(): pl.pallas_call(pack_kernel, out_shape=(jax.ShapeDtypeStruct((PIECE, DH),...  1.94 us
  transfers between devices with their start and end apart: 21, of which 13 were waited for; matrix products, arithmetic and copies ran while one was open for 1% of the time, Pallas kernels for 12%

profile of v3, /device:TPU:0, one launch (start us, length us, event | category | flops | bytes accessed | tf_op | source)
XLA Modules:
  0.0 91.8 jit_solution(3518641601903268467)
XLA Ops:
  0.6 1.9 %pack.1 = (bf16[1024,128]{1,0:T(8,128)(2,1)}, bf16[1024,128]{1,0:T(8,128)(2,1)}) custom-call(bf16[512,128]{1,0:T(8,128)(2,1)} %queries_ref.1, bf16[512,128]{1,0:T(8,128)(2,1)} %keys_ref.1, bf16[512,128]{1,0:T(8,128)(2,1)} %values_ref.1, bf16[512,128]{1,0:T(8,128)(2,1)} %grads_ref.1), custom_call_target="tpu_custom_call" | custom-call | tf_op jit(solution)/shard_map/pack/pallas_call | solution.py:356
  2.6 3.2 %collective-permute-start.2 = (bf16[1024,128]{1,0:T(8,128)(2,1)}, bf16[1024,128]{1,0:T(8,128)(2,1)S(1)}, u32[]{:S(2)}, u32[]{:S(2)}) collective-permute-start(bf16[1024,128]{1,0:T(8,128)(2,1)} %get-tuple-element.26), channel_id=1, source_target_pairs={{0,24},{8,0},{16,8},{24,16},{1,25},{9,1},{17,9},{25,17},{2,26},{10... | collective-permute-start | bytes 786440 | tf_op jit(solution)/shard_map/ppermute | solution.py:368
  7.4 4.0 %collective-permute-start.4 = (bf16[1024,128]{1,0:T(8,128)(2,1)}, bf16[1024,128]{1,0:T(8,128)(2,1)S(1)}, u32[]{:S(2)}, u32[]{:S(2)}) collective-permute-start(bf16[1024,128]{1,0:T(8,128)(2,1)} %get-tuple-element.27.refs_3_.refs_7_), channel_id=1, source_target_pairs={{0,96},{32,0},{64,32},{96,64},{1,97},{33,1},{65,33},{97,65},{2,98}... | collective-permute-start | bytes 786440 | tf_op jit(solution)/shard_map/ppermute | solution.py:368
  12.4 4.9 %collective-permute-done.2 = bf16[1024,128]{1,0:T(8,128)(2,1)S(1)} collective-permute-done((bf16[1024,128]{1,0:T(8,128)(2,1)}, bf16[1024,128]{1,0:T(8,128)(2,1)S(1)}, u32[]{:S(2)}, u32[]{:S(2)}) %collective-permute-start.2) | collective-permute-done | bytes 262176 | tf_op jit(solution)/shard_map/ppermute | solution.py:368
  17.3 3.6 %collective-permute-done = bf16[1024,128]{1,0:T(8,128)(2,1)S(1)} collective-permute-done((bf16[1024,128]{1,0:T(8,128)(2,1)}, bf16[1024,128]{1,0:T(8,128)(2,1)S(1)}, u32[]{:S(2)}, u32[]{:S(2)}) %collective-permute-start) | collective-permute-done | bytes 262176 | tf_op jit(solution)/shard_map/ppermute | solution.py:368
  21.1 4.0 %collective-permute-start.6 = (bf16[1024,128]{1,0:T(8,128)(2,1)S(1)}, bf16[1024,128]{1,0:T(8,128)(2,1)S(1)}, u32[]{:S(2)}, u32[]{:S(2)}) collective-permute-start(bf16[1024,128]{1,0:T(8,128)(2,1)S(1)} %copy-done), channel_id=1, source_target_pairs={{0,64},{32,96},{64,0},{96,32},{1,65},{33,97},{65,1},{97,33},{2,66}... | collective-permute-start | bytes 786440 | tf_op jit(solution)/shard_map/ppermute | solution.py:368
  25.2 6.0 %stats.2 = (f32[16,8,256]{2,1,0:T(8,128)S(1)}, f32[16,8,256]{2,1,0:T(8,128)S(1)}, f32[16,8,256]{2,1,0:T(8,128)S(1)}) custom-call(s32[32,2]{1,0:T(8,128)S(1)} %copy.11.refs_0_, bf16[4096,128]{1,0:T(8,128)(2,1)S(1)} %constant_dynamic-update-slice_fusion.refs_1_.refs_5_, bf16[4096,128]{1,0:T(8,128)(2,1)S(1)} %collective-permute-done.5.refs_2_.refs_6_, ...), custom_call_target="tpu_custom_call" | custom-call | flops 1610612736 | bytes 3145728 | tf_op jit(solution)/shard_map/stats/pallas_call | solution.py:294
  31.9 2.9 %stats.3 = f32[3,16,256]{2,1,0:T(8,128)S(1)} custom-call(s32[32,2]{1,0:T(8,128)S(1)} %copy.11.refs_0_, bf16[4096,128]{1,0:T(8,128)(2,1)S(1)} %constant_dynamic-update-slice_fusion.refs_1_.refs_5_, bf16[4096,128]{1,0:T(8,128)(2,1)S(1)} %collective-permute-done.5.refs_2_.refs_6_, bf16[1024,128]{1,0:T(8,128)(2,1)S(1)} %collective-permute-done.6.refs_3_.refs_8_, ...), custom_call_target="tpu_custom_call" | custom-call | flops 536870912 | bytes 3145728 | tf_op jit(solution)/shard_map/stats/pallas_call | solution.py:294
  34.9 1.2 %collective-permute-done.7 = f32[3,16,256]{2,1,0:T(8,128)S(1)} collective-permute-done((f32[3,16,256]{2,1,0:T(8,128)S(1)}, f32[3,16,256]{2,1,0:T(8,128)S(1)}, u32[]{:S(2)}, u32[]{:S(2)}) %collective-permute-start.7) | collective-permute-done | bytes 49184 | tf_op jit(solution)/shard_map/ppermute | solution.py:376
  36.9 1.6 %collective-permute-start.9 = (f32[3,16,256]{2,1,0:T(8,128)S(1)}, f32[3,16,256]{2,1,0:T(8,128)S(1)}, u32[]{:S(2)}, u32[]{:S(2)}) collective-permute-start(f32[3,16,256]{2,1,0:T(8,128)S(1)} %pad_maximum_fusion.refs_1_), channel_id=1, source_target_pairs={{0,16},{8,24},{16,0},{24,8},{1,17},{9,25},{17,1},{25,9},{2,18},{10... | collective-permute-start | bytes 147464 | tf_op jit(solution)/shard_map/ppermute | solution.py:368
  38.5 2.1 %collective-permute-done.10.refs_4_ = f32[3,16,256]{2,1,0:T(8,128)S(1)} collective-permute-done((f32[3,16,256]{2,1,0:T(8,128)S(1)}, f32[3,16,256]{2,1,0:T(8,128)S(1)}, u32[]{:S(2)}, u32[]{:S(2)}) %collective-permute-start.10) | collective-permute-done | bytes 49184 | tf_op jit(solution)/shard_map/ppermute | solution.py:368
  40.6 2.0 %collective-permute-done.9.refs_3_ = f32[3,16,256]{2,1,0:T(8,128)S(1)} collective-permute-done((f32[3,16,256]{2,1,0:T(8,128)S(1)}, f32[3,16,256]{2,1,0:T(8,128)S(1)}, u32[]{:S(2)}, u32[]{:S(2)}) %collective-permute-start.9) | collective-permute-done | bytes 49184 | tf_op jit(solution)/shard_map/ppermute | solution.py:368
  42.6 1.2 %collective-permute-done.8.refs_2_ = f32[3,16,256]{2,1,0:T(8,128)S(1)} collective-permute-done((f32[3,16,256]{2,1,0:T(8,128)S(1)}, f32[3,16,256]{2,1,0:T(8,128)S(1)}, u32[]{:S(2)}, u32[]{:S(2)}) %collective-permute-start.8) | collective-permute-done | bytes 49184 | tf_op jit(solution)/shard_map/ppermute | solution.py:368
  43.8 9.5 %grads.2 = (bf16[1024,128]{1,0:T(8,128)(2,1)S(1)}, bf16[1024,128]{1,0:T(8,128)(2,1)S(1)}, bf16[1024,128]{1,0:T(8,128)(2,1)S(1)}, f32[16,128,256]{2,1,0:T(8,128)S(1)}) custom-call(s32[32,2]{1,0:T(8,128)S(1)} %copy.11.refs_0_, f32[3,16,256]{2,1,0:T(8,128)S(1)} %pad_maximum_fusion.refs_1_, f32[3,16,256]{2,1,0:T(8,128)S(1)} %collective-permute-done.8.refs_2_, ...), custom_call_target="tpu_custom_call" | custom-call | flops 4026531840 | bytes 4194304 | tf_op jit(solution)/shard_map/grads/pallas_call | solution.py:318
  53.3 2.7 %collective-permute-start.11 = (bf16[1024,128]{1,0:T(8,128)(2,1)S(1)}, bf16[1024,128]{1,0:T(8,128)(2,1)S(1)}, u32[]{:S(2)}, u32[]{:S(2)}) collective-permute-start(bf16[1024,128]{1,0:T(8,128)(2,1)S(1)} %get-tuple-element.39), channel_id=1, source_target_pairs={{0,96},{32,0},{64,32},{96,64},{1,97},{33,1},{65,33},{97,65},{2,98}... | collective-permute-start | bytes 786440 | tf_op jit(solution)/shard_map/ppermute | solution.py:372
  56.1 1.3 %collective-permute-start.13 = (bf16[1024,128]{1,0:T(8,128)(2,1)S(1)}, bf16[1024,128]{1,0:T(8,128)(2,1)S(1)}, u32[]{:S(2)}, u32[]{:S(2)}) collective-permute-start(bf16[1024,128]{1,0:T(8,128)(2,1)S(1)} %get-tuple-element.41), channel_id=1, source_target_pairs={{0,32},{32,64},{64,96},{96,0},{1,33},{33,65},{65,97},{97,1},{2,34}... | collective-permute-start | bytes 786440 | tf_op jit(solution)/shard_map/ppermute | solution.py:372
  57.4 4.8 %grads.3 = (f32[1024,128]{1,0:T(8,128)S(1)}, f32[2048,128]{1,0:T(8,128)S(1)}, bf16[2048,128]{1,0:T(8,128)(2,1)S(1)}) custom-call(s32[32,2]{1,0:T(8,128)S(1)} %copy.11.refs_0_, f32[3,16,256]{2,1,0:T(8,128)S(1)} %pad_maximum_fusion.refs_1_, f32[3,16,256]{2,1,0:T(8,128)S(1)} %collective-permute-done.8.refs_2_, ...), custom_call_target="tpu_custom_call" | custom-call | flops 1342177280 | bytes 4194304 | tf_op jit(solution)/shard_map/grads/pallas_call | solution.py:318
  62.1 4.4 %collective-permute-done.11.z1_ref = bf16[1024,128]{1,0:T(8,128)(2,1)S(1)} collective-permute-done((bf16[1024,128]{1,0:T(8,128)(2,1)S(1)}, bf16[1024,128]{1,0:T(8,128)(2,1)S(1)}, u32[]{:S(2)}, u32[]{:S(2)}) %collective-permute-start.11) | collective-permute-done | bytes 262176 | tf_op jit(solution)/shard_map/ppermute | solution.py:372
  66.8 3.0 %collective-permute-done.13.z3_ref = bf16[1024,128]{1,0:T(8,128)(2,1)S(1)} collective-permute-done((bf16[1024,128]{1,0:T(8,128)(2,1)S(1)}, bf16[1024,128]{1,0:T(8,128)(2,1)S(1)}, u32[]{:S(2)}, u32[]{:S(2)}) %collective-permute-start.13) | collective-permute-done | bytes 262176 | tf_op jit(solution)/shard_map/ppermute | solution.py:372
  70.1 2.8 %collective-permute-start.16 = (bf16[1024,128]{1,0:T(8,128)(2,1)S(1)}, bf16[1024,128]{1,0:T(8,128)(2,1)S(1)}, u32[]{:S(2)}, u32[]{:S(2)}) collective-permute-start(bf16[1024,128]{1,0:T(8,128)(2,1)S(1)} %middle.1.sum_ref), channel_id=1, source_target_pairs={{0,3},{1,0},{2,1},{3,2},{4,7},{5,4},{6,5},{7,6},{8,11},{9,8},{10,9... | collective-permute-start | bytes 786440 | tf_op jit(solution)/shard_map/ppermute | solution.py:368
  74.7 1.8 %collective-permute-start.18 = (bf16[512,128]{1,0:T(8,128)(2,1)S(1)}, bf16[512,128]{1,0:T(8,128)(2,1)S(1)}, u32[]{:S(2)}, u32[]{:S(2)}) collective-permute-start(bf16[512,128]{1,0:T(8,128)(2,1)S(1)} %get-tuple-element.46), channel_id=1, source_target_pairs={{0,24},{8,0},{16,8},{24,16},{1,25},{9,1},{17,9},{25,17},{2,26},{10... | collective-permute-start | bytes 393224 | tf_op jit(solution)/shard_map/ppermute | solution.py:372
  77.4 7.4 %collective-permute-done.16.x3_ref = bf16[1024,128]{1,0:T(8,128)(2,1)S(1)} collective-permute-done((bf16[1024,128]{1,0:T(8,128)(2,1)S(1)}, bf16[1024,128]{1,0:T(8,128)(2,1)S(1)}, u32[]{:S(2)}, u32[]{:S(2)}) %collective-permute-start.16) | collective-permute-done | bytes 262176 | tf_op jit(solution)/shard_map/ppermute | solution.py:368
  85.3 3.1 %collective-permute-done.14.x1_ref = bf16[1024,128]{1,0:T(8,128)(2,1)S(1)} collective-permute-done((bf16[1024,128]{1,0:T(8,128)(2,1)S(1)}, bf16[1024,128]{1,0:T(8,128)(2,1)S(1)}, u32[]{:S(2)}, u32[]{:S(2)}) %collective-permute-start.14) | collective-permute-done | bytes 262176 | tf_op jit(solution)/shard_map/ppermute | solution.py:368
  88.4 2.5 %collective-permute-done.20.y3_ref = bf16[512,128]{1,0:T(8,128)(2,1)S(1)} collective-permute-done((bf16[512,128]{1,0:T(8,128)(2,1)S(1)}, bf16[512,128]{1,0:T(8,128)(2,1)S(1)}, u32[]{:S(2)}, u32[]{:S(2)}) %collective-permute-start.20) | collective-permute-done | bytes 131104 | tf_op jit(solution)/shard_map/ppermute | solution.py:372
  (38 shorter events, 9.1 us)
Async XLA Ops:
  0.6 24.4 %copy-start.1 = (s32[32,2]{0,1:T(2,128)S(1)}, s32[32,2]{0,1:T(2,128)}, u32[]{:S(2)}) copy-start(s32[32,2]{0,1:T(2,128)} %param.5) | copy-start | bytes 772
  2.6 18.5 %copy-start = (bf16[1024,128]{1,0:T(8,128)(2,1)S(1)}, bf16[1024,128]{1,0:T(8,128)(2,1)}, u32[]{:S(2)}) copy-start(bf16[1024,128]{1,0:T(8,128)(2,1)} %get-tuple-element.27.refs_3_.refs_7_) | copy-start | bytes 786436
  2.6 14.7 %collective-permute-start.2 = (bf16[1024,128]{1,0:T(8,128)(2,1)}, bf16[1024,128]{1,0:T(8,128)(2,1)S(1)}, u32[]{:S(2)}, u32[]{:S(2)}) collective-permute-start(bf16[1024,128]{1,0:T(8,128)(2,1)} %get-tuple-element.26), channel_id=1, source_target_pairs={{0,24},{8,0},{16,8},{24,16},{1,25},{9,1},{17,9},{25,17},{2,26},{10... | collective-permute-start | bytes 786440 | tf_op jit(solution)/shard_map/ppermute | solution.py:368
  5.8 11.5 %collective-permute-start.1 = (bf16[1024,128]{1,0:T(8,128)(2,1)}, bf16[1024,128]{1,0:T(8,128)(2,1)S(1)}, u32[]{:S(2)}, u32[]{:S(2)}) collective-permute-start(bf16[1024,128]{1,0:T(8,128)(2,1)} %get-tuple-element.26), channel_id=1, source_target_pairs={{0,16},{8,24},{16,0},{24,8},{1,17},{9,25},{17,1},{25,9},{2,18},{10... | collective-permute-start | bytes 786440 | tf_op jit(solution)/shard_map/ppermute | solution.py:368
  6.4 14.5 %collective-permute-start = (bf16[1024,128]{1,0:T(8,128)(2,1)}, bf16[1024,128]{1,0:T(8,128)(2,1)S(1)}, u32[]{:S(2)}, u32[]{:S(2)}) collective-permute-start(bf16[1024,128]{1,0:T(8,128)(2,1)} %get-tuple-element.26), channel_id=1, source_target_pairs={{0,8},{8,16},{16,24},{24,0},{1,9},{9,17},{17,25},{25,1},{2,10},{10... | collective-permute-start | bytes 786440 | tf_op jit(solution)/shard_map/ppermute | solution.py:368
  7.4 13.5 %collective-permute-start.4 = (bf16[1024,128]{1,0:T(8,128)(2,1)}, bf16[1024,128]{1,0:T(8,128)(2,1)S(1)}, u32[]{:S(2)}, u32[]{:S(2)}) collective-permute-start(bf16[1024,128]{1,0:T(8,128)(2,1)} %get-tuple-element.27.refs_3_.refs_7_), channel_id=1, source_target_pairs={{0,96},{32,0},{64,32},{96,64},{1,97},{33,1},{65,33},{97,65},{2,98}... | collective-permute-start | bytes 786440 | tf_op jit(solution)/shard_map/ppermute | solution.py:368
  11.4 9.5 %collective-permute-start.3 = (bf16[1024,128]{1,0:T(8,128)(2,1)}, bf16[1024,128]{1,0:T(8,128)(2,1)S(1)}, u32[]{:S(2)}, u32[]{:S(2)}) collective-permute-start(bf16[1024,128]{1,0:T(8,128)(2,1)} %get-tuple-element.27.refs_3_.refs_7_), channel_id=1, source_target_pairs={{0,32},{32,64},{64,96},{96,0},{1,33},{33,65},{65,97},{97,1},{2,34}... | collective-permute-start | bytes 786440 | tf_op jit(solution)/shard_map/ppermute | solution.py:368
  21.0 4.2 %collective-permute-start.5 = (bf16[4096,128]{1,0:T(8,128)(2,1)S(1)}, bf16[4096,128]{1,0:T(8,128)(2,1)S(1)}, u32[]{:S(2)}, u32[]{:S(2)}) collective-permute-start(bf16[4096,128]{1,0:T(8,128)(2,1)S(1)} %constant_dynamic-update-slice_fusion.refs_1_.refs_5_), channel_id=1, source_target_pairs={{0,4},{4,0},{1,5},{5,1},{2,6},{6,2},{3,7},{7,3},{8,12},{12,8},{9,1... | collective-permute-start | bytes 3145736 | tf_op jit(solution)/shard_map/ppermute | solution.py:376
  21.1 10.8 %collective-permute-start.6 = (bf16[1024,128]{1,0:T(8,128)(2,1)S(1)}, bf16[1024,128]{1,0:T(8,128)(2,1)S(1)}, u32[]{:S(2)}, u32[]{:S(2)}) collective-permute-start(bf16[1024,128]{1,0:T(8,128)(2,1)S(1)} %copy-done), channel_id=1, source_target_pairs={{0,64},{32,96},{64,0},{96,32},{1,65},{33,97},{65,1},{97,33},{2,66}... | collective-permute-start | bytes 786440 | tf_op jit(solution)/shard_map/ppermute | solution.py:368
  34.8 1.3 %collective-permute-start.7 = (f32[3,16,256]{2,1,0:T(8,128)S(1)}, f32[3,16,256]{2,1,0:T(8,128)S(1)}, u32[]{:S(2)}, u32[]{:S(2)}) collective-permute-start(f32[3,16,256]{2,1,0:T(8,128)S(1)} %stats.3), channel_id=1, source_target_pairs={{0,4},{4,0},{1,5},{5,1},{2,6},{6,2},{3,7},{7,3},{8,12},{12,8},{9,1... | collective-permute-start | bytes 147464 | tf_op jit(solution)/shard_map/ppermute | solution.py:376
  36.2 4.4 %collective-permute-start.10 = (f32[3,16,256]{2,1,0:T(8,128)S(1)}, f32[3,16,256]{2,1,0:T(8,128)S(1)}, u32[]{:S(2)}, u32[]{:S(2)}) collective-permute-start(f32[3,16,256]{2,1,0:T(8,128)S(1)} %pad_maximum_fusion.refs_1_), channel_id=1, source_target_pairs={{0,24},{8,0},{16,8},{24,16},{1,25},{9,1},{17,9},{25,17},{2,26},{10... | collective-permute-start | bytes 147464 | tf_op jit(solution)/shard_map/ppermute | solution.py:368
  36.9 5.7 %collective-permute-start.9 = (f32[3,16,256]{2,1,0:T(8,128)S(1)}, f32[3,16,256]{2,1,0:T(8,128)S(1)}, u32[]{:S(2)}, u32[]{:S(2)}) collective-permute-start(f32[3,16,256]{2,1,0:T(8,128)S(1)} %pad_maximum_fusion.refs_1_), channel_id=1, source_target_pairs={{0,16},{8,24},{16,0},{24,8},{1,17},{9,25},{17,1},{25,9},{2,18},{10... | collective-permute-start | bytes 147464 | tf_op jit(solution)/shard_map/ppermute | solution.py:368
  38.5 5.3 %collective-permute-start.8 = (f32[3,16,256]{2,1,0:T(8,128)S(1)}, f32[3,16,256]{2,1,0:T(8,128)S(1)}, u32[]{:S(2)}, u32[]{:S(2)}) collective-permute-start(f32[3,16,256]{2,1,0:T(8,128)S(1)} %pad_maximum_fusion.refs_1_), channel_id=1, source_target_pairs={{0,8},{8,16},{16,24},{24,0},{1,9},{9,17},{17,25},{25,1},{2,10},{10... | collective-permute-start | bytes 147464 | tf_op jit(solution)/shard_map/ppermute | solution.py:368
  53.3 13.2 %collective-permute-start.11 = (bf16[1024,128]{1,0:T(8,128)(2,1)S(1)}, bf16[1024,128]{1,0:T(8,128)(2,1)S(1)}, u32[]{:S(2)}, u32[]{:S(2)}) collective-permute-start(bf16[1024,128]{1,0:T(8,128)(2,1)S(1)} %get-tuple-element.39), channel_id=1, source_target_pairs={{0,96},{32,0},{64,32},{96,64},{1,97},{33,1},{65,33},{97,65},{2,98}... | collective-permute-start | bytes 786440 | tf_op jit(solution)/shard_map/ppermute | solution.py:372
  56.1 10.7 %collective-permute-start.12 = (bf16[1024,128]{1,0:T(8,128)(2,1)S(1)}, bf16[1024,128]{1,0:T(8,128)(2,1)S(1)}, u32[]{:S(2)}, u32[]{:S(2)}) collective-permute-start(bf16[1024,128]{1,0:T(8,128)(2,1)S(1)} %get-tuple-element.40), channel_id=1, source_target_pairs={{0,64},{32,96},{64,0},{96,32},{1,65},{33,97},{65,1},{97,33},{2,66}... | collective-permute-start | bytes 786440 | tf_op jit(solution)/shard_map/ppermute | solution.py:372
  56.1 13.8 %collective-permute-start.13 = (bf16[1024,128]{1,0:T(8,128)(2,1)S(1)}, bf16[1024,128]{1,0:T(8,128)(2,1)S(1)}, u32[]{:S(2)}, u32[]{:S(2)}) collective-permute-start(bf16[1024,128]{1,0:T(8,128)(2,1)S(1)} %get-tuple-element.41), channel_id=1, source_target_pairs={{0,32},{32,64},{64,96},{96,0},{1,33},{33,65},{65,97},{97,1},{2,34}... | collective-permute-start | bytes 786440 | tf_op jit(solution)/shard_map/ppermute | solution.py:372
  70.0 4.6 %collective-permute-start.17 = (bf16[2048,128]{1,0:T(8,128)(2,1)S(1)}, bf16[2048,128]{1,0:T(8,128)(2,1)S(1)}, u32[]{:S(2)}, u32[]{:S(2)}) collective-permute-start(bf16[2048,128]{1,0:T(8,128)(2,1)S(1)} %get-tuple-element.44), channel_id=1, source_target_pairs={{0,4},{4,0},{1,5},{5,1},{2,6},{6,2},{3,7},{7,3},{8,12},{12,8},{9,1... | collective-permute-start | bytes 1572872 | tf_op jit(solution)/shard_map/ppermute | solution.py:376
  70.1 14.7 %collective-permute-start.16 = (bf16[1024,128]{1,0:T(8,128)(2,1)S(1)}, bf16[1024,128]{1,0:T(8,128)(2,1)S(1)}, u32[]{:S(2)}, u32[]{:S(2)}) collective-permute-start(bf16[1024,128]{1,0:T(8,128)(2,1)S(1)} %middle.1.sum_ref), channel_id=1, source_target_pairs={{0,3},{1,0},{2,1},{3,2},{4,7},{5,4},{6,5},{7,6},{8,11},{9,8},{10,9... | collective-permute-start | bytes 786440 | tf_op jit(solution)/shard_map/ppermute | solution.py:368
  72.9 12.4 %collective-permute-start.15 = (bf16[1024,128]{1,0:T(8,128)(2,1)S(1)}, bf16[1024,128]{1,0:T(8,128)(2,1)S(1)}, u32[]{:S(2)}, u32[]{:S(2)}) collective-permute-start(bf16[1024,128]{1,0:T(8,128)(2,1)S(1)} %middle.1.sum_ref), channel_id=1, source_target_pairs={{0,2},{1,3},{2,0},{3,1},{4,6},{5,7},{6,4},{7,5},{8,10},{9,11},{10,... | collective-permute-start | bytes 786440 | tf_op jit(solution)/shard_map/ppermute | solution.py:368
  73.7 14.7 %collective-permute-start.14 = (bf16[1024,128]{1,0:T(8,128)(2,1)S(1)}, bf16[1024,128]{1,0:T(8,128)(2,1)S(1)}, u32[]{:S(2)}, u32[]{:S(2)}) collective-permute-start(bf16[1024,128]{1,0:T(8,128)(2,1)S(1)} %middle.1.sum_ref), channel_id=1, source_target_pairs={{0,1},{1,2},{2,3},{3,0},{4,5},{5,6},{6,7},{7,4},{8,9},{9,10},{10,1... | collective-permute-start | bytes 786440 | tf_op jit(solution)/shard_map/ppermute | solution.py:368
  74.7 13.7 %collective-permute-start.18 = (bf16[512,128]{1,0:T(8,128)(2,1)S(1)}, bf16[512,128]{1,0:T(8,128)(2,1)S(1)}, u32[]{:S(2)}, u32[]{:S(2)}) collective-permute-start(bf16[512,128]{1,0:T(8,128)(2,1)S(1)} %get-tuple-element.46), channel_id=1, source_target_pairs={{0,24},{8,0},{16,8},{24,16},{1,25},{9,1},{17,9},{25,17},{2,26},{10... | collective-permute-start | bytes 393224 | tf_op jit(solution)/shard_map/ppermute | solution.py:372
  76.5 11.9 %collective-permute-start.19 = (bf16[512,128]{1,0:T(8,128)(2,1)S(1)}, bf16[512,128]{1,0:T(8,128)(2,1)S(1)}, u32[]{:S(2)}, u32[]{:S(2)}) collective-permute-start(bf16[512,128]{1,0:T(8,128)(2,1)S(1)} %get-tuple-element.47), channel_id=1, source_target_pairs={{0,16},{8,24},{16,0},{24,8},{1,17},{9,25},{17,1},{25,9},{2,18},{10... | collective-permute-start | bytes 393224 | tf_op jit(solution)/shard_map/ppermute | solution.py:372
  84.8 6.2 %collective-permute-start.20 = (bf16[512,128]{1,0:T(8,128)(2,1)S(1)}, bf16[512,128]{1,0:T(8,128)(2,1)S(1)}, u32[]{:S(2)}, u32[]{:S(2)}) collective-permute-start(bf16[512,128]{1,0:T(8,128)(2,1)S(1)} %get-tuple-element.48), channel_id=1, source_target_pairs={{0,8},{8,16},{16,24},{24,0},{1,9},{9,17},{17,25},{25,1},{2,10},{10... | collective-permute-start | bytes 393224 | tf_op jit(solution)/shard_map/ppermute | solution.py:372

commit v4 on v3

--- a/solution.py
+++ b/solution.py
@@ -109,36 +109,26 @@
     lax.fori_loop(0, (8 - start) // step, some, 0)
 
 
-def stats_kernel(pieces, first, last, *refs):
-    refs = list(refs)
-    order_ref, near_ref, far_ref = refs[:3]
-    del refs[:3]
-    kv_refs = refs[: len(pieces)]
-    del refs[: len(pieces)]
-    before = [] if first else refs[:3]
-    del refs[: len(before)]
-    if last:
-        out_ref = refs.pop(0)
-        q_ref, kv_ref, top_ref, total_ref, weighted_ref = refs
-    else:
-        top_ref, total_ref, weighted_ref, q_ref, kv_ref = refs
-    q_ref[0:4] = near_ref[...].reshape(4, PIECE, DH)
-    q_ref[4:8] = far_ref[...].reshape(4, PIECE, DH)
-    for i, ref in enumerate(kv_refs):
-        kv_ref[i] = ref[...]
-    if first:
-        top_ref[...] = jnp.full(top_ref.shape, NEG, F32)
-        total_ref[...] = jnp.zeros(total_ref.shape, F32)
-        weighted_ref[...] = jnp.zeros(weighted_ref.shape, F32)
-    else:
-        for ref, source in zip((top_ref, total_ref, weighted_ref), before):
-            ref[...] = source[...]
+def stats_kernel(far, order_ref, q_ref, *refs):
+    kv_refs, refs = refs[:4], refs[4:]
+    if far:
+        before_ref, refs = refs[0], refs[1:]
+    out_ref, kv_ref, top_ref, total_ref, weighted_ref = refs
+    if far:
+        out_ref[...] = before_ref[...]
+    for b, ref in enumerate(kv_refs):
+        kv_ref[b] = ref[...]
+    top_ref[...] = jnp.full(top_ref.shape, NEG, F32)
+    total_ref[...] = jnp.zeros(total_ref.shape, F32)
+    weighted_ref[...] = jnp.zeros(weighted_ref.shape, F32)
+    base = 4 if far else 0
+    pieces = (0, 1, 2, 3)
 
     def begin(a, q_which, b, k_which, masked):
-        scores, dprobs = products(q_ref, kv_ref, a, q_which, pieces.index(b), k_which)
+        scores, dprobs = products(q_ref, kv_ref, a - base, q_which, b, k_which)
         if masked:
             scores = jnp.where(diagonal_visible(), scores, NEG)
-        return a * 2 + q_which, masked, scores.reshape(32, 8, SPAN), dprobs.reshape(32, 8, SPAN)
+        return (a - base) * 2 + q_which, masked, scores.reshape(32, 8, SPAN), dprobs.reshape(32, 8, SPAN)
 
     def finish(state):
         slot, masked, scores, dprobs = state
@@ -152,10 +142,20 @@
         total_ref[slot] = total_ref[slot] * shrink + jnp.sum(expon, axis=0)
         weighted_ref[slot] = weighted_ref[slot] * shrink + jnp.sum(expon * dprobs, axis=0)
 
-    run_tiles(order_ref, *in_flight(begin, finish, 2), pieces)
-    if not last:
-        return
-    for slot in range(16):
+    tile, drain = in_flight(begin, finish, 2)
+    step = 2 if far else 1
+    if not far:
+        one_query_piece(order_ref, tile, 0, pieces, True)
+        drain()
+
+    def some(i, carry):
+        for j in range(step):
+            one_query_piece(order_ref, tile, (4 if far else 1) + i * step + j, pieces, False)
+        drain()
+        return carry
+
+    lax.fori_loop(0, 2 if far else 3, some, 0)
+    for slot in range(8):
         tops = top_ref[slot]
         top = jnp.max(tops, axis=0, keepdims=True)
         factor = jnp.exp2(tops - top)
@@ -164,7 +164,7 @@
             jnp.sum(total_ref[slot] * factor, axis=0, keepdims=True),
             jnp.sum(weighted_ref[slot] * factor, axis=0, keepdims=True),
         )
-        place = query_place(slot // 2) + slot % 2
+        place = query_place(base + slot // 2) + slot % 2
         for kind, row in enumerate(rows):
             out_ref[kind, pl.ds(place, 1), :] = row
 
@@ -287,21 +287,17 @@
 PIECE = 4 * SPAN
 
 
-def call_stats(pieces, first, last, span_order, q_near, q_far, kvs, before):
-    shape = (3, 16, SPAN) if last else (16, 8, SPAN)
-    running = [pltpu.VMEM((16, 8, SPAN), F32)] * 3 if last else []
-    args = [span_order, q_near, q_far, *[kvs[b] for b in pieces], *before]
+def call_stats(far, span_order, q_pieces, kvs, *before):
+    args = [span_order, q_pieces.reshape(4, PIECE, DH), *kvs, *before]
     return pl.pallas_call(
-        functools.partial(stats_kernel, pieces, first, last),
-        out_shape=(jax.ShapeDtypeStruct(shape, F32),) * (1 if last else 3),
+        functools.partial(stats_kernel, far),
+        out_shape=jax.ShapeDtypeStruct((3, 16, SPAN), F32),
         in_specs=[SMEM] + [VMEM] * (len(args) - 1),
-        out_specs=(VMEM,) * (1 if last else 3),
-        scratch_shapes=[pltpu.VMEM((8, PIECE, DH), BF16), pltpu.VMEM((len(pieces), PIECE, DH), BF16)] + running,
+        out_specs=VMEM,
+        scratch_shapes=[pltpu.VMEM((4, PIECE, DH), BF16)] + [pltpu.VMEM((8, 8, SPAN), F32)] * 3,
         compiler_params=pltpu.CompilerParams(vmem_limit_bytes=32 * 2**20),
         cost_estimate=pl.CostEstimate(
-            flops=16 * len(pieces) * 2 * 2 * SPAN * SPAN * DH,
-            bytes_accessed=3 * 2**20,
-            transcendentals=16 * len(pieces) * SPAN * SPAN,
+            flops=32 * 2 * 2 * SPAN * SPAN * DH, bytes_accessed=2**21, transcendentals=32 * SPAN * SPAN
         ),
         name="stats",
     )(*args)
@@ -385,14 +381,16 @@
 def local(span_order, queries, key_rows, value_rows, out_grads):
     q_own, kv_own = call_pack(queries, key_rows, value_rows, out_grads)
     q_got = [back(q_own, "y", k) for k in (1, 2, 3)]
-    kv_got = [back(kv_own, "z", k) for k in (1, 2, 3)]
-    q_got, kv_got[0], kv_got[2] = lax.optimization_barrier((q_got, kv_got[0], kv_got[2]))
+    kv1, kv3 = back(kv_own, "z", 1), back(kv_own, "z", 3)
+    kv_again, kv1, kv3 = lax.optimization_barrier((kv_own, kv1, kv3))
+    kv2 = back(kv_again, "z", 2)
+    q_got, kv2 = lax.optimization_barrier((q_got, kv2))
     q_near = jnp.concatenate([q_own] + q_got, axis=0)
     q_far = swap_core(q_near)
-    kvs = [kv_own] + kv_got
-
-    running = call_stats((0, 1, 3), True, False, span_order, q_near, q_far, kvs, ())
-    (stats,) = call_stats((2,), False, True, span_order, q_near, q_far, kvs, running)
+    kvs = [kv_own, kv1, kv2, kv3]
+
+    stats = call_stats(False, span_order, q_near, kvs)
+    stats = call_stats(True, span_order, q_far, kvs, stats)
     stats = merged(stats, swap_core(stats))
     stats = [stats] + [back(stats, "y", k) for k in (1, 2, 3)]
 

time: 92.8 us -> 92.4 us (level)
  starting transfers between devices: 27.1 us -> 22.5 us
  waiting for transfers between devices: 36.5 us -> 40.9 us
    ppermute x12, waiting for transfers between devices: 25 us -> 28.9 us  [back(): return lax.ppermute(value, axis, [(i, (i + k) % 4) for i in range(4)])]
    ppermute x6, starting transfers between devices: 7.24 us -> 3.87 us  [ahead(): return lax.ppermute(value, axis, [(i, (i - k) % 4) for i in range(4)])]
    ppermute x12, starting transfers between devices: 19.6 us -> 17.9 us  [back(): return lax.ppermute(value, axis, [(i, (i + k) % 4) for i in range(4)])]
  transfers between devices with their start and end apart: 21 -> 21, of which waited for: 13 -> 14; matrix products, arithmetic and copies ran while one was open for 1% -> 1% of each run, Pallas kernels for 12% -> 10%
where the time goes in v4:
time: 92.4 us; the launch traced here: 91.4 us
  waiting for transfers between devices  40.9 us (44%)
  Pallas kernels  26 us (28%)
  starting transfers between devices  22.5 us (24%)
  local copies, waits for them, and re-layouts  1.17 us (1%)
    ppermute x12, waiting for transfers between devices, back(): return lax.ppermute(value, axis, [(i, (i + k) % 4) for i in range(4)])  28.9 us
    ppermute x12, starting transfers between devices, back(): return lax.ppermute(value, axis, [(i, (i + k) % 4) for i in range(4)])  17.9 us
    pallas_call x2, Pallas kernels, call_grads(): pl.pallas_call(functools.partial(grads_kernel, pieces, first, last), out_...  14.3 us
    ppermute x6, waiting for transfers between devices, ahead(): return lax.ppermute(value, axis, [(i, (i - k) % 4) for i in range(4)])  11.1 us
    pallas_call x2, Pallas kernels, call_stats(): pl.pallas_call(functools.partial(stats_kernel, far), out_shape=jax.ShapeD...  8.68 us
    ppermute x6, starting transfers between devices, ahead(): return lax.ppermute(value, axis, [(i, (i - k) % 4) for i in range(4)])  3.87 us
    pallas_call x1, Pallas kernels, call_pack(): pl.pallas_call(pack_kernel, out_shape=(jax.ShapeDtypeStruct((PIECE, DH),...  1.94 us
  transfers between devices with their start and end apart: 21, of which 14 were waited for; matrix products, arithmetic and copies ran while one was open for 1% of the time, Pallas kernels for 10%

profile of v4, /device:TPU:0, one launch (start us, length us, event | category | flops | bytes accessed | tf_op | source)
XLA Modules:
  0.0 91.4 jit_solution(9228759453524062991)
XLA Ops:
  0.6 1.9 %pack.1 = (bf16[1024,128]{1,0:T(8,128)(2,1)}, bf16[1024,128]{1,0:T(8,128)(2,1)}) custom-call(bf16[512,128]{1,0:T(8,128)(2,1)} %queries_ref.1, bf16[512,128]{1,0:T(8,128)(2,1)} %keys_ref.1, bf16[512,128]{1,0:T(8,128)(2,1)} %values_ref.1, bf16[512,128]{1,0:T(8,128)(2,1)} %grads_ref.1), custom_call_target="tpu_custom_call" | custom-call | tf_op jit(solution)/shard_map/pack/pallas_call | solution.py:352
  2.6 4.2 %collective-permute-start.4 = (bf16[1024,128]{1,0:T(8,128)(2,1)}, bf16[1024,128]{1,0:T(8,128)(2,1)S(1)}, u32[]{:S(2)}, u32[]{:S(2)}) collective-permute-start(bf16[1024,128]{1,0:T(8,128)(2,1)} %get-tuple-element.27.refs_0_.refs_7_), channel_id=1, source_target_pairs={{0,96},{32,0},{64,32},{96,64},{1,97},{33,1},{65,33},{97,65},{2,98}... | collective-permute-start | bytes 786440 | tf_op jit(solution)/shard_map/ppermute | solution.py:364
  6.8 3.0 %collective-permute-start.2 = (bf16[1024,128]{1,0:T(8,128)(2,1)}, bf16[1024,128]{1,0:T(8,128)(2,1)S(1)}, u32[]{:S(2)}, u32[]{:S(2)}) collective-permute-start(bf16[1024,128]{1,0:T(8,128)(2,1)} %get-tuple-element.25), channel_id=1, source_target_pairs={{0,24},{8,0},{16,8},{24,16},{1,25},{9,1},{17,9},{25,17},{2,26},{10... | collective-permute-start | bytes 786440 | tf_op jit(solution)/shard_map/ppermute | solution.py:364
  10.4 1.0 %collective-permute-start = (bf16[1024,128]{1,0:T(8,128)(2,1)}, bf16[1024,128]{1,0:T(8,128)(2,1)S(1)}, u32[]{:S(2)}, u32[]{:S(2)}) collective-permute-start(bf16[1024,128]{1,0:T(8,128)(2,1)} %get-tuple-element.25), channel_id=1, source_target_pairs={{0,8},{8,16},{16,24},{24,0},{1,9},{9,17},{17,25},{25,1},{2,10},{10... | collective-permute-start | bytes 786440 | tf_op jit(solution)/shard_map/ppermute | solution.py:364
  11.4 1.3 %collective-permute-done.4.refs_3_.refs_9_ = bf16[1024,128]{1,0:T(8,128)(2,1)S(1)} collective-permute-done((bf16[1024,128]{1,0:T(8,128)(2,1)}, bf16[1024,128]{1,0:T(8,128)(2,1)S(1)}, u32[]{:S(2)}, u32[]{:S(2)}) %collective-permute-start.4) | collective-permute-done | bytes 262176 | tf_op jit(solution)/shard_map/ppermute | solution.py:364
  12.7 3.3 %collective-permute-done.3.refs_1_.refs_7_ = bf16[1024,128]{1,0:T(8,128)(2,1)S(1)} collective-permute-done((bf16[1024,128]{1,0:T(8,128)(2,1)}, bf16[1024,128]{1,0:T(8,128)(2,1)S(1)}, u32[]{:S(2)}, u32[]{:S(2)}) %collective-permute-start.3) | collective-permute-done | bytes 262176 | tf_op jit(solution)/shard_map/ppermute | solution.py:364
  16.0 1.0 %constant_dynamic-update-slice_fusion.3 = bf16[4096,128]{1,0:T(8,128)(2,1)S(1)} fusion(bf16[1024,128]{1,0:T(8,128)(2,1)} %get-tuple-element.25), kind=kLoop, calls=%fused_computation.13 | loop fusion | bytes 524288
  17.0 4.1 %collective-permute-done.2 = bf16[1024,128]{1,0:T(8,128)(2,1)S(1)} collective-permute-done((bf16[1024,128]{1,0:T(8,128)(2,1)}, bf16[1024,128]{1,0:T(8,128)(2,1)S(1)}, u32[]{:S(2)}, u32[]{:S(2)}) %collective-permute-start.2) | collective-permute-done | bytes 262176 | tf_op jit(solution)/shard_map/ppermute | solution.py:364
  21.0 3.6 %collective-permute-done = bf16[1024,128]{1,0:T(8,128)(2,1)S(1)} collective-permute-done((bf16[1024,128]{1,0:T(8,128)(2,1)}, bf16[1024,128]{1,0:T(8,128)(2,1)S(1)}, u32[]{:S(2)}, u32[]{:S(2)}) %collective-permute-start) | collective-permute-done | bytes 262176 | tf_op jit(solution)/shard_map/ppermute | solution.py:364
  25.0 4.5 %stats.2.refs_4_ = f32[3,16,256]{2,1,0:T(8,128)S(1)} custom-call(s32[32,2]{1,0:T(8,128)S(1)} %copy.11.order_ref.refs_0_, bf16[4,1024,128]{2,1,0:T(8,128)(2,1)S(1)} %bitcast.2, bf16[1024,128]{1,0:T(8,128)(2,1)S(1)} %copy-done, bf16[1024,128]{1,0:T(8,128)(2,1)S(1)} %collective-permute-done.3.refs_1_.refs_7_, ...), custom_call_target="tpu_custom_call" | custom-call | flops 1073741824 | bytes 2097152 | tf_op jit(solution)/shard_map/stats/pallas_call | solution.py:292
  29.5 4.1 %stats.3 = f32[3,16,256]{2,1,0:T(8,128)S(1)} custom-call(s32[32,2]{1,0:T(8,128)S(1)} %copy.11.order_ref.refs_0_, bf16[4,1024,128]{2,1,0:T(8,128)(2,1)S(1)} %bitcast.3, bf16[1024,128]{1,0:T(8,128)(2,1)S(1)} %copy-done, bf16[1024,128]{1,0:T(8,128)(2,1)S(1)} %collective-permute-done.3.refs_1_.refs_7_, ...), custom_call_target="tpu_custom_call" | custom-call | flops 1073741824 | bytes 2097152 | tf_op jit(solution)/shard_map/stats/pallas_call | solution.py:292
  35.1 3.0 %collective-permute-start.10 = (f32[3,16,256]{2,1,0:T(8,128)S(1)}, f32[3,16,256]{2,1,0:T(8,128)S(1)}, u32[]{:S(2)}, u32[]{:S(2)}) collective-permute-start(f32[3,16,256]{2,1,0:T(8,128)S(1)} %pad_maximum_fusion.refs_1_), channel_id=1, source_target_pairs={{0,24},{8,0},{16,8},{24,16},{1,25},{9,1},{17,9},{25,17},{2,26},{10... | collective-permute-start | bytes 147464 | tf_op jit(solution)/shard_map/ppermute | solution.py:364
  38.8 1.0 %collective-permute-start.8 = (f32[3,16,256]{2,1,0:T(8,128)S(1)}, f32[3,16,256]{2,1,0:T(8,128)S(1)}, u32[]{:S(2)}, u32[]{:S(2)}) collective-permute-start(f32[3,16,256]{2,1,0:T(8,128)S(1)} %pad_maximum_fusion.refs_1_), channel_id=1, source_target_pairs={{0,8},{8,16},{16,24},{24,0},{1,9},{9,17},{17,25},{25,1},{2,10},{10... | collective-permute-start | bytes 147464 | tf_op jit(solution)/shard_map/ppermute | solution.py:364
  40.3 3.6 %collective-permute-done.9.refs_3_ = f32[3,16,256]{2,1,0:T(8,128)S(1)} collective-permute-done((f32[3,16,256]{2,1,0:T(8,128)S(1)}, f32[3,16,256]{2,1,0:T(8,128)S(1)}, u32[]{:S(2)}, u32[]{:S(2)}) %collective-permute-start.9) | collective-permute-done | bytes 49184 | tf_op jit(solution)/shard_map/ppermute | solution.py:364
  44.4 9.5 %grads.2 = (bf16[1024,128]{1,0:T(8,128)(2,1)S(1)}, bf16[1024,128]{1,0:T(8,128)(2,1)S(1)}, bf16[1024,128]{1,0:T(8,128)(2,1)S(1)}, f32[16,128,256]{2,1,0:T(8,128)S(1)}) custom-call(s32[32,2]{1,0:T(8,128)S(1)} %copy.11.order_ref.refs_0_, f32[3,16,256]{2,1,0:T(8,128)S(1)} %pad_maximum_fusion.refs_1_, f32[3,16,256]{2,1,0:T(8,128)S(1)} %collective-permute-done.8.refs_2_, ...), custom_call_target="tpu_custom_call" | custom-call | flops 4026531840 | bytes 4194304 | tf_op jit(solution)/shard_map/grads/pallas_call | solution.py:314
  56.1 4.8 %grads.3 = (f32[1024,128]{1,0:T(8,128)S(1)}, f32[2048,128]{1,0:T(8,128)S(1)}, bf16[2048,128]{1,0:T(8,128)(2,1)S(1)}) custom-call(s32[32,2]{1,0:T(8,128)S(1)} %copy.11.order_ref.refs_0_, f32[3,16,256]{2,1,0:T(8,128)S(1)} %pad_maximum_fusion.refs_1_, f32[3,16,256]{2,1,0:T(8,128)S(1)} %collective-permute-done.8.refs_2_, ...), custom_call_target="tpu_custom_call" | custom-call | flops 1342177280 | bytes 4194304 | tf_op jit(solution)/shard_map/grads/pallas_call | solution.py:314
  60.9 2.4 %collective-permute-done.11.z1_ref = bf16[1024,128]{1,0:T(8,128)(2,1)S(1)} collective-permute-done((bf16[1024,128]{1,0:T(8,128)(2,1)S(1)}, bf16[1024,128]{1,0:T(8,128)(2,1)S(1)}, u32[]{:S(2)}, u32[]{:S(2)}) %collective-permute-start.11) | collective-permute-done | bytes 262176 | tf_op jit(solution)/shard_map/ppermute | solution.py:368
  63.3 2.2 %collective-permute-done.12.z2_ref = bf16[1024,128]{1,0:T(8,128)(2,1)S(1)} collective-permute-done((bf16[1024,128]{1,0:T(8,128)(2,1)S(1)}, bf16[1024,128]{1,0:T(8,128)(2,1)S(1)}, u32[]{:S(2)}, u32[]{:S(2)}) %collective-permute-start.12) | collective-permute-done | bytes 262176 | tf_op jit(solution)/shard_map/ppermute | solution.py:368
  65.5 4.0 %collective-permute-done.13.z3_ref = bf16[1024,128]{1,0:T(8,128)(2,1)S(1)} collective-permute-done((bf16[1024,128]{1,0:T(8,128)(2,1)S(1)}, bf16[1024,128]{1,0:T(8,128)(2,1)S(1)}, u32[]{:S(2)}, u32[]{:S(2)}) %collective-permute-start.13) | collective-permute-done | bytes 262176 | tf_op jit(solution)/shard_map/ppermute | solution.py:368
  69.7 2.8 %collective-permute-start.16 = (bf16[1024,128]{1,0:T(8,128)(2,1)S(1)}, bf16[1024,128]{1,0:T(8,128)(2,1)S(1)}, u32[]{:S(2)}, u32[]{:S(2)}) collective-permute-start(bf16[1024,128]{1,0:T(8,128)(2,1)S(1)} %middle.1.sum_ref), channel_id=1, source_target_pairs={{0,3},{1,0},{2,1},{3,2},{4,7},{5,4},{6,5},{7,6},{8,11},{9,8},{10,9... | collective-permute-start | bytes 786440 | tf_op jit(solution)/shard_map/ppermute | solution.py:364
  74.3 0.9 collective-permute-start.18
  76.1 8.3 %collective-permute-done.16.x3_ref = bf16[1024,128]{1,0:T(8,128)(2,1)S(1)} collective-permute-done((bf16[1024,128]{1,0:T(8,128)(2,1)S(1)}, bf16[1024,128]{1,0:T(8,128)(2,1)S(1)}, u32[]{:S(2)}, u32[]{:S(2)}) %collective-permute-start.16) | collective-permute-done | bytes 262176 | tf_op jit(solution)/shard_map/ppermute | solution.py:364
  84.3 3.7 %collective-permute-done.14.x1_ref = bf16[1024,128]{1,0:T(8,128)(2,1)S(1)} collective-permute-done((bf16[1024,128]{1,0:T(8,128)(2,1)S(1)}, bf16[1024,128]{1,0:T(8,128)(2,1)S(1)}, u32[]{:S(2)}, u32[]{:S(2)}) %collective-permute-start.14) | collective-permute-done | bytes 262176 | tf_op jit(solution)/shard_map/ppermute | solution.py:364
  88.0 2.5 %collective-permute-done.20.y3_ref = bf16[512,128]{1,0:T(8,128)(2,1)S(1)} collective-permute-done((bf16[512,128]{1,0:T(8,128)(2,1)S(1)}, bf16[512,128]{1,0:T(8,128)(2,1)S(1)}, u32[]{:S(2)}, u32[]{:S(2)}) %collective-permute-start.20) | collective-permute-done | bytes 131104 | tf_op jit(solution)/shard_map/ppermute | solution.py:368
  (38 shorter events, 9.9 us)
Async XLA Ops:
  0.6 24.2 %copy-start.1 = (s32[32,2]{0,1:T(2,128)S(1)}, s32[32,2]{0,1:T(2,128)}, u32[]{:S(2)}) copy-start(s32[32,2]{0,1:T(2,128)} %param.5) | copy-start | bytes 772
  2.6 22.4 %copy-start = (bf16[1024,128]{1,0:T(8,128)(2,1)S(1)}, bf16[1024,128]{1,0:T(8,128)(2,1)}, u32[]{:S(2)}) copy-start(bf16[1024,128]{1,0:T(8,128)(2,1)} %get-tuple-element.27.refs_0_.refs_7_) | copy-start | bytes 786436
  2.6 10.1 %collective-permute-start.4 = (bf16[1024,128]{1,0:T(8,128)(2,1)}, bf16[1024,128]{1,0:T(8,128)(2,1)S(1)}, u32[]{:S(2)}, u32[]{:S(2)}) collective-permute-start(bf16[1024,128]{1,0:T(8,128)(2,1)} %get-tuple-element.27.refs_0_.refs_7_), channel_id=1, source_target_pairs={{0,96},{32,0},{64,32},{96,64},{1,97},{33,1},{65,33},{97,65},{2,98}... | collective-permute-start | bytes 786440 | tf_op jit(solution)/shard_map/ppermute | solution.py:364
  6.8 9.2 %collective-permute-start.3 = (bf16[1024,128]{1,0:T(8,128)(2,1)}, bf16[1024,128]{1,0:T(8,128)(2,1)S(1)}, u32[]{:S(2)}, u32[]{:S(2)}) collective-permute-start(bf16[1024,128]{1,0:T(8,128)(2,1)} %get-tuple-element.27.refs_0_.refs_7_), channel_id=1, source_target_pairs={{0,32},{32,64},{64,96},{96,0},{1,33},{33,65},{65,97},{97,1},{2,34}... | collective-permute-start | bytes 786440 | tf_op jit(solution)/shard_map/ppermute | solution.py:364
  6.8 14.2 %collective-permute-start.2 = (bf16[1024,128]{1,0:T(8,128)(2,1)}, bf16[1024,128]{1,0:T(8,128)(2,1)S(1)}, u32[]{:S(2)}, u32[]{:S(2)}) collective-permute-start(bf16[1024,128]{1,0:T(8,128)(2,1)} %get-tuple-element.25), channel_id=1, source_target_pairs={{0,24},{8,0},{16,8},{24,16},{1,25},{9,1},{17,9},{25,17},{2,26},{10... | collective-permute-start | bytes 786440 | tf_op jit(solution)/shard_map/ppermute | solution.py:364
  9.8 11.2 %collective-permute-start.1 = (bf16[1024,128]{1,0:T(8,128)(2,1)}, bf16[1024,128]{1,0:T(8,128)(2,1)S(1)}, u32[]{:S(2)}, u32[]{:S(2)}) collective-permute-start(bf16[1024,128]{1,0:T(8,128)(2,1)} %get-tuple-element.25), channel_id=1, source_target_pairs={{0,16},{8,24},{16,0},{24,8},{1,17},{9,25},{17,1},{25,9},{2,18},{10... | collective-permute-start | bytes 786440 | tf_op jit(solution)/shard_map/ppermute | solution.py:364
  10.4 14.2 %collective-permute-start = (bf16[1024,128]{1,0:T(8,128)(2,1)}, bf16[1024,128]{1,0:T(8,128)(2,1)S(1)}, u32[]{:S(2)}, u32[]{:S(2)}) collective-permute-start(bf16[1024,128]{1,0:T(8,128)(2,1)} %get-tuple-element.25), channel_id=1, source_target_pairs={{0,8},{8,16},{16,24},{24,0},{1,9},{9,17},{17,25},{25,1},{2,10},{10... | collective-permute-start | bytes 786440 | tf_op jit(solution)/shard_map/ppermute | solution.py:364
  16.0 8.7 %collective-permute-start.5 = (bf16[1024,128]{1,0:T(8,128)(2,1)}, bf16[1024,128]{1,0:T(8,128)(2,1)S(1)}, u32[]{:S(2)}, u32[]{:S(2)}) collective-permute-start(bf16[1024,128]{1,0:T(8,128)(2,1)} %get-tuple-element.27.refs_0_.refs_7_), channel_id=1, source_target_pairs={{0,64},{32,96},{64,0},{96,32},{1,65},{33,97},{65,1},{97,33},{2,66}... | collective-permute-start | bytes 786440 | tf_op jit(solution)/shard_map/ppermute | solution.py:364
  24.8 4.7 %collective-permute-start.6 = (bf16[4096,128]{1,0:T(8,128)(2,1)S(1)}, bf16[4096,128]{1,0:T(8,128)(2,1)S(1)}, u32[]{:S(2)}, u32[]{:S(2)}) collective-permute-start(bf16[4096,128]{1,0:T(8,128)(2,1)S(1)} %constant_dynamic-update-slice_fusion.refs_5_), channel_id=1, source_target_pairs={{0,4},{4,0},{1,5},{5,1},{2,6},{6,2},{3,7},{7,3},{8,12},{12,8},{9,1... | collective-permute-start | bytes 3145736 | tf_op jit(solution)/shard_map/ppermute | solution.py:372
  33.7 1.4 %collective-permute-start.7 = (f32[3,16,256]{2,1,0:T(8,128)S(1)}, f32[3,16,256]{2,1,0:T(8,128)S(1)}, u32[]{:S(2)}, u32[]{:S(2)}) collective-permute-start(f32[3,16,256]{2,1,0:T(8,128)S(1)} %stats.3), channel_id=1, source_target_pairs={{0,4},{4,0},{1,5},{5,1},{2,6},{6,2},{3,7},{7,3},{8,12},{12,8},{9,1... | collective-permute-start | bytes 147464 | tf_op jit(solution)/shard_map/ppermute | solution.py:372
  35.1 5.2 %collective-permute-start.10 = (f32[3,16,256]{2,1,0:T(8,128)S(1)}, f32[3,16,256]{2,1,0:T(8,128)S(1)}, u32[]{:S(2)}, u32[]{:S(2)}) collective-permute-start(f32[3,16,256]{2,1,0:T(8,128)S(1)} %pad_maximum_fusion.refs_1_), channel_id=1, source_target_pairs={{0,24},{8,0},{16,8},{24,16},{1,25},{9,1},{17,9},{25,17},{2,26},{10... | collective-permute-start | bytes 147464 | tf_op jit(solution)/shard_map/ppermute | solution.py:364
  38.2 5.8 %collective-permute-start.9 = (f32[3,16,256]{2,1,0:T(8,128)S(1)}, f32[3,16,256]{2,1,0:T(8,128)S(1)}, u32[]{:S(2)}, u32[]{:S(2)}) collective-permute-start(f32[3,16,256]{2,1,0:T(8,128)S(1)} %pad_maximum_fusion.refs_1_), channel_id=1, source_target_pairs={{0,16},{8,24},{16,0},{24,8},{1,17},{9,25},{17,1},{25,9},{2,18},{10... | collective-permute-start | bytes 147464 | tf_op jit(solution)/shard_map/ppermute | solution.py:364
  38.8 5.7 %collective-permute-start.8 = (f32[3,16,256]{2,1,0:T(8,128)S(1)}, f32[3,16,256]{2,1,0:T(8,128)S(1)}, u32[]{:S(2)}, u32[]{:S(2)}) collective-permute-start(f32[3,16,256]{2,1,0:T(8,128)S(1)} %pad_maximum_fusion.refs_1_), channel_id=1, source_target_pairs={{0,8},{8,16},{16,24},{24,0},{1,9},{9,17},{17,25},{25,1},{2,10},{10... | collective-permute-start | bytes 147464 | tf_op jit(solution)/shard_map/ppermute | solution.py:364
  54.0 9.3 %collective-permute-start.11 = (bf16[1024,128]{1,0:T(8,128)(2,1)S(1)}, bf16[1024,128]{1,0:T(8,128)(2,1)S(1)}, u32[]{:S(2)}, u32[]{:S(2)}) collective-permute-start(bf16[1024,128]{1,0:T(8,128)(2,1)S(1)} %get-tuple-element.37), channel_id=1, source_target_pairs={{0,96},{32,0},{64,32},{96,64},{1,97},{33,1},{65,33},{97,65},{2,98}... | collective-permute-start | bytes 786440 | tf_op jit(solution)/shard_map/ppermute | solution.py:368
  54.7 10.8 %collective-permute-start.12 = (bf16[1024,128]{1,0:T(8,128)(2,1)S(1)}, bf16[1024,128]{1,0:T(8,128)(2,1)S(1)}, u32[]{:S(2)}, u32[]{:S(2)}) collective-permute-start(bf16[1024,128]{1,0:T(8,128)(2,1)S(1)} %get-tuple-element.38), channel_id=1, source_target_pairs={{0,64},{32,96},{64,0},{96,32},{1,65},{33,97},{65,1},{97,33},{2,66}... | collective-permute-start | bytes 786440 | tf_op jit(solution)/shard_map/ppermute | solution.py:368
  55.5 13.9 %collective-permute-start.13 = (bf16[1024,128]{1,0:T(8,128)(2,1)S(1)}, bf16[1024,128]{1,0:T(8,128)(2,1)S(1)}, u32[]{:S(2)}, u32[]{:S(2)}) collective-permute-start(bf16[1024,128]{1,0:T(8,128)(2,1)S(1)} %get-tuple-element.39), channel_id=1, source_target_pairs={{0,32},{32,64},{64,96},{96,0},{1,33},{33,65},{65,97},{97,1},{2,34}... | collective-permute-start | bytes 786440 | tf_op jit(solution)/shard_map/ppermute | solution.py:368
  69.6 4.6 %collective-permute-start.17 = (bf16[2048,128]{1,0:T(8,128)(2,1)S(1)}, bf16[2048,128]{1,0:T(8,128)(2,1)S(1)}, u32[]{:S(2)}, u32[]{:S(2)}) collective-permute-start(bf16[2048,128]{1,0:T(8,128)(2,1)S(1)} %get-tuple-element.42), channel_id=1, source_target_pairs={{0,4},{4,0},{1,5},{5,1},{2,6},{6,2},{3,7},{7,3},{8,12},{12,8},{9,1... | collective-permute-start | bytes 1572872 | tf_op jit(solution)/shard_map/ppermute | solution.py:372
  69.7 14.6 %collective-permute-start.16 = (bf16[1024,128]{1,0:T(8,128)(2,1)S(1)}, bf16[1024,128]{1,0:T(8,128)(2,1)S(1)}, u32[]{:S(2)}, u32[]{:S(2)}) collective-permute-start(bf16[1024,128]{1,0:T(8,128)(2,1)S(1)} %middle.1.sum_ref), channel_id=1, source_target_pairs={{0,3},{1,0},{2,1},{3,2},{4,7},{5,4},{6,5},{7,6},{8,11},{9,8},{10,9... | collective-permute-start | bytes 786440 | tf_op jit(solution)/shard_map/ppermute | solution.py:364
  72.5 11.8 %collective-permute-start.15 = (bf16[1024,128]{1,0:T(8,128)(2,1)S(1)}, bf16[1024,128]{1,0:T(8,128)(2,1)S(1)}, u32[]{:S(2)}, u32[]{:S(2)}) collective-permute-start(bf16[1024,128]{1,0:T(8,128)(2,1)S(1)} %middle.1.sum_ref), channel_id=1, source_target_pairs={{0,2},{1,3},{2,0},{3,1},{4,6},{5,7},{6,4},{7,5},{8,10},{9,11},{10,... | collective-permute-start | bytes 786440 | tf_op jit(solution)/shard_map/ppermute | solution.py:364
  73.3 14.7 %collective-permute-start.14 = (bf16[1024,128]{1,0:T(8,128)(2,1)S(1)}, bf16[1024,128]{1,0:T(8,128)(2,1)S(1)}, u32[]{:S(2)}, u32[]{:S(2)}) collective-permute-start(bf16[1024,128]{1,0:T(8,128)(2,1)S(1)} %middle.1.sum_ref), channel_id=1, source_target_pairs={{0,1},{1,2},{2,3},{3,0},{4,5},{5,6},{6,7},{7,4},{8,9},{9,10},{10,1... | collective-permute-start | bytes 786440 | tf_op jit(solution)/shard_map/ppermute | solution.py:364
  74.3 13.7 %collective-permute-start.18 = (bf16[512,128]{1,0:T(8,128)(2,1)S(1)}, bf16[512,128]{1,0:T(8,128)(2,1)S(1)}, u32[]{:S(2)}, u32[]{:S(2)}) collective-permute-start(bf16[512,128]{1,0:T(8,128)(2,1)S(1)} %get-tuple-element.44), channel_id=1, source_target_pairs={{0,24},{8,0},{16,8},{24,16},{1,25},{9,1},{17,9},{25,17},{2,26},{10... | collective-permute-start | bytes 393224 | tf_op jit(solution)/shard_map/ppermute | solution.py:368
  75.2 12.8 %collective-permute-start.19 = (bf16[512,128]{1,0:T(8,128)(2,1)S(1)}, bf16[512,128]{1,0:T(8,128)(2,1)S(1)}, u32[]{:S(2)}, u32[]{:S(2)}) collective-permute-start(bf16[512,128]{1,0:T(8,128)(2,1)S(1)} %get-tuple-element.45), channel_id=1, source_target_pairs={{0,16},{8,24},{16,0},{24,8},{1,17},{9,25},{17,1},{25,9},{2,18},{10... | collective-permute-start | bytes 393224 | tf_op jit(solution)/shard_map/ppermute | solution.py:368
  84.3 6.2 %collective-permute-start.20 = (bf16[512,128]{1,0:T(8,128)(2,1)S(1)}, bf16[512,128]{1,0:T(8,128)(2,1)S(1)}, u32[]{:S(2)}, u32[]{:S(2)}) collective-permute-start(bf16[512,128]{1,0:T(8,128)(2,1)S(1)} %get-tuple-element.46), channel_id=1, source_target_pairs={{0,8},{8,16},{16,24},{24,0},{1,9},{9,17},{17,25},{25,1},{2,10},{10... | collective-permute-start | bytes 393224 | tf_op jit(solution)/shard_map/ppermute | solution.py:368

commit v5 on v4

--- a/solution.py
+++ b/solution.py
@@ -90,23 +90,6 @@
             finish(waiting.pop(0))
 
     return tile, drain
-
-
-def run_tiles(order_ref, tile, drain, pieces):
-    start, step = 0, max(2, 4 // len(pieces))
-    if 0 in pieces:
-        one_query_piece(order_ref, tile, 0, pieces, True)
-        one_query_piece(order_ref, tile, 1, pieces, False)
-        start, step = 2, 3 if len(pieces) == 1 else 2
-        drain()
-
-    def some(i, carry):
-        for j in range(step):
-            one_query_piece(order_ref, tile, start + i * step + j, pieces, False)
-        drain()
-        return carry
-
-    lax.fori_loop(0, (8 - start) // step, some, 0)
 
 
 def stats_kernel(far, order_ref, q_ref, *refs):
@@ -143,18 +126,9 @@
         weighted_ref[slot] = weighted_ref[slot] * shrink + jnp.sum(expon * dprobs, axis=0)
 
     tile, drain = in_flight(begin, finish, 2)
-    step = 2 if far else 1
-    if not far:
-        one_query_piece(order_ref, tile, 0, pieces, True)
-        drain()
-
-    def some(i, carry):
-        for j in range(step):
-            one_query_piece(order_ref, tile, (4 if far else 1) + i * step + j, pieces, False)
-        drain()
-        return carry
-
-    lax.fori_loop(0, 2 if far else 3, some, 0)
+    for a in range(base, base + 4):
+        one_query_piece(order_ref, tile, a, pieces, a == 0)
+    drain()
     for slot in range(8):
         tops = top_ref[slot]
         top = jnp.max(tops, axis=0, keepdims=True)
@@ -189,15 +163,12 @@
     kv_refs = refs[: len(pieces)]
     del refs[: len(pieces)]
     dqt_in = None if first else refs.pop(0)
-    dkv_refs = dict(zip(pieces, refs[: len(pieces)]))
-    del refs[: len(pieces)]
+    dkv_refs = [refs.pop(0) for _ in dkv_parts(pieces)]
     dq_outs = [refs.pop(0), refs.pop(0)] if last else [refs.pop(0)]
-    q_ref, kv_ref, sum_ref, norm_ref, delta_ref, dk_ref, dv_ref, kt_ref = refs[:8]
-    dqt_ref = refs[8] if last else dq_outs[0]
+    kv_ref, sum_ref, norm_ref, delta_ref, dk_ref, dv_ref, kt_ref = refs[:7]
+    dqt_ref = refs[7] if last else dq_outs[0]
 
     norm_and_delta(stat_refs, sum_ref, norm_ref, delta_ref)
-    q_ref[0:4] = near_ref[...].reshape(4, PIECE, DH)
-    q_ref[4:8] = far_ref[...].reshape(4, PIECE, DH)
     for i, b in enumerate(pieces):
         kv_ref[i] = kv_refs[i][...]
         for which in range(2):
@@ -211,8 +182,9 @@
 
     def begin(a, q_which, b, k_which, masked):
         slot = a * 2 + q_which
-        queries = half(q_ref, a, q_which, 0)
-        out_grads = half(q_ref, a, q_which, 1)
+        q_ref, base = source
+        queries = half(q_ref, a - base, q_which, 0)
+        out_grads = half(q_ref, a - base, q_which, 1)
         i = pieces.index(b)
         scores = lax.dot_general(
             half(kv_ref, i, k_which, 0), queries, NT, preferred_element_type=F32
@@ -234,16 +206,18 @@
         dk_ref[key_slot] += lax.dot_general(dscores, queries, NN, preferred_element_type=F32)
         dqt_ref[slot] += lax.dot_general(kt_ref[key_slot], dscores, NN, preferred_element_type=F32)
 
-    run_tiles(order_ref, *in_flight(begin, finish, 1), pieces)
-    for i, b in enumerate(pieces):
-        ref = dkv_refs[b]
-        for which in range(2):
-            ref[pl.ds(which * SPAN, SPAN), :] = dk_ref[2 * i + which].astype(ref.dtype)
-            ref[pl.ds((2 + which) * SPAN, SPAN), :] = dv_ref[2 * i + which].astype(ref.dtype)
+    tile, drain = in_flight(begin, finish, 1)
+    for source in ((near_ref, 0), (far_ref, 4)):
+        for a in range(source[1], source[1] + 4):
+            one_query_piece(order_ref, tile, a, pieces, a == 0 and 0 in pieces)
+    drain()
+    parts = [ref for i in range(len(pieces)) for ref in (dk_ref.at[2 * i], dk_ref.at[2 * i + 1], dv_ref.at[2 * i], dv_ref.at[2 * i + 1])]
+    for ref in dkv_refs:
+        for j in range(ref.shape[0] // SPAN):
+            ref[pl.ds(j * SPAN, SPAN), :] = parts.pop(0)[...].astype(ref.dtype)
     if last:
-        for out, begin in zip(dq_outs, (0, 8)):
-            for slot in range(8):
-                out[pl.ds(slot * SPAN, SPAN), :] = dqt_ref[begin + slot].T.astype(out.dtype)
+        for out, first_slot in zip(dq_outs, (0, 8)):
+            out[...] = dqt_ref[first_slot : first_slot + 8].astype(out.dtype)
 
 
 def pack_kernel(queries_ref, keys_ref, values_ref, grads_ref, q_ref, kv_ref, sems):
@@ -260,15 +234,23 @@
         copy.wait()
 
 
-def middle_kernel(dkv_ref, z1_ref, z2_ref, z3_ref, sum_ref):
-    total = dkv_ref[...] + z1_ref[...].astype(F32) + z2_ref[...].astype(F32) + z3_ref[...].astype(F32)
+def relay_kernel(dkv1_ref, dkv3_ref, keys_ref, values_ref, out1_ref, out3_ref):
+    keys, values = pl.ds(0, 2 * SPAN), pl.ds(2 * SPAN, 2 * SPAN)
+    out1_ref[keys, :] = (dkv1_ref[keys, :] + keys_ref[...].astype(F32)).astype(BF16)
+    out1_ref[values, :] = dkv1_ref[values, :].astype(BF16)
+    out3_ref[keys, :] = dkv3_ref[keys, :].astype(BF16)
+    out3_ref[values, :] = (dkv3_ref[values, :] + values_ref[...].astype(F32)).astype(BF16)
+
+
+def middle_kernel(dkv_ref, z1_ref, z3_ref, sum_ref):
+    total = dkv_ref[...] + z1_ref[...].astype(F32) + z3_ref[...].astype(F32)
     sum_ref[...] = total.astype(BF16)
 
 
 def query_kernel(keep_ref, other_ref, dq_ref, r1_ref, r2_ref, r3_ref):
     for k, ref in enumerate((dq_ref, r1_ref, r2_ref, r3_ref)):
-        rows = pl.ds(k * 2 * SPAN, 2 * SPAN)
-        ref[...] = (keep_ref[rows, :] + other_ref[rows, :].astype(F32)).astype(ref.dtype)
+        slots = pl.ds(2 * k, 2)
+        ref[...] = (keep_ref[slots] + other_ref[slots].astype(F32)).astype(ref.dtype)
 
 
 def last_kernel(sum_ref, x1_ref, x2_ref, x3_ref, dq_ref, y1_ref, y2_ref, y3_ref, q_out, k_out, v_out):
@@ -279,7 +261,8 @@
     dq = dq_ref[...]
     for ref in (y1_ref, y2_ref, y3_ref):
         dq = dq + ref[...].astype(F32)
-    q_out[...] = (dq * SCALE).astype(BF16)
+    for slot in range(2):
+        q_out[pl.ds(slot * SPAN, SPAN), :] = (dq[slot] * SCALE).T.astype(BF16)
 
 
 SMEM = pl.BlockSpec(memory_space=pltpu.SMEM)
@@ -303,21 +286,27 @@
     )(*args)
 
 
+def dkv_parts(pieces):
+    if pieces == (2,):
+        return (jax.ShapeDtypeStruct((PIECE // 2, DH), BF16),) * 2
+    return (jax.ShapeDtypeStruct((PIECE, DH), F32),) * len(pieces)
+
+
 def call_grads(pieces, first, last, span_order, stats, q_near, q_far, kvs, dqt):
     tiles = 16 * len(pieces)
-    dkv_shapes = tuple(jax.ShapeDtypeStruct((PIECE, DH), BF16 if b else F32) for b in pieces)
+    dkv_shapes = dkv_parts(pieces)
     if last:
-        dq_shapes = tuple(jax.ShapeDtypeStruct((8 * SPAN, DH), dtype) for dtype in (F32, BF16))
+        dq_shapes = tuple(jax.ShapeDtypeStruct((8, DH, SPAN), dtype) for dtype in (F32, BF16))
     else:
         dq_shapes = (jax.ShapeDtypeStruct((16, DH, SPAN), F32),)
-    args = [span_order, *stats, q_near, q_far, *[kvs[b] for b in pieces]] + ([] if first else [dqt])
+    q_pieces = [q.reshape(4, PIECE, DH) for q in (q_near, q_far)]
+    args = [span_order, *stats, *q_pieces, *[kvs[b] for b in pieces]] + ([] if first else [dqt])
     out = pl.pallas_call(
         functools.partial(grads_kernel, pieces, first, last),
         out_shape=dkv_shapes + dq_shapes,
         in_specs=[SMEM] + [VMEM] * (len(args) - 1),
-        out_specs=(VMEM,) * (len(pieces) + len(dq_shapes)),
+        out_specs=(VMEM,) * (len(dkv_shapes) + len(dq_shapes)),
         scratch_shapes=[
-            pltpu.VMEM((8, PIECE, DH), BF16),
             pltpu.VMEM((len(pieces), PIECE, DH), BF16),
             pltpu.VMEM((2, 16, SPAN), F32),
             pltpu.VMEM((16, 8, SPAN), F32),
@@ -333,7 +322,7 @@
         ),
         name="grads",
     )(*args)
-    return out[: len(pieces)], out[len(pieces) :]
+    return out[: len(dkv_shapes)], out[len(dkv_shapes) :]
 
 
 def plain_call(kernel, name, out_shapes, *args):
@@ -395,15 +384,18 @@
     stats = [stats] + [back(stats, "y", k) for k in (1, 2, 3)]
 
     common = (span_order, stats, q_near, q_far, kvs)
-    (dkv1, dkv2, dkv3), (dqt,) = call_grads((1, 2, 3), True, False, *common, None)
+    (dk2, dv2), (dqt,) = call_grads((2,), True, False, *common, None)
+    dk_relay, dv_relay = ahead(dk2, "z", 1), ahead(dv2, "z", 3)
+    (dkv1, dkv3), (dqt,) = call_grads((1, 3), False, False, *common, dqt)
+    dkv1, dkv3 = plain_call(relay_kernel, "relay", [((PIECE, DH), BF16)] * 2, dkv1, dkv3, dk_relay, dv_relay)
     (dkv0,), (dq_keep, dq_send) = call_grads((0,), False, True, *common, dqt)
-    z1, z2, z3 = ahead(dkv1, "z", 1), ahead(dkv2, "z", 2), ahead(dkv3, "z", 3)
-    (summed,) = plain_call(middle_kernel, "middle", [((PIECE, DH), BF16)], dkv0, z1, z2, z3)
+    z1, z3 = ahead(dkv1, "z", 1), ahead(dkv3, "z", 3)
+    (summed,) = plain_call(middle_kernel, "middle", [((PIECE, DH), BF16)], dkv0, z1, z3)
     dq_send, summed = lax.optimization_barrier((dq_send, summed))
     dq_other = swap_core(dq_send)
-    rows = (2 * SPAN, DH)
+    rows, slots = (2 * SPAN, DH), (2, DH, SPAN)
     dq, r1, r2, r3 = plain_call(
-        query_kernel, "query", [(rows, F32), (rows, BF16), (rows, BF16), (rows, BF16)], dq_keep, dq_other
+        query_kernel, "query", [(slots, F32), (slots, BF16), (slots, BF16), (slots, BF16)], dq_keep, dq_other
     )
     xs = [back(summed, "x", k) for k in (1, 2, 3)]
     ys = [ahead(part, "y", k) for k, part in ((1, r1), (2, r2), (3, r3))]

time: 92.4 us -> 88.7 us (0.960)
  waiting for transfers between devices: 40.9 us -> 35.7 us
  starting transfers between devices: 22.5 us -> 25 us
  Pallas kernels: 26 us -> 25 us
    ppermute x6 -> x7, waiting for transfers between devices: 11.1 us -> 6.34 us  [ahead(): return lax.ppermute(value, axis, [(i, (i - k) % 4) for i in range(4)])]
    ppermute x6 -> x7, starting transfers between devices: 3.87 us -> 6.32 us  [ahead(): return lax.ppermute(value, axis, [(i, (i - k) % 4) for i in range(4)])]
    pallas_call x2, Pallas kernels: 8.68 us -> 7.62 us  [call_stats(): pl.pallas_call(functools.partial(stats_kernel, far), out_shape=jax.ShapeD...]
    pallas_call x2 -> x3, Pallas kernels: 14.3 us -> 14.2 us  [call_grads(): pl.pallas_call(functools.partial(grads_kernel, pieces, first, last), out_...]
  transfers between devices with their start and end apart: 21 -> 22, of which waited for: 14 -> 13; matrix products, arithmetic and copies ran while one was open for 1% -> 1% of each run, Pallas kernels for 10% -> 16%
where the time goes in v5:
time: 88.7 us; the launch traced here: 87.7 us
  waiting for transfers between devices  35.7 us (40%)
  Pallas kernels  25 us (28%)
  starting transfers between devices  25 us (28%)
  local copies, waits for them, and re-layouts  1.17 us (1%)
    ppermute x12, waiting for transfers between devices, back(): return lax.ppermute(value, axis, [(i, (i + k) % 4) for i in range(4)])  28.5 us
    ppermute x12, starting transfers between devices, back(): return lax.ppermute(value, axis, [(i, (i + k) % 4) for i in range(4)])  17.9 us
    pallas_call x3, Pallas kernels, call_grads(): pl.pallas_call(functools.partial(grads_kernel, pieces, first, last), out_...  14.2 us
    pallas_call x2, Pallas kernels, call_stats(): pl.pallas_call(functools.partial(stats_kernel, far), out_shape=jax.ShapeD...  7.62 us
    ppermute x7, waiting for transfers between devices, ahead(): return lax.ppermute(value, axis, [(i, (i - k) % 4) for i in range(4)])  6.34 us
    ppermute x7, starting transfers between devices, ahead(): return lax.ppermute(value, axis, [(i, (i - k) % 4) for i in range(4)])  6.32 us
    pallas_call x1, Pallas kernels, call_pack(): pl.pallas_call(pack_kernel, out_shape=(jax.ShapeDtypeStruct((PIECE, DH),...  1.96 us
  transfers between devices with their start and end apart: 22, of which 13 were waited for; matrix products, arithmetic and copies ran while one was open for 1% of the time, Pallas kernels for 16%

profile of v5, /device:TPU:0, one launch (start us, length us, event | category | flops | bytes accessed | tf_op | source)
XLA Modules:
  0.0 87.7 jit_solution(10749374151034736630)
XLA Ops:
  0.6 2.0 %pack.1 = (bf16[1024,128]{1,0:T(8,128)(2,1)}, bf16[1024,128]{1,0:T(8,128)(2,1)}) custom-call(bf16[512,128]{1,0:T(8,128)(2,1)} %queries_ref.1, bf16[512,128]{1,0:T(8,128)(2,1)} %keys_ref.1, bf16[512,128]{1,0:T(8,128)(2,1)} %values_ref.1, bf16[512,128]{1,0:T(8,128)(2,1)} %grads_ref.1), custom_call_target="tpu_custom_call" | custom-call | tf_op jit(solution)/shard_map/pack/pallas_call | solution.py:341
  2.6 4.2 %collective-permute-start.4 = (bf16[1024,128]{1,0:T(8,128)(2,1)}, bf16[1024,128]{1,0:T(8,128)(2,1)S(1)}, u32[]{:S(2)}, u32[]{:S(2)}) collective-permute-start(bf16[1024,128]{1,0:T(8,128)(2,1)} %get-tuple-element.31.refs_0_.refs_7_), channel_id=1, source_target_pairs={{0,96},{32,0},{64,32},{96,64},{1,97},{33,1},{65,33},{97,65},{2,98}... | collective-permute-start | bytes 786440 | tf_op jit(solution)/shard_map/ppermute | solution.py:353
  6.8 3.0 %collective-permute-start.2 = (bf16[1024,128]{1,0:T(8,128)(2,1)}, bf16[1024,128]{1,0:T(8,128)(2,1)S(1)}, u32[]{:S(2)}, u32[]{:S(2)}) collective-permute-start(bf16[1024,128]{1,0:T(8,128)(2,1)} %get-tuple-element.29), channel_id=1, source_target_pairs={{0,24},{8,0},{16,8},{24,16},{1,25},{9,1},{17,9},{25,17},{2,26},{10... | collective-permute-start | bytes 786440 | tf_op jit(solution)/shard_map/ppermute | solution.py:353
  10.5 1.0 %collective-permute-start = (bf16[1024,128]{1,0:T(8,128)(2,1)}, bf16[1024,128]{1,0:T(8,128)(2,1)S(1)}, u32[]{:S(2)}, u32[]{:S(2)}) collective-permute-start(bf16[1024,128]{1,0:T(8,128)(2,1)} %get-tuple-element.29), channel_id=1, source_target_pairs={{0,8},{8,16},{16,24},{24,0},{1,9},{9,17},{17,25},{25,1},{2,10},{10... | collective-permute-start | bytes 786440 | tf_op jit(solution)/shard_map/ppermute | solution.py:353
  11.4 1.3 %collective-permute-done.4.refs_3_.refs_8_ = bf16[1024,128]{1,0:T(8,128)(2,1)S(1)} collective-permute-done((bf16[1024,128]{1,0:T(8,128)(2,1)}, bf16[1024,128]{1,0:T(8,128)(2,1)S(1)}, u32[]{:S(2)}, u32[]{:S(2)}) %collective-permute-start.4) | collective-permute-done | bytes 262176 | tf_op jit(solution)/shard_map/ppermute | solution.py:353
  12.7 3.3 %collective-permute-done.3.refs_1_.refs_7_ = bf16[1024,128]{1,0:T(8,128)(2,1)S(1)} collective-permute-done((bf16[1024,128]{1,0:T(8,128)(2,1)}, bf16[1024,128]{1,0:T(8,128)(2,1)S(1)}, u32[]{:S(2)}, u32[]{:S(2)}) %collective-permute-start.3) | collective-permute-done | bytes 262176 | tf_op jit(solution)/shard_map/ppermute | solution.py:353
  16.0 1.0 %constant_dynamic-update-slice_fusion.3 = bf16[4096,128]{1,0:T(8,128)(2,1)S(1)} fusion(bf16[1024,128]{1,0:T(8,128)(2,1)} %get-tuple-element.29), kind=kLoop, calls=%fused_computation.13 | loop fusion | bytes 524288
  17.0 4.1 %collective-permute-done.2 = bf16[1024,128]{1,0:T(8,128)(2,1)S(1)} collective-permute-done((bf16[1024,128]{1,0:T(8,128)(2,1)}, bf16[1024,128]{1,0:T(8,128)(2,1)S(1)}, u32[]{:S(2)}, u32[]{:S(2)}) %collective-permute-start.2) | collective-permute-done | bytes 262176 | tf_op jit(solution)/shard_map/ppermute | solution.py:353
  21.0 3.6 %collective-permute-done = bf16[1024,128]{1,0:T(8,128)(2,1)S(1)} collective-permute-done((bf16[1024,128]{1,0:T(8,128)(2,1)}, bf16[1024,128]{1,0:T(8,128)(2,1)S(1)}, u32[]{:S(2)}, u32[]{:S(2)}) %collective-permute-start) | collective-permute-done | bytes 262176 | tf_op jit(solution)/shard_map/ppermute | solution.py:353
  25.0 3.8 %stats.2.refs_4_ = f32[3,16,256]{2,1,0:T(8,128)S(1)} custom-call(s32[32,2]{1,0:T(8,128)S(1)} %copy.12.order_ref.refs_0_, bf16[4,1024,128]{2,1,0:T(8,128)(2,1)S(1)} %bitcast.2, bf16[1024,128]{1,0:T(8,128)(2,1)S(1)} %copy-done, bf16[1024,128]{1,0:T(8,128)(2,1)S(1)} %collective-permute-done.3.refs_1_.refs_7_, ...), custom_call_target="tpu_custom_call" | custom-call | flops 1073741824 | bytes 2097152 | tf_op jit(solution)/shard_map/stats/pallas_call | solution.py:275
  28.8 3.8 %stats.3 = f32[3,16,256]{2,1,0:T(8,128)S(1)} custom-call(s32[32,2]{1,0:T(8,128)S(1)} %copy.12.order_ref.refs_0_, bf16[4,1024,128]{2,1,0:T(8,128)(2,1)S(1)} %bitcast.6, bf16[1024,128]{1,0:T(8,128)(2,1)S(1)} %copy-done, bf16[1024,128]{1,0:T(8,128)(2,1)S(1)} %collective-permute-done.3.refs_1_.refs_7_, ...), custom_call_target="tpu_custom_call" | custom-call | flops 1073741824 | bytes 2097152 | tf_op jit(solution)/shard_map/stats/pallas_call | solution.py:275
  34.1 3.0 %collective-permute-start.10 = (f32[3,16,256]{2,1,0:T(8,128)S(1)}, f32[3,16,256]{2,1,0:T(8,128)S(1)}, u32[]{:S(2)}, u32[]{:S(2)}) collective-permute-start(f32[3,16,256]{2,1,0:T(8,128)S(1)} %pad_maximum_fusion.refs_1_), channel_id=1, source_target_pairs={{0,24},{8,0},{16,8},{24,16},{1,25},{9,1},{17,9},{25,17},{2,26},{10... | collective-permute-start | bytes 147464 | tf_op jit(solution)/shard_map/ppermute | solution.py:353
  39.3 3.6 %collective-permute-done.9.refs_3_ = f32[3,16,256]{2,1,0:T(8,128)S(1)} collective-permute-done((f32[3,16,256]{2,1,0:T(8,128)S(1)}, f32[3,16,256]{2,1,0:T(8,128)S(1)}, u32[]{:S(2)}, u32[]{:S(2)}) %collective-permute-start.9) | collective-permute-done | bytes 49184 | tf_op jit(solution)/shard_map/ppermute | solution.py:353
  43.4 3.7 %grads.3 = (bf16[512,128]{1,0:T(8,128)(2,1)S(1)}, bf16[512,128]{1,0:T(8,128)(2,1)S(1)}, f32[16,128,256]{2,1,0:T(8,128)S(1)}) custom-call(s32[32,2]{1,0:T(8,128)S(1)} %copy.12.order_ref.refs_0_, f32[3,16,256]{2,1,0:T(8,128)S(1)} %pad_maximum_fusion.refs_1_, f32[3,16,256]{2,1,0:T(8,128)S(1)} %collective-permute-done.8.refs_2_, ...), custom_call_target="tpu_custom_call" | custom-call | flops 1342177280 | bytes 4194304 | tf_op jit(solution)/shard_map/grads/pallas_call | solution.py:304
  47.9 1.4 %collective-permute-start.12 = (bf16[512,128]{1,0:T(8,128)(2,1)S(1)}, bf16[512,128]{1,0:T(8,128)(2,1)S(1)}, u32[]{:S(2)}, u32[]{:S(2)}) collective-permute-start(bf16[512,128]{1,0:T(8,128)(2,1)S(1)} %get-tuple-element.45), channel_id=1, source_target_pairs={{0,32},{32,64},{64,96},{96,0},{1,33},{33,65},{65,97},{97,1},{2,34}... | collective-permute-start | bytes 393224 | tf_op jit(solution)/shard_map/ppermute | solution.py:357
  49.2 6.2 %grads.4 = (f32[1024,128]{1,0:T(8,128)S(1)}, f32[1024,128]{1,0:T(8,128)S(1)}, f32[16,128,256]{2,1,0:T(8,128)S(1)}) custom-call(s32[32,2]{1,0:T(8,128)S(1)} %copy.12.order_ref.refs_0_, f32[3,16,256]{2,1,0:T(8,128)S(1)} %pad_maximum_fusion.refs_1_, f32[3,16,256]{2,1,0:T(8,128)S(1)} %collective-permute-done.8.refs_2_, ...), custom_call_target="tpu_custom_call" | custom-call | flops 2684354560 | bytes 4194304 | tf_op jit(solution)/shard_map/grads/pallas_call | solution.py:304
  55.5 1.9 %collective-permute-start.13 = (bf16[1024,128]{1,0:T(8,128)(2,1)S(1)}, bf16[1024,128]{1,0:T(8,128)(2,1)S(1)}, u32[]{:S(2)}, u32[]{:S(2)}) collective-permute-start(bf16[1024,128]{1,0:T(8,128)(2,1)S(1)} %get-tuple-element.46), channel_id=1, source_target_pairs={{0,96},{32,0},{64,32},{96,64},{1,97},{33,1},{65,33},{97,65},{2,98}... | collective-permute-start | bytes 786440 | tf_op jit(solution)/shard_map/ppermute | solution.py:357
  57.6 4.3 %grads.5 = (f32[1024,128]{1,0:T(8,128)S(1)}, f32[8,128,256]{2,1,0:T(8,128)S(1)}, bf16[8,128,256]{2,1,0:T(8,128)(2,1)S(1)}) custom-call(s32[32,2]{1,0:T(8,128)S(1)} %copy.12.order_ref.refs_0_, f32[3,16,256]{2,1,0:T(8,128)S(1)} %pad_maximum_fusion.refs_1_, f32[3,16,256]{2,1,0:T(8,128)S(1)} %collective-permute-done.8.refs_2_, ...), custom_call_target="tpu_custom_call" | custom-call | flops 1342177280 | bytes 4194304 | tf_op jit(solution)/shard_map/grads/pallas_call | solution.py:304
  62.4 3.3 %collective-permute-done.14.z3_ref = bf16[1024,128]{1,0:T(8,128)(2,1)S(1)} collective-permute-done((bf16[1024,128]{1,0:T(8,128)(2,1)S(1)}, bf16[1024,128]{1,0:T(8,128)(2,1)S(1)}, u32[]{:S(2)}, u32[]{:S(2)}) %collective-permute-start.14) | collective-permute-done | bytes 262176 | tf_op jit(solution)/shard_map/ppermute | solution.py:357
  65.9 2.8 %collective-permute-start.17 = (bf16[1024,128]{1,0:T(8,128)(2,1)S(1)}, bf16[1024,128]{1,0:T(8,128)(2,1)S(1)}, u32[]{:S(2)}, u32[]{:S(2)}) collective-permute-start(bf16[1024,128]{1,0:T(8,128)(2,1)S(1)} %middle.1.sum_ref), channel_id=1, source_target_pairs={{0,3},{1,0},{2,1},{3,2},{4,7},{5,4},{6,5},{7,6},{8,11},{9,8},{10,9... | collective-permute-start | bytes 786440 | tf_op jit(solution)/shard_map/ppermute | solution.py:353
  70.5 1.2 %collective-permute-start.19 = (bf16[2,128,256]{2,1,0:T(8,128)(2,1)S(1)}, bf16[2,128,256]{2,1,0:T(8,128)(2,1)S(1)}, u32[]{:S(2)}, u32[]{:S(2)}) collective-permute-start(bf16[2,128,256]{2,1,0:T(8,128)(2,1)S(1)} %get-tuple-element.52), channel_id=1, source_target_pairs={{0,24},{8,0},{16,8},{24,16},{1,25},{9,1},{17,9},{25,17},{2,26},{10... | collective-permute-start | bytes 393224 | tf_op jit(solution)/shard_map/ppermute | solution.py:357
  72.7 7.9 %collective-permute-done.17.x3_ref = bf16[1024,128]{1,0:T(8,128)(2,1)S(1)} collective-permute-done((bf16[1024,128]{1,0:T(8,128)(2,1)S(1)}, bf16[1024,128]{1,0:T(8,128)(2,1)S(1)}, u32[]{:S(2)}, u32[]{:S(2)}) %collective-permute-start.17) | collective-permute-done | bytes 262176 | tf_op jit(solution)/shard_map/ppermute | solution.py:353
  80.6 3.7 %collective-permute-done.15.x1_ref = bf16[1024,128]{1,0:T(8,128)(2,1)S(1)} collective-permute-done((bf16[1024,128]{1,0:T(8,128)(2,1)S(1)}, bf16[1024,128]{1,0:T(8,128)(2,1)S(1)}, u32[]{:S(2)}, u32[]{:S(2)}) %collective-permute-start.15) | collective-permute-done | bytes 262176 | tf_op jit(solution)/shard_map/ppermute | solution.py:353
  84.2 2.5 %collective-permute-done.21.y3_ref = bf16[2,128,256]{2,1,0:T(8,128)(2,1)S(1)} collective-permute-done((bf16[2,128,256]{2,1,0:T(8,128)(2,1)S(1)}, bf16[2,128,256]{2,1,0:T(8,128)(2,1)S(1)}, u32[]{:S(2)}, u32[]{:S(2)}) %collective-permute-start.21) | collective-permute-done | bytes 131104 | tf_op jit(solution)/shard_map/ppermute | solution.py:357
  (42 shorter events, 10.4 us)
Async XLA Ops:
  0.6 24.2 %copy-start.1 = (s32[32,2]{0,1:T(2,128)S(1)}, s32[32,2]{0,1:T(2,128)}, u32[]{:S(2)}) copy-start(s32[32,2]{0,1:T(2,128)} %param.5) | copy-start | bytes 772
  2.6 22.4 %copy-start = (bf16[1024,128]{1,0:T(8,128)(2,1)S(1)}, bf16[1024,128]{1,0:T(8,128)(2,1)}, u32[]{:S(2)}) copy-start(bf16[1024,128]{1,0:T(8,128)(2,1)} %get-tuple-element.31.refs_0_.refs_7_) | copy-start | bytes 786436
  2.6 10.1 %collective-permute-start.4 = (bf16[1024,128]{1,0:T(8,128)(2,1)}, bf16[1024,128]{1,0:T(8,128)(2,1)S(1)}, u32[]{:S(2)}, u32[]{:S(2)}) collective-permute-start(bf16[1024,128]{1,0:T(8,128)(2,1)} %get-tuple-element.31.refs_0_.refs_7_), channel_id=1, source_target_pairs={{0,96},{32,0},{64,32},{96,64},{1,97},{33,1},{65,33},{97,65},{2,98}... | collective-permute-start | bytes 786440 | tf_op jit(solution)/shard_map/ppermute | solution.py:353
  6.8 9.2 %collective-permute-start.3 = (bf16[1024,128]{1,0:T(8,128)(2,1)}, bf16[1024,128]{1,0:T(8,128)(2,1)S(1)}, u32[]{:S(2)}, u32[]{:S(2)}) collective-permute-start(bf16[1024,128]{1,0:T(8,128)(2,1)} %get-tuple-element.31.refs_0_.refs_7_), channel_id=1, source_target_pairs={{0,32},{32,64},{64,96},{96,0},{1,33},{33,65},{65,97},{97,1},{2,34}... | collective-permute-start | bytes 786440 | tf_op jit(solution)/shard_map/ppermute | solution.py:353
  6.8 14.2 %collective-permute-start.2 = (bf16[1024,128]{1,0:T(8,128)(2,1)}, bf16[1024,128]{1,0:T(8,128)(2,1)S(1)}, u32[]{:S(2)}, u32[]{:S(2)}) collective-permute-start(bf16[1024,128]{1,0:T(8,128)(2,1)} %get-tuple-element.29), channel_id=1, source_target_pairs={{0,24},{8,0},{16,8},{24,16},{1,25},{9,1},{17,9},{25,17},{2,26},{10... | collective-permute-start | bytes 786440 | tf_op jit(solution)/shard_map/ppermute | solution.py:353
  9.8 11.2 %collective-permute-start.1 = (bf16[1024,128]{1,0:T(8,128)(2,1)}, bf16[1024,128]{1,0:T(8,128)(2,1)S(1)}, u32[]{:S(2)}, u32[]{:S(2)}) collective-permute-start(bf16[1024,128]{1,0:T(8,128)(2,1)} %get-tuple-element.29), channel_id=1, source_target_pairs={{0,16},{8,24},{16,0},{24,8},{1,17},{9,25},{17,1},{25,9},{2,18},{10... | collective-permute-start | bytes 786440 | tf_op jit(solution)/shard_map/ppermute | solution.py:353
  10.5 14.2 %collective-permute-start = (bf16[1024,128]{1,0:T(8,128)(2,1)}, bf16[1024,128]{1,0:T(8,128)(2,1)S(1)}, u32[]{:S(2)}, u32[]{:S(2)}) collective-permute-start(bf16[1024,128]{1,0:T(8,128)(2,1)} %get-tuple-element.29), channel_id=1, source_target_pairs={{0,8},{8,16},{16,24},{24,0},{1,9},{9,17},{17,25},{25,1},{2,10},{10... | collective-permute-start | bytes 786440 | tf_op jit(solution)/shard_map/ppermute | solution.py:353
  16.0 8.7 %collective-permute-start.5 = (bf16[1024,128]{1,0:T(8,128)(2,1)}, bf16[1024,128]{1,0:T(8,128)(2,1)S(1)}, u32[]{:S(2)}, u32[]{:S(2)}) collective-permute-start(bf16[1024,128]{1,0:T(8,128)(2,1)} %get-tuple-element.31.refs_0_.refs_7_), channel_id=1, source_target_pairs={{0,64},{32,96},{64,0},{96,32},{1,65},{33,97},{65,1},{97,33},{2,66}... | collective-permute-start | bytes 786440 | tf_op jit(solution)/shard_map/ppermute | solution.py:353
  24.8 4.0 %collective-permute-start.6 = (bf16[4096,128]{1,0:T(8,128)(2,1)S(1)}, bf16[4096,128]{1,0:T(8,128)(2,1)S(1)}, u32[]{:S(2)}, u32[]{:S(2)}) collective-permute-start(bf16[4096,128]{1,0:T(8,128)(2,1)S(1)} %constant_dynamic-update-slice_fusion), channel_id=1, source_target_pairs={{0,4},{4,0},{1,5},{5,1},{2,6},{6,2},{3,7},{7,3},{8,12},{12,8},{9,1... | collective-permute-start | bytes 3145736 | tf_op jit(solution)/shard_map/ppermute | solution.py:361
  32.6 1.4 %collective-permute-start.7 = (f32[3,16,256]{2,1,0:T(8,128)S(1)}, f32[3,16,256]{2,1,0:T(8,128)S(1)}, u32[]{:S(2)}, u32[]{:S(2)}) collective-permute-start(f32[3,16,256]{2,1,0:T(8,128)S(1)} %stats.3), channel_id=1, source_target_pairs={{0,4},{4,0},{1,5},{5,1},{2,6},{6,2},{3,7},{7,3},{8,12},{12,8},{9,1... | collective-permute-start | bytes 147464 | tf_op jit(solution)/shard_map/ppermute | solution.py:361
  34.1 5.2 %collective-permute-start.10 = (f32[3,16,256]{2,1,0:T(8,128)S(1)}, f32[3,16,256]{2,1,0:T(8,128)S(1)}, u32[]{:S(2)}, u32[]{:S(2)}) collective-permute-start(f32[3,16,256]{2,1,0:T(8,128)S(1)} %pad_maximum_fusion.refs_1_), channel_id=1, source_target_pairs={{0,24},{8,0},{16,8},{24,16},{1,25},{9,1},{17,9},{25,17},{2,26},{10... | collective-permute-start | bytes 147464 | tf_op jit(solution)/shard_map/ppermute | solution.py:353
  37.1 5.8 %collective-permute-start.9 = (f32[3,16,256]{2,1,0:T(8,128)S(1)}, f32[3,16,256]{2,1,0:T(8,128)S(1)}, u32[]{:S(2)}, u32[]{:S(2)}) collective-permute-start(f32[3,16,256]{2,1,0:T(8,128)S(1)} %pad_maximum_fusion.refs_1_), channel_id=1, source_target_pairs={{0,16},{8,24},{16,0},{24,8},{1,17},{9,25},{17,1},{25,9},{2,18},{10... | collective-permute-start | bytes 147464 | tf_op jit(solution)/shard_map/ppermute | solution.py:353
  37.8 5.6 %collective-permute-start.8 = (f32[3,16,256]{2,1,0:T(8,128)S(1)}, f32[3,16,256]{2,1,0:T(8,128)S(1)}, u32[]{:S(2)}, u32[]{:S(2)}) collective-permute-start(f32[3,16,256]{2,1,0:T(8,128)S(1)} %pad_maximum_fusion.refs_1_), channel_id=1, source_target_pairs={{0,8},{8,16},{16,24},{24,0},{1,9},{9,17},{17,25},{25,1},{2,10},{10... | collective-permute-start | bytes 147464 | tf_op jit(solution)/shard_map/ppermute | solution.py:353
  47.1 8.3 %collective-permute-start.11 = (bf16[512,128]{1,0:T(8,128)(2,1)S(1)}, bf16[512,128]{1,0:T(8,128)(2,1)S(1)}, u32[]{:S(2)}, u32[]{:S(2)}) collective-permute-start(bf16[512,128]{1,0:T(8,128)(2,1)S(1)} %get-tuple-element.44), channel_id=1, source_target_pairs={{0,96},{32,0},{64,32},{96,64},{1,97},{33,1},{65,33},{97,65},{2,98}... | collective-permute-start | bytes 393224 | tf_op jit(solution)/shard_map/ppermute | solution.py:357
  47.9 7.5 %collective-permute-start.12 = (bf16[512,128]{1,0:T(8,128)(2,1)S(1)}, bf16[512,128]{1,0:T(8,128)(2,1)S(1)}, u32[]{:S(2)}, u32[]{:S(2)}) collective-permute-start(bf16[512,128]{1,0:T(8,128)(2,1)S(1)} %get-tuple-element.45), channel_id=1, source_target_pairs={{0,32},{32,64},{64,96},{96,0},{1,33},{33,65},{65,97},{97,1},{2,34}... | collective-permute-start | bytes 393224 | tf_op jit(solution)/shard_map/ppermute | solution.py:357
  55.5 6.9 %collective-permute-start.13 = (bf16[1024,128]{1,0:T(8,128)(2,1)S(1)}, bf16[1024,128]{1,0:T(8,128)(2,1)S(1)}, u32[]{:S(2)}, u32[]{:S(2)}) collective-permute-start(bf16[1024,128]{1,0:T(8,128)(2,1)S(1)} %get-tuple-element.46), channel_id=1, source_target_pairs={{0,96},{32,0},{64,32},{96,64},{1,97},{33,1},{65,33},{97,65},{2,98}... | collective-permute-start | bytes 786440 | tf_op jit(solution)/shard_map/ppermute | solution.py:357
  57.4 8.3 %collective-permute-start.14 = (bf16[1024,128]{1,0:T(8,128)(2,1)S(1)}, bf16[1024,128]{1,0:T(8,128)(2,1)S(1)}, u32[]{:S(2)}, u32[]{:S(2)}) collective-permute-start(bf16[1024,128]{1,0:T(8,128)(2,1)S(1)} %get-tuple-element.47), channel_id=1, source_target_pairs={{0,32},{32,64},{64,96},{96,0},{1,33},{33,65},{65,97},{97,1},{2,34}... | collective-permute-start | bytes 786440 | tf_op jit(solution)/shard_map/ppermute | solution.py:357
  65.8 4.6 %collective-permute-start.18 = (bf16[8,128,256]{2,1,0:T(8,128)(2,1)S(1)}, bf16[8,128,256]{2,1,0:T(8,128)(2,1)S(1)}, u32[]{:S(2)}, u32[]{:S(2)}) collective-permute-start(bf16[8,128,256]{2,1,0:T(8,128)(2,1)S(1)} %get-tuple-element.50), channel_id=1, source_target_pairs={{0,4},{4,0},{1,5},{5,1},{2,6},{6,2},{3,7},{7,3},{8,12},{12,8},{9,1... | collective-permute-start | bytes 1572872 | tf_op jit(solution)/shard_map/ppermute | solution.py:361
  65.9 14.7 %collective-permute-start.17 = (bf16[1024,128]{1,0:T(8,128)(2,1)S(1)}, bf16[1024,128]{1,0:T(8,128)(2,1)S(1)}, u32[]{:S(2)}, u32[]{:S(2)}) collective-permute-start(bf16[1024,128]{1,0:T(8,128)(2,1)S(1)} %middle.1.sum_ref), channel_id=1, source_target_pairs={{0,3},{1,0},{2,1},{3,2},{4,7},{5,4},{6,5},{7,6},{8,11},{9,8},{10,9... | collective-permute-start | bytes 786440 | tf_op jit(solution)/shard_map/ppermute | solution.py:353
  68.7 11.8 %collective-permute-start.16 = (bf16[1024,128]{1,0:T(8,128)(2,1)S(1)}, bf16[1024,128]{1,0:T(8,128)(2,1)S(1)}, u32[]{:S(2)}, u32[]{:S(2)}) collective-permute-start(bf16[1024,128]{1,0:T(8,128)(2,1)S(1)} %middle.1.sum_ref), channel_id=1, source_target_pairs={{0,2},{1,3},{2,0},{3,1},{4,6},{5,7},{6,4},{7,5},{8,10},{9,11},{10,... | collective-permute-start | bytes 786440 | tf_op jit(solution)/shard_map/ppermute | solution.py:353
  69.5 14.7 %collective-permute-start.15 = (bf16[1024,128]{1,0:T(8,128)(2,1)S(1)}, bf16[1024,128]{1,0:T(8,128)(2,1)S(1)}, u32[]{:S(2)}, u32[]{:S(2)}) collective-permute-start(bf16[1024,128]{1,0:T(8,128)(2,1)S(1)} %middle.1.sum_ref), channel_id=1, source_target_pairs={{0,1},{1,2},{2,3},{3,0},{4,5},{5,6},{6,7},{7,4},{8,9},{9,10},{10,1... | collective-permute-start | bytes 786440 | tf_op jit(solution)/shard_map/ppermute | solution.py:353
  70.5 13.7 %collective-permute-start.19 = (bf16[2,128,256]{2,1,0:T(8,128)(2,1)S(1)}, bf16[2,128,256]{2,1,0:T(8,128)(2,1)S(1)}, u32[]{:S(2)}, u32[]{:S(2)}) collective-permute-start(bf16[2,128,256]{2,1,0:T(8,128)(2,1)S(1)} %get-tuple-element.52), channel_id=1, source_target_pairs={{0,24},{8,0},{16,8},{24,16},{1,25},{9,1},{17,9},{25,17},{2,26},{10... | collective-permute-start | bytes 393224 | tf_op jit(solution)/shard_map/ppermute | solution.py:357
  71.8 12.5 %collective-permute-start.20 = (bf16[2,128,256]{2,1,0:T(8,128)(2,1)S(1)}, bf16[2,128,256]{2,1,0:T(8,128)(2,1)S(1)}, u32[]{:S(2)}, u32[]{:S(2)}) collective-permute-start(bf16[2,128,256]{2,1,0:T(8,128)(2,1)S(1)} %get-tuple-element.53), channel_id=1, source_target_pairs={{0,16},{8,24},{16,0},{24,8},{1,17},{9,25},{17,1},{25,9},{2,18},{10... | collective-permute-start | bytes 393224 | tf_op jit(solution)/shard_map/ppermute | solution.py:357
  80.6 6.2 %collective-permute-start.21 = (bf16[2,128,256]{2,1,0:T(8,128)(2,1)S(1)}, bf16[2,128,256]{2,1,0:T(8,128)(2,1)S(1)}, u32[]{:S(2)}, u32[]{:S(2)}) collective-permute-start(bf16[2,128,256]{2,1,0:T(8,128)(2,1)S(1)} %get-tuple-element.54), channel_id=1, source_target_pairs={{0,8},{8,16},{16,24},{24,0},{1,9},{9,17},{17,25},{25,1},{2,10},{10... | collective-permute-start | bytes 393224 | tf_op jit(solution)/shard_map/ppermute | solution.py:357

commit v6 on v5

--- a/solution.py
+++ b/solution.py
@@ -247,19 +247,28 @@
     sum_ref[...] = total.astype(BF16)
 
 
-def query_kernel(keep_ref, other_ref, dq_ref, r1_ref, r2_ref, r3_ref):
-    for k, ref in enumerate((dq_ref, r1_ref, r2_ref, r3_ref)):
+def query_kernel(keep_ref, other_ref, dq_ref, r1_ref, r3_ref, first_ref, second_ref):
+    for k, ref in ((0, dq_ref), (1, r1_ref), (3, r3_ref)):
         slots = pl.ds(2 * k, 2)
-        ref[...] = (keep_ref[slots] + other_ref[slots].astype(F32)).astype(ref.dtype)
-
-
-def last_kernel(sum_ref, x1_ref, x2_ref, x3_ref, dq_ref, y1_ref, y2_ref, y3_ref, q_out, k_out, v_out):
+        ref[...] = keep_ref[slots] + other_ref[slots].astype(F32)
+    for slot, ref in ((4, first_ref), (5, second_ref)):
+        ref[...] = (keep_ref[slot] + other_ref[slot].astype(F32)).astype(BF16)
+
+
+def query_relay_kernel(r1_ref, r3_ref, first_ref, second_ref, out1_ref, out3_ref):
+    out1_ref[0] = (r1_ref[0] + first_ref[...].astype(F32)).astype(BF16)
+    out1_ref[1] = r1_ref[1].astype(BF16)
+    out3_ref[0] = r3_ref[0].astype(BF16)
+    out3_ref[1] = (r3_ref[1] + second_ref[...].astype(F32)).astype(BF16)
+
+
+def last_kernel(sum_ref, x1_ref, x2_ref, x3_ref, dq_ref, y1_ref, y3_ref, q_out, k_out, v_out):
     own, x1, x2, x3 = [ref[...].astype(F32) for ref in (sum_ref, x1_ref, x2_ref, x3_ref)]
     total = (own + x2) + (x1 + x3)
     k_out[...] = (total[: 2 * SPAN] * SCALE).astype(BF16)
     v_out[...] = total[2 * SPAN :].astype(BF16)
     dq = dq_ref[...]
-    for ref in (y1_ref, y2_ref, y3_ref):
+    for ref in (y1_ref, y3_ref):
         dq = dq + ref[...].astype(F32)
     for slot in range(2):
         q_out[pl.ds(slot * SPAN, SPAN), :] = (dq[slot] * SCALE).T.astype(BF16)
@@ -394,11 +403,15 @@
     dq_send, summed = lax.optimization_barrier((dq_send, summed))
     dq_other = swap_core(dq_send)
     rows, slots = (2 * SPAN, DH), (2, DH, SPAN)
-    dq, r1, r2, r3 = plain_call(
-        query_kernel, "query", [(slots, F32), (slots, BF16), (slots, BF16), (slots, BF16)], dq_keep, dq_other
+    one = (DH, SPAN)
+    dq, r1, r3, first, second = plain_call(
+        query_kernel, "query", [(slots, F32)] * 3 + [(one, BF16)] * 2, dq_keep, dq_other
+    )
+    r1, r3 = plain_call(
+        query_relay_kernel, "query_relay", [(slots, BF16)] * 2, r1, r3, ahead(first, "y", 1), ahead(second, "y", 3)
     )
     xs = [back(summed, "x", k) for k in (1, 2, 3)]
-    ys = [ahead(part, "y", k) for k, part in ((1, r1), (2, r2), (3, r3))]
+    ys = [ahead(r1, "y", 1), ahead(r3, "y", 3)]
     return plain_call(last_kernel, "last", [(rows, BF16)] * 3, summed, *xs, dq, *ys)
 
 

time: 88.7 us -> 86.2 us (0.972)
  waiting for transfers between devices: 35.7 us -> 31.1 us
  starting transfers between devices: 25 us -> 27 us
    ppermute x12, waiting for transfers between devices: 28.5 us -> 21.8 us  [back(): return lax.ppermute(value, axis, [(i, (i + k) % 4) for i in range(4)])]
    ppermute x7 -> x8, waiting for transfers between devices: 6.34 us -> 8.48 us  [ahead(): return lax.ppermute(value, axis, [(i, (i - k) % 4) for i in range(4)])]
    ppermute x7 -> x8, starting transfers between devices: 6.32 us -> 8.37 us  [ahead(): return lax.ppermute(value, axis, [(i, (i - k) % 4) for i in range(4)])]
  transfers between devices with their start and end apart: 22 -> 23, of which waited for: 13 -> 14; matrix products, arithmetic and copies ran while one was open for 1% -> 1% of each run, Pallas kernels for 16% -> 17%
where the time goes in v6:
time: 86.2 us; the launch traced here: 85.2 us
  waiting for transfers between devices  31.1 us (36%)
  starting transfers between devices  27 us (31%)
  Pallas kernels  25 us (29%)
  local copies, waits for them, and re-layouts  1.17 us (1%)
    ppermute x12, waiting for transfers between devices, back(): return lax.ppermute(value, axis, [(i, (i + k) % 4) for i in range(4)])  21.8 us
    ppermute x12, starting transfers between devices, back(): return lax.ppermute(value, axis, [(i, (i + k) % 4) for i in range(4)])  17.9 us
    pallas_call x3, Pallas kernels, call_grads(): pl.pallas_call(functools.partial(grads_kernel, pieces, first, last), out_...  14.2 us
    ppermute x8, waiting for transfers between devices, ahead(): return lax.ppermute(value, axis, [(i, (i - k) % 4) for i in range(4)])  8.48 us
    ppermute x8, starting transfers between devices, ahead(): return lax.ppermute(value, axis, [(i, (i - k) % 4) for i in range(4)])  8.37 us
    pallas_call x2, Pallas kernels, call_stats(): pl.pallas_call(functools.partial(stats_kernel, far), out_shape=jax.ShapeD...  7.63 us
    pallas_call x1, Pallas kernels, call_pack(): pl.pallas_call(pack_kernel, out_shape=(jax.ShapeDtypeStruct((PIECE, DH),...  1.94 us
  transfers between devices with their start and end apart: 23, of which 14 were waited for; matrix products, arithmetic and copies ran while one was open for 1% of the time, Pallas kernels for 17%

profile of v6, /device:TPU:0, one launch (start us, length us, event | category | flops | bytes accessed | tf_op | source)
XLA Modules:
  0.0 85.2 jit_solution(12146371382170197775)
XLA Ops:
  0.6 1.9 %pack.1 = (bf16[1024,128]{1,0:T(8,128)(2,1)}, bf16[1024,128]{1,0:T(8,128)(2,1)}) custom-call(bf16[512,128]{1,0:T(8,128)(2,1)} %queries_ref.1, bf16[512,128]{1,0:T(8,128)(2,1)} %keys_ref.1, bf16[512,128]{1,0:T(8,128)(2,1)} %values_ref.1, bf16[512,128]{1,0:T(8,128)(2,1)} %grads_ref.1), custom_call_target="tpu_custom_call" | custom-call | tf_op jit(solution)/shard_map/pack/pallas_call | solution.py:350
  2.6 4.2 %collective-permute-start.4 = (bf16[1024,128]{1,0:T(8,128)(2,1)}, bf16[1024,128]{1,0:T(8,128)(2,1)S(1)}, u32[]{:S(2)}, u32[]{:S(2)}) collective-permute-start(bf16[1024,128]{1,0:T(8,128)(2,1)} %get-tuple-element.34.refs_0_.refs_7_), channel_id=1, source_target_pairs={{0,96},{32,0},{64,32},{96,64},{1,97},{33,1},{65,33},{97,65},{2,98}... | collective-permute-start | bytes 786440 | tf_op jit(solution)/shard_map/ppermute | solution.py:362
  6.8 3.0 %collective-permute-start.2 = (bf16[1024,128]{1,0:T(8,128)(2,1)}, bf16[1024,128]{1,0:T(8,128)(2,1)S(1)}, u32[]{:S(2)}, u32[]{:S(2)}) collective-permute-start(bf16[1024,128]{1,0:T(8,128)(2,1)} %get-tuple-element.32), channel_id=1, source_target_pairs={{0,24},{8,0},{16,8},{24,16},{1,25},{9,1},{17,9},{25,17},{2,26},{10... | collective-permute-start | bytes 786440 | tf_op jit(solution)/shard_map/ppermute | solution.py:362
  11.4 1.3 %collective-permute-done.4.refs_3_.refs_8_ = bf16[1024,128]{1,0:T(8,128)(2,1)S(1)} collective-permute-done((bf16[1024,128]{1,0:T(8,128)(2,1)}, bf16[1024,128]{1,0:T(8,128)(2,1)S(1)}, u32[]{:S(2)}, u32[]{:S(2)}) %collective-permute-start.4) | collective-permute-done | bytes 262176 | tf_op jit(solution)/shard_map/ppermute | solution.py:362
  12.7 3.3 %collective-permute-done.3.refs_1_.refs_7_ = bf16[1024,128]{1,0:T(8,128)(2,1)S(1)} collective-permute-done((bf16[1024,128]{1,0:T(8,128)(2,1)}, bf16[1024,128]{1,0:T(8,128)(2,1)S(1)}, u32[]{:S(2)}, u32[]{:S(2)}) %collective-permute-start.3) | collective-permute-done | bytes 262176 | tf_op jit(solution)/shard_map/ppermute | solution.py:362
  17.0 4.1 %collective-permute-done.2 = bf16[1024,128]{1,0:T(8,128)(2,1)S(1)} collective-permute-done((bf16[1024,128]{1,0:T(8,128)(2,1)}, bf16[1024,128]{1,0:T(8,128)(2,1)S(1)}, u32[]{:S(2)}, u32[]{:S(2)}) %collective-permute-start.2) | collective-permute-done | bytes 262176 | tf_op jit(solution)/shard_map/ppermute | solution.py:362
  21.0 3.6 %collective-permute-done = bf16[1024,128]{1,0:T(8,128)(2,1)S(1)} collective-permute-done((bf16[1024,128]{1,0:T(8,128)(2,1)}, bf16[1024,128]{1,0:T(8,128)(2,1)S(1)}, u32[]{:S(2)}, u32[]{:S(2)}) %collective-permute-start) | collective-permute-done | bytes 262176 | tf_op jit(solution)/shard_map/ppermute | solution.py:362
  25.0 3.8 %stats.2.refs_4_ = f32[3,16,256]{2,1,0:T(8,128)S(1)} custom-call(s32[32,2]{1,0:T(8,128)S(1)} %copy.12.order_ref.refs_0_, bf16[4,1024,128]{2,1,0:T(8,128)(2,1)S(1)} %bitcast.2, bf16[1024,128]{1,0:T(8,128)(2,1)S(1)} %copy-done, bf16[1024,128]{1,0:T(8,128)(2,1)S(1)} %collective-permute-done.3.refs_1_.refs_7_, ...), custom_call_target="tpu_custom_call" | custom-call | flops 1073741824 | bytes 2097152 | tf_op jit(solution)/shard_map/stats/pallas_call | solution.py:284
  28.8 3.8 %stats.3 = f32[3,16,256]{2,1,0:T(8,128)S(1)} custom-call(s32[32,2]{1,0:T(8,128)S(1)} %copy.12.order_ref.refs_0_, bf16[4,1024,128]{2,1,0:T(8,128)(2,1)S(1)} %bitcast.6, bf16[1024,128]{1,0:T(8,128)(2,1)S(1)} %copy-done, bf16[1024,128]{1,0:T(8,128)(2,1)S(1)} %collective-permute-done.3.refs_1_.refs_7_, ...), custom_call_target="tpu_custom_call" | custom-call | flops 1073741824 | bytes 2097152 | tf_op jit(solution)/shard_map/stats/pallas_call | solution.py:284
  34.1 3.0 %collective-permute-start.10 = (f32[3,16,256]{2,1,0:T(8,128)S(1)}, f32[3,16,256]{2,1,0:T(8,128)S(1)}, u32[]{:S(2)}, u32[]{:S(2)}) collective-permute-start(f32[3,16,256]{2,1,0:T(8,128)S(1)} %pad_maximum_fusion.refs_1_), channel_id=1, source_target_pairs={{0,24},{8,0},{16,8},{24,16},{1,25},{9,1},{17,9},{25,17},{2,26},{10... | collective-permute-start | bytes 147464 | tf_op jit(solution)/shard_map/ppermute | solution.py:362
  39.3 3.6 %collective-permute-done.9.refs_3_ = f32[3,16,256]{2,1,0:T(8,128)S(1)} collective-permute-done((f32[3,16,256]{2,1,0:T(8,128)S(1)}, f32[3,16,256]{2,1,0:T(8,128)S(1)}, u32[]{:S(2)}, u32[]{:S(2)}) %collective-permute-start.9) | collective-permute-done | bytes 49184 | tf_op jit(solution)/shard_map/ppermute | solution.py:362
  43.4 3.7 %grads.3 = (bf16[512,128]{1,0:T(8,128)(2,1)S(1)}, bf16[512,128]{1,0:T(8,128)(2,1)S(1)}, f32[16,128,256]{2,1,0:T(8,128)S(1)}) custom-call(s32[32,2]{1,0:T(8,128)S(1)} %copy.12.order_ref.refs_0_, f32[3,16,256]{2,1,0:T(8,128)S(1)} %pad_maximum_fusion.refs_1_, f32[3,16,256]{2,1,0:T(8,128)S(1)} %collective-permute-done.8.refs_2_, ...), custom_call_target="tpu_custom_call" | custom-call | flops 1342177280 | bytes 4194304 | tf_op jit(solution)/shard_map/grads/pallas_call | solution.py:313
  47.8 1.4 %collective-permute-start.12 = (bf16[512,128]{1,0:T(8,128)(2,1)S(1)}, bf16[512,128]{1,0:T(8,128)(2,1)S(1)}, u32[]{:S(2)}, u32[]{:S(2)}) collective-permute-start(bf16[512,128]{1,0:T(8,128)(2,1)S(1)} %get-tuple-element.48), channel_id=1, source_target_pairs={{0,32},{32,64},{64,96},{96,0},{1,33},{33,65},{65,97},{97,1},{2,34}... | collective-permute-start | bytes 393224 | tf_op jit(solution)/shard_map/ppermute | solution.py:366
  49.2 6.2 %grads.4 = (f32[1024,128]{1,0:T(8,128)S(1)}, f32[1024,128]{1,0:T(8,128)S(1)}, f32[16,128,256]{2,1,0:T(8,128)S(1)}) custom-call(s32[32,2]{1,0:T(8,128)S(1)} %copy.12.order_ref.refs_0_, f32[3,16,256]{2,1,0:T(8,128)S(1)} %pad_maximum_fusion.refs_1_, f32[3,16,256]{2,1,0:T(8,128)S(1)} %collective-permute-done.8.refs_2_, ...), custom_call_target="tpu_custom_call" | custom-call | flops 2684354560 | bytes 4194304 | tf_op jit(solution)/shard_map/grads/pallas_call | solution.py:313
  55.5 2.0 %collective-permute-start.13 = (bf16[1024,128]{1,0:T(8,128)(2,1)S(1)}, bf16[1024,128]{1,0:T(8,128)(2,1)S(1)}, u32[]{:S(2)}, u32[]{:S(2)}) collective-permute-start(bf16[1024,128]{1,0:T(8,128)(2,1)S(1)} %get-tuple-element.49), channel_id=1, source_target_pairs={{0,96},{32,0},{64,32},{96,64},{1,97},{33,1},{65,33},{97,65},{2,98}... | collective-permute-start | bytes 786440 | tf_op jit(solution)/shard_map/ppermute | solution.py:366
  57.6 4.3 %grads.5 = (f32[1024,128]{1,0:T(8,128)S(1)}, f32[8,128,256]{2,1,0:T(8,128)S(1)}, bf16[8,128,256]{2,1,0:T(8,128)(2,1)S(1)}) custom-call(s32[32,2]{1,0:T(8,128)S(1)} %copy.12.order_ref.refs_0_, f32[3,16,256]{2,1,0:T(8,128)S(1)} %pad_maximum_fusion.refs_1_, f32[3,16,256]{2,1,0:T(8,128)S(1)} %collective-permute-done.8.refs_2_, ...), custom_call_target="tpu_custom_call" | custom-call | flops 1342177280 | bytes 4194304 | tf_op jit(solution)/shard_map/grads/pallas_call | solution.py:313
  62.4 3.3 %collective-permute-done.14.z3_ref = bf16[1024,128]{1,0:T(8,128)(2,1)S(1)} collective-permute-done((bf16[1024,128]{1,0:T(8,128)(2,1)S(1)}, bf16[1024,128]{1,0:T(8,128)(2,1)S(1)}, u32[]{:S(2)}, u32[]{:S(2)}) %collective-permute-start.14) | collective-permute-done | bytes 262176 | tf_op jit(solution)/shard_map/ppermute | solution.py:366
  65.9 2.8 %collective-permute-start.17 = (bf16[1024,128]{1,0:T(8,128)(2,1)S(1)}, bf16[1024,128]{1,0:T(8,128)(2,1)S(1)}, u32[]{:S(2)}, u32[]{:S(2)}) collective-permute-start(bf16[1024,128]{1,0:T(8,128)(2,1)S(1)} %middle.1.sum_ref), channel_id=1, source_target_pairs={{0,3},{1,0},{2,1},{3,2},{4,7},{5,4},{6,5},{7,6},{8,11},{9,8},{10,9... | collective-permute-start | bytes 786440 | tf_op jit(solution)/shard_map/ppermute | solution.py:362
  70.5 1.3 %collective-permute-start.19 = (bf16[128,256]{1,0:T(8,128)(2,1)S(1)}, bf16[128,256]{1,0:T(8,128)(2,1)S(1)}, u32[]{:S(2)}, u32[]{:S(2)}) collective-permute-start(bf16[128,256]{1,0:T(8,128)(2,1)S(1)} %get-tuple-element.57), channel_id=1, source_target_pairs={{0,24},{8,0},{16,8},{24,16},{1,25},{9,1},{17,9},{25,17},{2,26},{10... | collective-permute-start | bytes 196616 | tf_op jit(solution)/shard_map/ppermute | solution.py:366
  72.6 2.2 %collective-permute-done.19.first_ref = bf16[128,256]{1,0:T(8,128)(2,1)S(1)} collective-permute-done((bf16[128,256]{1,0:T(8,128)(2,1)S(1)}, bf16[128,256]{1,0:T(8,128)(2,1)S(1)}, u32[]{:S(2)}, u32[]{:S(2)}) %collective-permute-start.19) | collective-permute-done | bytes 65568 | tf_op jit(solution)/shard_map/ppermute | solution.py:366
  74.8 2.4 %collective-permute-done.20.second_ref = bf16[128,256]{1,0:T(8,128)(2,1)S(1)} collective-permute-done((bf16[128,256]{1,0:T(8,128)(2,1)S(1)}, bf16[128,256]{1,0:T(8,128)(2,1)S(1)}, u32[]{:S(2)}, u32[]{:S(2)}) %collective-permute-start.20) | collective-permute-done | bytes 65568 | tf_op jit(solution)/shard_map/ppermute | solution.py:366
  77.3 2.0 %collective-permute-start.22 = (bf16[2,128,256]{2,1,0:T(8,128)(2,1)S(1)}, bf16[2,128,256]{2,1,0:T(8,128)(2,1)S(1)}, u32[]{:S(2)}, u32[]{:S(2)}) collective-permute-start(bf16[2,128,256]{2,1,0:T(8,128)(2,1)S(1)} %get-tuple-element.60), channel_id=1, source_target_pairs={{0,8},{8,16},{16,24},{24,0},{1,9},{9,17},{17,25},{25,1},{2,10},{10... | collective-permute-start | bytes 393224 | tf_op jit(solution)/shard_map/ppermute | solution.py:366
  79.3 1.2 %collective-permute-done.17.x3_ref = bf16[1024,128]{1,0:T(8,128)(2,1)S(1)} collective-permute-done((bf16[1024,128]{1,0:T(8,128)(2,1)S(1)}, bf16[1024,128]{1,0:T(8,128)(2,1)S(1)}, u32[]{:S(2)}, u32[]{:S(2)}) %collective-permute-start.17) | collective-permute-done | bytes 262176 | tf_op jit(solution)/shard_map/ppermute | solution.py:362
  80.5 3.7 %collective-permute-done.15.x1_ref = bf16[1024,128]{1,0:T(8,128)(2,1)S(1)} collective-permute-done((bf16[1024,128]{1,0:T(8,128)(2,1)S(1)}, bf16[1024,128]{1,0:T(8,128)(2,1)S(1)}, u32[]{:S(2)}, u32[]{:S(2)}) %collective-permute-start.15) | collective-permute-done | bytes 262176 | tf_op jit(solution)/shard_map/ppermute | solution.py:362
  (45 shorter events, 12.4 us)
Async XLA Ops:
  0.6 24.2 %copy-start.1 = (s32[32,2]{0,1:T(2,128)S(1)}, s32[32,2]{0,1:T(2,128)}, u32[]{:S(2)}) copy-start(s32[32,2]{0,1:T(2,128)} %param.5) | copy-start | bytes 772
  2.6 10.1 %collective-permute-start.4 = (bf16[1024,128]{1,0:T(8,128)(2,1)}, bf16[1024,128]{1,0:T(8,128)(2,1)S(1)}, u32[]{:S(2)}, u32[]{:S(2)}) collective-permute-start(bf16[1024,128]{1,0:T(8,128)(2,1)} %get-tuple-element.34.refs_0_.refs_7_), channel_id=1, source_target_pairs={{0,96},{32,0},{64,32},{96,64},{1,97},{33,1},{65,33},{97,65},{2,98}... | collective-permute-start | bytes 786440 | tf_op jit(solution)/shard_map/ppermute | solution.py:362
  6.8 9.2 %collective-permute-start.3 = (bf16[1024,128]{1,0:T(8,128)(2,1)}, bf16[1024,128]{1,0:T(8,128)(2,1)S(1)}, u32[]{:S(2)}, u32[]{:S(2)}) collective-permute-start(bf16[1024,128]{1,0:T(8,128)(2,1)} %get-tuple-element.34.refs_0_.refs_7_), channel_id=1, source_target_pairs={{0,32},{32,64},{64,96},{96,0},{1,33},{33,65},{65,97},{97,1},{2,34}... | collective-permute-start | bytes 786440 | tf_op jit(solution)/shard_map/ppermute | solution.py:362
  6.8 14.2 %collective-permute-start.2 = (bf16[1024,128]{1,0:T(8,128)(2,1)}, bf16[1024,128]{1,0:T(8,128)(2,1)S(1)}, u32[]{:S(2)}, u32[]{:S(2)}) collective-permute-start(bf16[1024,128]{1,0:T(8,128)(2,1)} %get-tuple-element.32), channel_id=1, source_target_pairs={{0,24},{8,0},{16,8},{24,16},{1,25},{9,1},{17,9},{25,17},{2,26},{10... | collective-permute-start | bytes 786440 | tf_op jit(solution)/shard_map/ppermute | solution.py:362
  9.8 11.2 %collective-permute-start.1 = (bf16[1024,128]{1,0:T(8,128)(2,1)}, bf16[1024,128]{1,0:T(8,128)(2,1)S(1)}, u32[]{:S(2)}, u32[]{:S(2)}) collective-permute-start(bf16[1024,128]{1,0:T(8,128)(2,1)} %get-tuple-element.32), channel_id=1, source_target_pairs={{0,16},{8,24},{16,0},{24,8},{1,17},{9,25},{17,1},{25,9},{2,18},{10... | collective-permute-start | bytes 786440 | tf_op jit(solution)/shard_map/ppermute | solution.py:362
  10.4 14.2 %collective-permute-start = (bf16[1024,128]{1,0:T(8,128)(2,1)}, bf16[1024,128]{1,0:T(8,128)(2,1)S(1)}, u32[]{:S(2)}, u32[]{:S(2)}) collective-permute-start(bf16[1024,128]{1,0:T(8,128)(2,1)} %get-tuple-element.32), channel_id=1, source_target_pairs={{0,8},{8,16},{16,24},{24,0},{1,9},{9,17},{17,25},{25,1},{2,10},{10... | collective-permute-start | bytes 786440 | tf_op jit(solution)/shard_map/ppermute | solution.py:362
  16.0 8.7 %collective-permute-start.5 = (bf16[1024,128]{1,0:T(8,128)(2,1)}, bf16[1024,128]{1,0:T(8,128)(2,1)S(1)}, u32[]{:S(2)}, u32[]{:S(2)}) collective-permute-start(bf16[1024,128]{1,0:T(8,128)(2,1)} %get-tuple-element.34.refs_0_.refs_7_), channel_id=1, source_target_pairs={{0,64},{32,96},{64,0},{96,32},{1,65},{33,97},{65,1},{97,33},{2,66}... | collective-permute-start | bytes 786440 | tf_op jit(solution)/shard_map/ppermute | solution.py:362
  24.8 4.0 %collective-permute-start.6 = (bf16[4096,128]{1,0:T(8,128)(2,1)S(1)}, bf16[4096,128]{1,0:T(8,128)(2,1)S(1)}, u32[]{:S(2)}, u32[]{:S(2)}) collective-permute-start(bf16[4096,128]{1,0:T(8,128)(2,1)S(1)} %constant_dynamic-update-slice_fusion), channel_id=1, source_target_pairs={{0,4},{4,0},{1,5},{5,1},{2,6},{6,2},{3,7},{7,3},{8,12},{12,8},{9,1... | collective-permute-start | bytes 3145736 | tf_op jit(solution)/shard_map/ppermute | solution.py:370
  32.6 1.4 %collective-permute-start.7 = (f32[3,16,256]{2,1,0:T(8,128)S(1)}, f32[3,16,256]{2,1,0:T(8,128)S(1)}, u32[]{:S(2)}, u32[]{:S(2)}) collective-permute-start(f32[3,16,256]{2,1,0:T(8,128)S(1)} %stats.3), channel_id=1, source_target_pairs={{0,4},{4,0},{1,5},{5,1},{2,6},{6,2},{3,7},{7,3},{8,12},{12,8},{9,1... | collective-permute-start | bytes 147464 | tf_op jit(solution)/shard_map/ppermute | solution.py:370
  34.1 5.2 %collective-permute-start.10 = (f32[3,16,256]{2,1,0:T(8,128)S(1)}, f32[3,16,256]{2,1,0:T(8,128)S(1)}, u32[]{:S(2)}, u32[]{:S(2)}) collective-permute-start(f32[3,16,256]{2,1,0:T(8,128)S(1)} %pad_maximum_fusion.refs_1_), channel_id=1, source_target_pairs={{0,24},{8,0},{16,8},{24,16},{1,25},{9,1},{17,9},{25,17},{2,26},{10... | collective-permute-start | bytes 147464 | tf_op jit(solution)/shard_map/ppermute | solution.py:362
  37.1 5.8 %collective-permute-start.9 = (f32[3,16,256]{2,1,0:T(8,128)S(1)}, f32[3,16,256]{2,1,0:T(8,128)S(1)}, u32[]{:S(2)}, u32[]{:S(2)}) collective-permute-start(f32[3,16,256]{2,1,0:T(8,128)S(1)} %pad_maximum_fusion.refs_1_), channel_id=1, source_target_pairs={{0,16},{8,24},{16,0},{24,8},{1,17},{9,25},{17,1},{25,9},{2,18},{10... | collective-permute-start | bytes 147464 | tf_op jit(solution)/shard_map/ppermute | solution.py:362
  37.7 5.6 %collective-permute-start.8 = (f32[3,16,256]{2,1,0:T(8,128)S(1)}, f32[3,16,256]{2,1,0:T(8,128)S(1)}, u32[]{:S(2)}, u32[]{:S(2)}) collective-permute-start(f32[3,16,256]{2,1,0:T(8,128)S(1)} %pad_maximum_fusion.refs_1_), channel_id=1, source_target_pairs={{0,8},{8,16},{16,24},{24,0},{1,9},{9,17},{17,25},{25,1},{2,10},{10... | collective-permute-start | bytes 147464 | tf_op jit(solution)/shard_map/ppermute | solution.py:362
  47.1 8.3 %collective-permute-start.11 = (bf16[512,128]{1,0:T(8,128)(2,1)S(1)}, bf16[512,128]{1,0:T(8,128)(2,1)S(1)}, u32[]{:S(2)}, u32[]{:S(2)}) collective-permute-start(bf16[512,128]{1,0:T(8,128)(2,1)S(1)} %get-tuple-element.47), channel_id=1, source_target_pairs={{0,96},{32,0},{64,32},{96,64},{1,97},{33,1},{65,33},{97,65},{2,98}... | collective-permute-start | bytes 393224 | tf_op jit(solution)/shard_map/ppermute | solution.py:366
  47.8 7.5 %collective-permute-start.12 = (bf16[512,128]{1,0:T(8,128)(2,1)S(1)}, bf16[512,128]{1,0:T(8,128)(2,1)S(1)}, u32[]{:S(2)}, u32[]{:S(2)}) collective-permute-start(bf16[512,128]{1,0:T(8,128)(2,1)S(1)} %get-tuple-element.48), channel_id=1, source_target_pairs={{0,32},{32,64},{64,96},{96,0},{1,33},{33,65},{65,97},{97,1},{2,34}... | collective-permute-start | bytes 393224 | tf_op jit(solution)/shard_map/ppermute | solution.py:366
  55.5 7.0 %collective-permute-start.13 = (bf16[1024,128]{1,0:T(8,128)(2,1)S(1)}, bf16[1024,128]{1,0:T(8,128)(2,1)S(1)}, u32[]{:S(2)}, u32[]{:S(2)}) collective-permute-start(bf16[1024,128]{1,0:T(8,128)(2,1)S(1)} %get-tuple-element.49), channel_id=1, source_target_pairs={{0,96},{32,0},{64,32},{96,64},{1,97},{33,1},{65,33},{97,65},{2,98}... | collective-permute-start | bytes 786440 | tf_op jit(solution)/shard_map/ppermute | solution.py:366
  57.4 8.3 %collective-permute-start.14 = (bf16[1024,128]{1,0:T(8,128)(2,1)S(1)}, bf16[1024,128]{1,0:T(8,128)(2,1)S(1)}, u32[]{:S(2)}, u32[]{:S(2)}) collective-permute-start(bf16[1024,128]{1,0:T(8,128)(2,1)S(1)} %get-tuple-element.50), channel_id=1, source_target_pairs={{0,32},{32,64},{64,96},{96,0},{1,33},{33,65},{65,97},{97,1},{2,34}... | collective-permute-start | bytes 786440 | tf_op jit(solution)/shard_map/ppermute | solution.py:366
  65.8 4.6 %collective-permute-start.18 = (bf16[8,128,256]{2,1,0:T(8,128)(2,1)S(1)}, bf16[8,128,256]{2,1,0:T(8,128)(2,1)S(1)}, u32[]{:S(2)}, u32[]{:S(2)}) collective-permute-start(bf16[8,128,256]{2,1,0:T(8,128)(2,1)S(1)} %get-tuple-element.53), channel_id=1, source_target_pairs={{0,4},{4,0},{1,5},{5,1},{2,6},{6,2},{3,7},{7,3},{8,12},{12,8},{9,1... | collective-permute-start | bytes 1572872 | tf_op jit(solution)/shard_map/ppermute | solution.py:370
  65.9 14.7 %collective-permute-start.17 = (bf16[1024,128]{1,0:T(8,128)(2,1)S(1)}, bf16[1024,128]{1,0:T(8,128)(2,1)S(1)}, u32[]{:S(2)}, u32[]{:S(2)}) collective-permute-start(bf16[1024,128]{1,0:T(8,128)(2,1)S(1)} %middle.1.sum_ref), channel_id=1, source_target_pairs={{0,3},{1,0},{2,1},{3,2},{4,7},{5,4},{6,5},{7,6},{8,11},{9,8},{10,9... | collective-permute-start | bytes 786440 | tf_op jit(solution)/shard_map/ppermute | solution.py:362
  68.7 11.8 %collective-permute-start.16 = (bf16[1024,128]{1,0:T(8,128)(2,1)S(1)}, bf16[1024,128]{1,0:T(8,128)(2,1)S(1)}, u32[]{:S(2)}, u32[]{:S(2)}) collective-permute-start(bf16[1024,128]{1,0:T(8,128)(2,1)S(1)} %middle.1.sum_ref), channel_id=1, source_target_pairs={{0,2},{1,3},{2,0},{3,1},{4,6},{5,7},{6,4},{7,5},{8,10},{9,11},{10,... | collective-permute-start | bytes 786440 | tf_op jit(solution)/shard_map/ppermute | solution.py:362
  69.5 14.7 %collective-permute-start.15 = (bf16[1024,128]{1,0:T(8,128)(2,1)S(1)}, bf16[1024,128]{1,0:T(8,128)(2,1)S(1)}, u32[]{:S(2)}, u32[]{:S(2)}) collective-permute-start(bf16[1024,128]{1,0:T(8,128)(2,1)S(1)} %middle.1.sum_ref), channel_id=1, source_target_pairs={{0,1},{1,2},{2,3},{3,0},{4,5},{5,6},{6,7},{7,4},{8,9},{9,10},{10,1... | collective-permute-start | bytes 786440 | tf_op jit(solution)/shard_map/ppermute | solution.py:362
  70.5 4.3 %collective-permute-start.19 = (bf16[128,256]{1,0:T(8,128)(2,1)S(1)}, bf16[128,256]{1,0:T(8,128)(2,1)S(1)}, u32[]{:S(2)}, u32[]{:S(2)}) collective-permute-start(bf16[128,256]{1,0:T(8,128)(2,1)S(1)} %get-tuple-element.57), channel_id=1, source_target_pairs={{0,24},{8,0},{16,8},{24,16},{1,25},{9,1},{17,9},{25,17},{2,26},{10... | collective-permute-start | bytes 196616 | tf_op jit(solution)/shard_map/ppermute | solution.py:366
  71.7 5.5 %collective-permute-start.20 = (bf16[128,256]{1,0:T(8,128)(2,1)S(1)}, bf16[128,256]{1,0:T(8,128)(2,1)S(1)}, u32[]{:S(2)}, u32[]{:S(2)}) collective-permute-start(bf16[128,256]{1,0:T(8,128)(2,1)S(1)} %get-tuple-element.58), channel_id=1, source_target_pairs={{0,8},{8,16},{16,24},{24,0},{1,9},{9,17},{17,25},{25,1},{2,10},{10... | collective-permute-start | bytes 196616 | tf_op jit(solution)/shard_map/ppermute | solution.py:366
  77.3 7.0 %collective-permute-start.21 = (bf16[2,128,256]{2,1,0:T(8,128)(2,1)S(1)}, bf16[2,128,256]{2,1,0:T(8,128)(2,1)S(1)}, u32[]{:S(2)}, u32[]{:S(2)}) collective-permute-start(bf16[2,128,256]{2,1,0:T(8,128)(2,1)S(1)} %get-tuple-element.59), channel_id=1, source_target_pairs={{0,24},{8,0},{16,8},{24,16},{1,25},{9,1},{17,9},{25,17},{2,26},{10... | collective-permute-start | bytes 393224 | tf_op jit(solution)/shard_map/ppermute | solution.py:366
  77.3 6.9 %collective-permute-start.22 = (bf16[2,128,256]{2,1,0:T(8,128)(2,1)S(1)}, bf16[2,128,256]{2,1,0:T(8,128)(2,1)S(1)}, u32[]{:S(2)}, u32[]{:S(2)}) collective-permute-start(bf16[2,128,256]{2,1,0:T(8,128)(2,1)S(1)} %get-tuple-element.60), channel_id=1, source_target_pairs={{0,8},{8,16},{16,24},{24,0},{1,9},{9,17},{17,25},{25,1},{2,10},{10... | collective-permute-start | bytes 393224 | tf_op jit(solution)/shard_map/ppermute | solution.py:366
  (1 other events, 22.4 us)

commit v7 on v6

--- a/solution.py
+++ b/solution.py
@@ -13,6 +13,7 @@
 LOG2E = 1.4426950408889634
 SCALE2 = SCALE * LOG2E
 NEG = -1e30
+TINY = 1e-30
 NT = (((1,), (1,)), ((), ()))
 NN = (((1,), (0,)), ((), ()))
 F32 = jnp.float32
@@ -144,12 +145,12 @@
 
 
 def norm_and_delta(stat_refs, sum_ref, norm_ref, delta_ref):
-    found = [[ref[kind] for kind in range(3)] for ref in stat_refs]
-    top = functools.reduce(jnp.maximum, [f[0] for f in found])
-    factors = [jnp.exp2(f[0] - top) for f in found]
-    total = sum(f[1] * g for f, g in zip(found, factors))
+    found = [(ref[0], ref[1]) for ref in stat_refs]
+    top = functools.reduce(jnp.maximum, [norm for norm, _ in found])
+    factors = [jnp.exp2(norm - top) for norm, _ in found]
+    total = sum(factors)
     sum_ref[0] = top + jnp.log2(total)
-    sum_ref[1] = sum(f[2] * g for f, g in zip(found, factors)) / total
+    sum_ref[1] = sum(delta * g for (_, delta), g in zip(found, factors)) / total
     for slot in range(16):
         place = query_place(slot // 2) + slot % 2
         norm_ref[slot] = jnp.broadcast_to(sum_ref[0, pl.ds(place, 1), :], (8, SPAN))
@@ -390,6 +391,8 @@
     stats = call_stats(False, span_order, q_near, kvs)
     stats = call_stats(True, span_order, q_far, kvs, stats)
     stats = merged(stats, swap_core(stats))
+    total = jnp.maximum(stats[1], TINY)
+    stats = jnp.stack([stats[0] + jnp.log2(total), stats[2] / total])
     stats = [stats] + [back(stats, "y", k) for k in (1, 2, 3)]
 
     common = (span_order, stats, q_near, q_far, kvs)

time: 86.2 us -> 85.4 us (level)
    ppermute x12, waiting for transfers between devices: 21.8 us -> 20.7 us  [back(): return lax.ppermute(value, axis, [(i, (i + k) % 4) for i in range(4)])]
  transfers between devices with their start and end apart: 23 -> 23, of which waited for: 14 -> 13; matrix products, arithmetic and copies ran while one was open for 1% -> 1% of each run, Pallas kernels for 17% -> 17%
where the time goes in v7:
time: 85.4 us; the launch traced here: 84.3 us
  waiting for transfers between devices  30.3 us (35%)
  starting transfers between devices  27.1 us (32%)
  Pallas kernels  25 us (29%)
  local copies, waits for them, and re-layouts  1.17 us (1%)
    ppermute x12, waiting for transfers between devices, back(): return lax.ppermute(value, axis, [(i, (i + k) % 4) for i in range(4)])  20.7 us
    ppermute x12, starting transfers between devices, back(): return lax.ppermute(value, axis, [(i, (i + k) % 4) for i in range(4)])  17.9 us
    pallas_call x3, Pallas kernels, call_grads(): pl.pallas_call(functools.partial(grads_kernel, pieces, first, last), out_...  14.2 us
    ppermute x8, waiting for transfers between devices, ahead(): return lax.ppermute(value, axis, [(i, (i - k) % 4) for i in range(4)])  8.74 us
    ppermute x8, starting transfers between devices, ahead(): return lax.ppermute(value, axis, [(i, (i - k) % 4) for i in range(4)])  8.39 us
    pallas_call x2, Pallas kernels, call_stats(): pl.pallas_call(functools.partial(stats_kernel, far), out_shape=jax.ShapeD...  7.63 us
    pallas_call x1, Pallas kernels, call_pack(): pl.pallas_call(pack_kernel, out_shape=(jax.ShapeDtypeStruct((PIECE, DH),...  1.94 us
  transfers between devices with their start and end apart: 23, of which 13 were waited for; matrix products, arithmetic and copies ran while one was open for 1% of the time, Pallas kernels for 17%

profile of v7, /device:TPU:0, one launch (start us, length us, event | category | flops | bytes accessed | tf_op | source)
XLA Modules:
  0.0 84.3 jit_solution(15119871171876163645)
XLA Ops:
  0.6 1.9 %pack.1 = (bf16[1024,128]{1,0:T(8,128)(2,1)}, bf16[1024,128]{1,0:T(8,128)(2,1)}) custom-call(bf16[512,128]{1,0:T(8,128)(2,1)} %queries_ref.1, bf16[512,128]{1,0:T(8,128)(2,1)} %keys_ref.1, bf16[512,128]{1,0:T(8,128)(2,1)} %values_ref.1, bf16[512,128]{1,0:T(8,128)(2,1)} %grads_ref.1), custom_call_target="tpu_custom_call" | custom-call | tf_op jit(solution)/shard_map/pack/pallas_call | solution.py:351
  2.6 4.2 %collective-permute-start.4 = (bf16[1024,128]{1,0:T(8,128)(2,1)}, bf16[1024,128]{1,0:T(8,128)(2,1)S(1)}, u32[]{:S(2)}, u32[]{:S(2)}) collective-permute-start(bf16[1024,128]{1,0:T(8,128)(2,1)} %get-tuple-element.34.refs_0_.refs_7_), channel_id=1, source_target_pairs={{0,96},{32,0},{64,32},{96,64},{1,97},{33,1},{65,33},{97,65},{2,98}... | collective-permute-start | bytes 786440 | tf_op jit(solution)/shard_map/ppermute | solution.py:363
  6.8 3.0 %collective-permute-start.2 = (bf16[1024,128]{1,0:T(8,128)(2,1)}, bf16[1024,128]{1,0:T(8,128)(2,1)S(1)}, u32[]{:S(2)}, u32[]{:S(2)}) collective-permute-start(bf16[1024,128]{1,0:T(8,128)(2,1)} %get-tuple-element.32), channel_id=1, source_target_pairs={{0,24},{8,0},{16,8},{24,16},{1,25},{9,1},{17,9},{25,17},{2,26},{10... | collective-permute-start | bytes 786440 | tf_op jit(solution)/shard_map/ppermute | solution.py:363
  11.4 1.3 %collective-permute-done.4.refs_3_.refs_8_ = bf16[1024,128]{1,0:T(8,128)(2,1)S(1)} collective-permute-done((bf16[1024,128]{1,0:T(8,128)(2,1)}, bf16[1024,128]{1,0:T(8,128)(2,1)S(1)}, u32[]{:S(2)}, u32[]{:S(2)}) %collective-permute-start.4) | collective-permute-done | bytes 262176 | tf_op jit(solution)/shard_map/ppermute | solution.py:363
  12.7 3.3 %collective-permute-done.3.refs_1_.refs_7_ = bf16[1024,128]{1,0:T(8,128)(2,1)S(1)} collective-permute-done((bf16[1024,128]{1,0:T(8,128)(2,1)}, bf16[1024,128]{1,0:T(8,128)(2,1)S(1)}, u32[]{:S(2)}, u32[]{:S(2)}) %collective-permute-start.3) | collective-permute-done | bytes 262176 | tf_op jit(solution)/shard_map/ppermute | solution.py:363
  17.0 4.1 %collective-permute-done.2 = bf16[1024,128]{1,0:T(8,128)(2,1)S(1)} collective-permute-done((bf16[1024,128]{1,0:T(8,128)(2,1)}, bf16[1024,128]{1,0:T(8,128)(2,1)S(1)}, u32[]{:S(2)}, u32[]{:S(2)}) %collective-permute-start.2) | collective-permute-done | bytes 262176 | tf_op jit(solution)/shard_map/ppermute | solution.py:363
  21.0 3.6 %collective-permute-done = bf16[1024,128]{1,0:T(8,128)(2,1)S(1)} collective-permute-done((bf16[1024,128]{1,0:T(8,128)(2,1)}, bf16[1024,128]{1,0:T(8,128)(2,1)S(1)}, u32[]{:S(2)}, u32[]{:S(2)}) %collective-permute-start) | collective-permute-done | bytes 262176 | tf_op jit(solution)/shard_map/ppermute | solution.py:363
  25.0 3.8 %stats.2.refs_4_ = f32[3,16,256]{2,1,0:T(8,128)S(1)} custom-call(s32[32,2]{1,0:T(8,128)S(1)} %copy.12.order_ref.refs_0_, bf16[4,1024,128]{2,1,0:T(8,128)(2,1)S(1)} %bitcast.2, bf16[1024,128]{1,0:T(8,128)(2,1)S(1)} %copy-done, bf16[1024,128]{1,0:T(8,128)(2,1)S(1)} %collective-permute-done.3.refs_1_.refs_7_, ...), custom_call_target="tpu_custom_call" | custom-call | flops 1073741824 | bytes 2097152 | tf_op jit(solution)/shard_map/stats/pallas_call | solution.py:285
  28.8 3.8 %stats.3 = f32[3,16,256]{2,1,0:T(8,128)S(1)} custom-call(s32[32,2]{1,0:T(8,128)S(1)} %copy.12.order_ref.refs_0_, bf16[4,1024,128]{2,1,0:T(8,128)(2,1)S(1)} %bitcast.6, bf16[1024,128]{1,0:T(8,128)(2,1)S(1)} %copy-done, bf16[1024,128]{1,0:T(8,128)(2,1)S(1)} %collective-permute-done.3.refs_1_.refs_7_, ...), custom_call_target="tpu_custom_call" | custom-call | flops 1073741824 | bytes 2097152 | tf_op jit(solution)/shard_map/stats/pallas_call | solution.py:285
  34.1 3.0 %collective-permute-start.10 = (f32[2,16,256]{2,1,0:T(8,128)S(1)}, f32[2,16,256]{2,1,0:T(8,128)S(1)}, u32[]{:S(2)}, u32[]{:S(2)}) collective-permute-start(f32[2,16,256]{2,1,0:T(8,128)S(1)} %pad_maximum_fusion.refs_1_), channel_id=1, source_target_pairs={{0,24},{8,0},{16,8},{24,16},{1,25},{9,1},{17,9},{25,17},{2,26},{10... | collective-permute-start | bytes 98312 | tf_op jit(solution)/shard_map/ppermute | solution.py:363
  37.7 1.0 %collective-permute-start.8 = (f32[2,16,256]{2,1,0:T(8,128)S(1)}, f32[2,16,256]{2,1,0:T(8,128)S(1)}, u32[]{:S(2)}, u32[]{:S(2)}) collective-permute-start(f32[2,16,256]{2,1,0:T(8,128)S(1)} %pad_maximum_fusion.refs_1_), channel_id=1, source_target_pairs={{0,8},{8,16},{16,24},{24,0},{1,9},{9,17},{17,25},{25,1},{2,10},{10... | collective-permute-start | bytes 98312 | tf_op jit(solution)/shard_map/ppermute | solution.py:363
  38.7 3.8 %collective-permute-done.9.refs_3_ = f32[2,16,256]{2,1,0:T(8,128)S(1)} collective-permute-done((f32[2,16,256]{2,1,0:T(8,128)S(1)}, f32[2,16,256]{2,1,0:T(8,128)S(1)}, u32[]{:S(2)}, u32[]{:S(2)}) %collective-permute-start.9) | collective-permute-done | bytes 32800 | tf_op jit(solution)/shard_map/ppermute | solution.py:363
  42.9 3.7 %grads.3 = (bf16[512,128]{1,0:T(8,128)(2,1)S(1)}, bf16[512,128]{1,0:T(8,128)(2,1)S(1)}, f32[16,128,256]{2,1,0:T(8,128)S(1)}) custom-call(s32[32,2]{1,0:T(8,128)S(1)} %copy.12.order_ref.refs_0_, f32[2,16,256]{2,1,0:T(8,128)S(1)} %pad_maximum_fusion.refs_1_, f32[2,16,256]{2,1,0:T(8,128)S(1)} %collective-permute-done.8.refs_2_, ...), custom_call_target="tpu_custom_call" | custom-call | flops 1342177280 | bytes 4194304 | tf_op jit(solution)/shard_map/grads/pallas_call | solution.py:314
  47.5 1.2 %collective-permute-start.12 = (bf16[512,128]{1,0:T(8,128)(2,1)S(1)}, bf16[512,128]{1,0:T(8,128)(2,1)S(1)}, u32[]{:S(2)}, u32[]{:S(2)}) collective-permute-start(bf16[512,128]{1,0:T(8,128)(2,1)S(1)} %get-tuple-element.48), channel_id=1, source_target_pairs={{0,32},{32,64},{64,96},{96,0},{1,33},{33,65},{65,97},{97,1},{2,34}... | collective-permute-start | bytes 393224 | tf_op jit(solution)/shard_map/ppermute | solution.py:367
  48.7 6.2 %grads.4 = (f32[1024,128]{1,0:T(8,128)S(1)}, f32[1024,128]{1,0:T(8,128)S(1)}, f32[16,128,256]{2,1,0:T(8,128)S(1)}) custom-call(s32[32,2]{1,0:T(8,128)S(1)} %copy.12.order_ref.refs_0_, f32[2,16,256]{2,1,0:T(8,128)S(1)} %pad_maximum_fusion.refs_1_, f32[2,16,256]{2,1,0:T(8,128)S(1)} %collective-permute-done.8.refs_2_, ...), custom_call_target="tpu_custom_call" | custom-call | flops 2684354560 | bytes 4194304 | tf_op jit(solution)/shard_map/grads/pallas_call | solution.py:314
  54.9 2.1 %collective-permute-start.13 = (bf16[1024,128]{1,0:T(8,128)(2,1)S(1)}, bf16[1024,128]{1,0:T(8,128)(2,1)S(1)}, u32[]{:S(2)}, u32[]{:S(2)}) collective-permute-start(bf16[1024,128]{1,0:T(8,128)(2,1)S(1)} %get-tuple-element.49), channel_id=1, source_target_pairs={{0,96},{32,0},{64,32},{96,64},{1,97},{33,1},{65,33},{97,65},{2,98}... | collective-permute-start | bytes 786440 | tf_op jit(solution)/shard_map/ppermute | solution.py:367
  57.1 4.3 %grads.5 = (f32[1024,128]{1,0:T(8,128)S(1)}, f32[8,128,256]{2,1,0:T(8,128)S(1)}, bf16[8,128,256]{2,1,0:T(8,128)(2,1)S(1)}) custom-call(s32[32,2]{1,0:T(8,128)S(1)} %copy.12.order_ref.refs_0_, f32[2,16,256]{2,1,0:T(8,128)S(1)} %pad_maximum_fusion.refs_1_, f32[2,16,256]{2,1,0:T(8,128)S(1)} %collective-permute-done.8.refs_2_, ...), custom_call_target="tpu_custom_call" | custom-call | flops 1342177280 | bytes 4194304 | tf_op jit(solution)/shard_map/grads/pallas_call | solution.py:314
  61.6 3.3 %collective-permute-done.14.z3_ref = bf16[1024,128]{1,0:T(8,128)(2,1)S(1)} collective-permute-done((bf16[1024,128]{1,0:T(8,128)(2,1)S(1)}, bf16[1024,128]{1,0:T(8,128)(2,1)S(1)}, u32[]{:S(2)}, u32[]{:S(2)}) %collective-permute-start.14) | collective-permute-done | bytes 262176 | tf_op jit(solution)/shard_map/ppermute | solution.py:367
  65.0 2.8 %collective-permute-start.17 = (bf16[1024,128]{1,0:T(8,128)(2,1)S(1)}, bf16[1024,128]{1,0:T(8,128)(2,1)S(1)}, u32[]{:S(2)}, u32[]{:S(2)}) collective-permute-start(bf16[1024,128]{1,0:T(8,128)(2,1)S(1)} %middle.1.sum_ref), channel_id=1, source_target_pairs={{0,3},{1,0},{2,1},{3,2},{4,7},{5,4},{6,5},{7,6},{8,11},{9,8},{10,9... | collective-permute-start | bytes 786440 | tf_op jit(solution)/shard_map/ppermute | solution.py:363
  69.7 1.9 %collective-permute-start.19 = (bf16[128,256]{1,0:T(8,128)(2,1)S(1)}, bf16[128,256]{1,0:T(8,128)(2,1)S(1)}, u32[]{:S(2)}, u32[]{:S(2)}) collective-permute-start(bf16[128,256]{1,0:T(8,128)(2,1)S(1)} %get-tuple-element.57), channel_id=1, source_target_pairs={{0,24},{8,0},{16,8},{24,16},{1,25},{9,1},{17,9},{25,17},{2,26},{10... | collective-permute-start | bytes 196616 | tf_op jit(solution)/shard_map/ppermute | solution.py:367
  71.8 2.2 %collective-permute-done.19.first_ref = bf16[128,256]{1,0:T(8,128)(2,1)S(1)} collective-permute-done((bf16[128,256]{1,0:T(8,128)(2,1)S(1)}, bf16[128,256]{1,0:T(8,128)(2,1)S(1)}, u32[]{:S(2)}, u32[]{:S(2)}) %collective-permute-start.19) | collective-permute-done | bytes 65568 | tf_op jit(solution)/shard_map/ppermute | solution.py:367
  74.0 3.0 %collective-permute-done.20.second_ref = bf16[128,256]{1,0:T(8,128)(2,1)S(1)} collective-permute-done((bf16[128,256]{1,0:T(8,128)(2,1)S(1)}, bf16[128,256]{1,0:T(8,128)(2,1)S(1)}, u32[]{:S(2)}, u32[]{:S(2)}) %collective-permute-start.20) | collective-permute-done | bytes 65568 | tf_op jit(solution)/shard_map/ppermute | solution.py:367
  77.1 2.0 %collective-permute-start.22 = (bf16[2,128,256]{2,1,0:T(8,128)(2,1)S(1)}, bf16[2,128,256]{2,1,0:T(8,128)(2,1)S(1)}, u32[]{:S(2)}, u32[]{:S(2)}) collective-permute-start(bf16[2,128,256]{2,1,0:T(8,128)(2,1)S(1)} %get-tuple-element.60), channel_id=1, source_target_pairs={{0,8},{8,16},{16,24},{24,0},{1,9},{9,17},{17,25},{25,1},{2,10},{10... | collective-permute-start | bytes 393224 | tf_op jit(solution)/shard_map/ppermute | solution.py:367
  79.7 3.7 %collective-permute-done.15.x1_ref = bf16[1024,128]{1,0:T(8,128)(2,1)S(1)} collective-permute-done((bf16[1024,128]{1,0:T(8,128)(2,1)S(1)}, bf16[1024,128]{1,0:T(8,128)(2,1)S(1)}, u32[]{:S(2)}, u32[]{:S(2)}) %collective-permute-start.15) | collective-permute-done | bytes 262176 | tf_op jit(solution)/shard_map/ppermute | solution.py:363
  (44 shorter events, 10.3 us)
Async XLA Ops:
  0.6 24.2 %copy-start.1 = (s32[32,2]{0,1:T(2,128)S(1)}, s32[32,2]{0,1:T(2,128)}, u32[]{:S(2)}) copy-start(s32[32,2]{0,1:T(2,128)} %param.5) | copy-start | bytes 772
  2.6 10.1 %collective-permute-start.4 = (bf16[1024,128]{1,0:T(8,128)(2,1)}, bf16[1024,128]{1,0:T(8,128)(2,1)S(1)}, u32[]{:S(2)}, u32[]{:S(2)}) collective-permute-start(bf16[1024,128]{1,0:T(8,128)(2,1)} %get-tuple-element.34.refs_0_.refs_7_), channel_id=1, source_target_pairs={{0,96},{32,0},{64,32},{96,64},{1,97},{33,1},{65,33},{97,65},{2,98}... | collective-permute-start | bytes 786440 | tf_op jit(solution)/shard_map/ppermute | solution.py:363
  6.8 9.2 %collective-permute-start.3 = (bf16[1024,128]{1,0:T(8,128)(2,1)}, bf16[1024,128]{1,0:T(8,128)(2,1)S(1)}, u32[]{:S(2)}, u32[]{:S(2)}) collective-permute-start(bf16[1024,128]{1,0:T(8,128)(2,1)} %get-tuple-element.34.refs_0_.refs_7_), channel_id=1, source_target_pairs={{0,32},{32,64},{64,96},{96,0},{1,33},{33,65},{65,97},{97,1},{2,34}... | collective-permute-start | bytes 786440 | tf_op jit(solution)/shard_map/ppermute | solution.py:363
  6.8 14.2 %collective-permute-start.2 = (bf16[1024,128]{1,0:T(8,128)(2,1)}, bf16[1024,128]{1,0:T(8,128)(2,1)S(1)}, u32[]{:S(2)}, u32[]{:S(2)}) collective-permute-start(bf16[1024,128]{1,0:T(8,128)(2,1)} %get-tuple-element.32), channel_id=1, source_target_pairs={{0,24},{8,0},{16,8},{24,16},{1,25},{9,1},{17,9},{25,17},{2,26},{10... | collective-permute-start | bytes 786440 | tf_op jit(solution)/shard_map/ppermute | solution.py:363
  9.8 11.2 %collective-permute-start.1 = (bf16[1024,128]{1,0:T(8,128)(2,1)}, bf16[1024,128]{1,0:T(8,128)(2,1)S(1)}, u32[]{:S(2)}, u32[]{:S(2)}) collective-permute-start(bf16[1024,128]{1,0:T(8,128)(2,1)} %get-tuple-element.32), channel_id=1, source_target_pairs={{0,16},{8,24},{16,0},{24,8},{1,17},{9,25},{17,1},{25,9},{2,18},{10... | collective-permute-start | bytes 786440 | tf_op jit(solution)/shard_map/ppermute | solution.py:363
  10.4 14.2 %collective-permute-start = (bf16[1024,128]{1,0:T(8,128)(2,1)}, bf16[1024,128]{1,0:T(8,128)(2,1)S(1)}, u32[]{:S(2)}, u32[]{:S(2)}) collective-permute-start(bf16[1024,128]{1,0:T(8,128)(2,1)} %get-tuple-element.32), channel_id=1, source_target_pairs={{0,8},{8,16},{16,24},{24,0},{1,9},{9,17},{17,25},{25,1},{2,10},{10... | collective-permute-start | bytes 786440 | tf_op jit(solution)/shard_map/ppermute | solution.py:363
  16.0 8.7 %collective-permute-start.5 = (bf16[1024,128]{1,0:T(8,128)(2,1)}, bf16[1024,128]{1,0:T(8,128)(2,1)S(1)}, u32[]{:S(2)}, u32[]{:S(2)}) collective-permute-start(bf16[1024,128]{1,0:T(8,128)(2,1)} %get-tuple-element.34.refs_0_.refs_7_), channel_id=1, source_target_pairs={{0,64},{32,96},{64,0},{96,32},{1,65},{33,97},{65,1},{97,33},{2,66}... | collective-permute-start | bytes 786440 | tf_op jit(solution)/shard_map/ppermute | solution.py:363
  24.8 4.0 %collective-permute-start.6 = (bf16[4096,128]{1,0:T(8,128)(2,1)S(1)}, bf16[4096,128]{1,0:T(8,128)(2,1)S(1)}, u32[]{:S(2)}, u32[]{:S(2)}) collective-permute-start(bf16[4096,128]{1,0:T(8,128)(2,1)S(1)} %constant_dynamic-update-slice_fusion), channel_id=1, source_target_pairs={{0,4},{4,0},{1,5},{5,1},{2,6},{6,2},{3,7},{7,3},{8,12},{12,8},{9,1... | collective-permute-start | bytes 3145736 | tf_op jit(solution)/shard_map/ppermute | solution.py:371
  32.6 1.4 %collective-permute-start.7 = (f32[3,16,256]{2,1,0:T(8,128)S(1)}, f32[3,16,256]{2,1,0:T(8,128)S(1)}, u32[]{:S(2)}, u32[]{:S(2)}) collective-permute-start(f32[3,16,256]{2,1,0:T(8,128)S(1)} %stats.3), channel_id=1, source_target_pairs={{0,4},{4,0},{1,5},{5,1},{2,6},{6,2},{3,7},{7,3},{8,12},{12,8},{9,1... | collective-permute-start | bytes 147464 | tf_op jit(solution)/shard_map/ppermute | solution.py:371
  34.1 4.6 %collective-permute-start.10 = (f32[2,16,256]{2,1,0:T(8,128)S(1)}, f32[2,16,256]{2,1,0:T(8,128)S(1)}, u32[]{:S(2)}, u32[]{:S(2)}) collective-permute-start(f32[2,16,256]{2,1,0:T(8,128)S(1)} %pad_maximum_fusion.refs_1_), channel_id=1, source_target_pairs={{0,24},{8,0},{16,8},{24,16},{1,25},{9,1},{17,9},{25,17},{2,26},{10... | collective-permute-start | bytes 98312 | tf_op jit(solution)/shard_map/ppermute | solution.py:363
  37.1 5.4 %collective-permute-start.9 = (f32[2,16,256]{2,1,0:T(8,128)S(1)}, f32[2,16,256]{2,1,0:T(8,128)S(1)}, u32[]{:S(2)}, u32[]{:S(2)}) collective-permute-start(f32[2,16,256]{2,1,0:T(8,128)S(1)} %pad_maximum_fusion.refs_1_), channel_id=1, source_target_pairs={{0,16},{8,24},{16,0},{24,8},{1,17},{9,25},{17,1},{25,9},{2,18},{10... | collective-permute-start | bytes 98312 | tf_op jit(solution)/shard_map/ppermute | solution.py:363
  37.7 5.1 %collective-permute-start.8 = (f32[2,16,256]{2,1,0:T(8,128)S(1)}, f32[2,16,256]{2,1,0:T(8,128)S(1)}, u32[]{:S(2)}, u32[]{:S(2)}) collective-permute-start(f32[2,16,256]{2,1,0:T(8,128)S(1)} %pad_maximum_fusion.refs_1_), channel_id=1, source_target_pairs={{0,8},{8,16},{16,24},{24,0},{1,9},{9,17},{17,25},{25,1},{2,10},{10... | collective-permute-start | bytes 98312 | tf_op jit(solution)/shard_map/ppermute | solution.py:363
  46.6 8.3 %collective-permute-start.11 = (bf16[512,128]{1,0:T(8,128)(2,1)S(1)}, bf16[512,128]{1,0:T(8,128)(2,1)S(1)}, u32[]{:S(2)}, u32[]{:S(2)}) collective-permute-start(bf16[512,128]{1,0:T(8,128)(2,1)S(1)} %get-tuple-element.47), channel_id=1, source_target_pairs={{0,96},{32,0},{64,32},{96,64},{1,97},{33,1},{65,33},{97,65},{2,98}... | collective-permute-start | bytes 393224 | tf_op jit(solution)/shard_map/ppermute | solution.py:367
  47.5 7.4 %collective-permute-start.12 = (bf16[512,128]{1,0:T(8,128)(2,1)S(1)}, bf16[512,128]{1,0:T(8,128)(2,1)S(1)}, u32[]{:S(2)}, u32[]{:S(2)}) collective-permute-start(bf16[512,128]{1,0:T(8,128)(2,1)S(1)} %get-tuple-element.48), channel_id=1, source_target_pairs={{0,32},{32,64},{64,96},{96,0},{1,33},{33,65},{65,97},{97,1},{2,34}... | collective-permute-start | bytes 393224 | tf_op jit(solution)/shard_map/ppermute | solution.py:367
  54.9 6.6 %collective-permute-start.13 = (bf16[1024,128]{1,0:T(8,128)(2,1)S(1)}, bf16[1024,128]{1,0:T(8,128)(2,1)S(1)}, u32[]{:S(2)}, u32[]{:S(2)}) collective-permute-start(bf16[1024,128]{1,0:T(8,128)(2,1)S(1)} %get-tuple-element.49), channel_id=1, source_target_pairs={{0,96},{32,0},{64,32},{96,64},{1,97},{33,1},{65,33},{97,65},{2,98}... | collective-permute-start | bytes 786440 | tf_op jit(solution)/shard_map/ppermute | solution.py:367
  57.1 7.8 %collective-permute-start.14 = (bf16[1024,128]{1,0:T(8,128)(2,1)S(1)}, bf16[1024,128]{1,0:T(8,128)(2,1)S(1)}, u32[]{:S(2)}, u32[]{:S(2)}) collective-permute-start(bf16[1024,128]{1,0:T(8,128)(2,1)S(1)} %get-tuple-element.50), channel_id=1, source_target_pairs={{0,32},{32,64},{64,96},{96,0},{1,33},{33,65},{65,97},{97,1},{2,34}... | collective-permute-start | bytes 786440 | tf_op jit(solution)/shard_map/ppermute | solution.py:367
  65.0 4.6 %collective-permute-start.18 = (bf16[8,128,256]{2,1,0:T(8,128)(2,1)S(1)}, bf16[8,128,256]{2,1,0:T(8,128)(2,1)S(1)}, u32[]{:S(2)}, u32[]{:S(2)}) collective-permute-start(bf16[8,128,256]{2,1,0:T(8,128)(2,1)S(1)} %get-tuple-element.53), channel_id=1, source_target_pairs={{0,4},{4,0},{1,5},{5,1},{2,6},{6,2},{3,7},{7,3},{8,12},{12,8},{9,1... | collective-permute-start | bytes 1572872 | tf_op jit(solution)/shard_map/ppermute | solution.py:371
  65.0 14.7 %collective-permute-start.17 = (bf16[1024,128]{1,0:T(8,128)(2,1)S(1)}, bf16[1024,128]{1,0:T(8,128)(2,1)S(1)}, u32[]{:S(2)}, u32[]{:S(2)}) collective-permute-start(bf16[1024,128]{1,0:T(8,128)(2,1)S(1)} %middle.1.sum_ref), channel_id=1, source_target_pairs={{0,3},{1,0},{2,1},{3,2},{4,7},{5,4},{6,5},{7,6},{8,11},{9,8},{10,9... | collective-permute-start | bytes 786440 | tf_op jit(solution)/shard_map/ppermute | solution.py:363
  67.9 11.8 %collective-permute-start.16 = (bf16[1024,128]{1,0:T(8,128)(2,1)S(1)}, bf16[1024,128]{1,0:T(8,128)(2,1)S(1)}, u32[]{:S(2)}, u32[]{:S(2)}) collective-permute-start(bf16[1024,128]{1,0:T(8,128)(2,1)S(1)} %middle.1.sum_ref), channel_id=1, source_target_pairs={{0,2},{1,3},{2,0},{3,1},{4,6},{5,7},{6,4},{7,5},{8,10},{9,11},{10,... | collective-permute-start | bytes 786440 | tf_op jit(solution)/shard_map/ppermute | solution.py:363
  68.7 14.7 %collective-permute-start.15 = (bf16[1024,128]{1,0:T(8,128)(2,1)S(1)}, bf16[1024,128]{1,0:T(8,128)(2,1)S(1)}, u32[]{:S(2)}, u32[]{:S(2)}) collective-permute-start(bf16[1024,128]{1,0:T(8,128)(2,1)S(1)} %middle.1.sum_ref), channel_id=1, source_target_pairs={{0,1},{1,2},{2,3},{3,0},{4,5},{5,6},{6,7},{7,4},{8,9},{9,10},{10,1... | collective-permute-start | bytes 786440 | tf_op jit(solution)/shard_map/ppermute | solution.py:363
  69.7 4.3 %collective-permute-start.19 = (bf16[128,256]{1,0:T(8,128)(2,1)S(1)}, bf16[128,256]{1,0:T(8,128)(2,1)S(1)}, u32[]{:S(2)}, u32[]{:S(2)}) collective-permute-start(bf16[128,256]{1,0:T(8,128)(2,1)S(1)} %get-tuple-element.57), channel_id=1, source_target_pairs={{0,24},{8,0},{16,8},{24,16},{1,25},{9,1},{17,9},{25,17},{2,26},{10... | collective-permute-start | bytes 196616 | tf_op jit(solution)/shard_map/ppermute | solution.py:367
  71.5 5.5 %collective-permute-start.20 = (bf16[128,256]{1,0:T(8,128)(2,1)S(1)}, bf16[128,256]{1,0:T(8,128)(2,1)S(1)}, u32[]{:S(2)}, u32[]{:S(2)}) collective-permute-start(bf16[128,256]{1,0:T(8,128)(2,1)S(1)} %get-tuple-element.58), channel_id=1, source_target_pairs={{0,8},{8,16},{16,24},{24,0},{1,9},{9,17},{17,25},{25,1},{2,10},{10... | collective-permute-start | bytes 196616 | tf_op jit(solution)/shard_map/ppermute | solution.py:367
  77.0 6.3 %collective-permute-start.21 = (bf16[2,128,256]{2,1,0:T(8,128)(2,1)S(1)}, bf16[2,128,256]{2,1,0:T(8,128)(2,1)S(1)}, u32[]{:S(2)}, u32[]{:S(2)}) collective-permute-start(bf16[2,128,256]{2,1,0:T(8,128)(2,1)S(1)} %get-tuple-element.59), channel_id=1, source_target_pairs={{0,24},{8,0},{16,8},{24,16},{1,25},{9,1},{17,9},{25,17},{2,26},{10... | collective-permute-start | bytes 393224 | tf_op jit(solution)/shard_map/ppermute | solution.py:367
  77.1 6.3 %collective-permute-start.22 = (bf16[2,128,256]{2,1,0:T(8,128)(2,1)S(1)}, bf16[2,128,256]{2,1,0:T(8,128)(2,1)S(1)}, u32[]{:S(2)}, u32[]{:S(2)}) collective-permute-start(bf16[2,128,256]{2,1,0:T(8,128)(2,1)S(1)} %get-tuple-element.60), channel_id=1, source_target_pairs={{0,8},{8,16},{16,24},{24,0},{1,9},{9,17},{17,25},{25,1},{2,10},{10... | collective-permute-start | bytes 393224 | tf_op jit(solution)/shard_map/ppermute | solution.py:367
  (1 other events, 22.4 us)

commit v8 on v7

--- a/solution.py
+++ b/solution.py
@@ -134,11 +134,9 @@
         tops = top_ref[slot]
         top = jnp.max(tops, axis=0, keepdims=True)
         factor = jnp.exp2(tops - top)
-        rows = (
-            top,
-            jnp.sum(total_ref[slot] * factor, axis=0, keepdims=True),
-            jnp.sum(weighted_ref[slot] * factor, axis=0, keepdims=True),
-        )
+        total = jnp.maximum(jnp.sum(total_ref[slot] * factor, axis=0, keepdims=True), TINY)
+        weighted = jnp.sum(weighted_ref[slot] * factor, axis=0, keepdims=True)
+        rows = (top + jnp.log2(total), weighted / total)
         place = query_place(base + slot // 2) + slot % 2
         for kind, row in enumerate(rows):
             out_ref[kind, pl.ds(place, 1), :] = row
@@ -284,7 +282,7 @@
     args = [span_order, q_pieces.reshape(4, PIECE, DH), *kvs, *before]
     return pl.pallas_call(
         functools.partial(stats_kernel, far),
-        out_shape=jax.ShapeDtypeStruct((3, 16, SPAN), F32),
+        out_shape=jax.ShapeDtypeStruct((2, 16, SPAN), F32),
         in_specs=[SMEM] + [VMEM] * (len(args) - 1),
         out_specs=VMEM,
         scratch_shapes=[pltpu.VMEM((4, PIECE, DH), BF16)] + [pltpu.VMEM((8, 8, SPAN), F32)] * 3,
@@ -374,7 +372,8 @@
 def merged(mine, theirs):
     top = jnp.maximum(mine[0], theirs[0])
     mine_by, theirs_by = jnp.exp2(mine[0] - top), jnp.exp2(theirs[0] - top)
-    return jnp.stack([top, mine[1] * mine_by + theirs[1] * theirs_by, mine[2] * mine_by + theirs[2] * theirs_by])
+    total = mine_by + theirs_by
+    return jnp.stack([top + jnp.log2(total), (mine[1] * mine_by + theirs[1] * theirs_by) / total])
 
 
 def local(span_order, queries, key_rows, value_rows, out_grads):
@@ -391,8 +390,6 @@
     stats = call_stats(False, span_order, q_near, kvs)
     stats = call_stats(True, span_order, q_far, kvs, stats)
     stats = merged(stats, swap_core(stats))
-    total = jnp.maximum(stats[1], TINY)
-    stats = jnp.stack([stats[0] + jnp.log2(total), stats[2] / total])
     stats = [stats] + [back(stats, "y", k) for k in (1, 2, 3)]
 
     common = (span_order, stats, q_near, q_far, kvs)

time: 85.4 us -> 85.5 us (level)
  no operation moved by 1% of the time
where the time goes in v8:
time: 85.5 us; the launch traced here: 84.4 us
  waiting for transfers between devices  30.3 us (35%)
  starting transfers between devices  27.1 us (32%)
  Pallas kernels  25.1 us (29%)
  local copies, waits for them, and re-layouts  1.17 us (1%)
    ppermute x12, waiting for transfers between devices, back(): return lax.ppermute(value, axis, [(i, (i + k) % 4) for i in range(4)])  20.6 us
    ppermute x12, starting transfers between devices, back(): return lax.ppermute(value, axis, [(i, (i + k) % 4) for i in range(4)])  17.9 us
    pallas_call x3, Pallas kernels, call_grads(): pl.pallas_call(functools.partial(grads_kernel, pieces, first, last), out_...  14.2 us
    ppermute x8, waiting for transfers between devices, ahead(): return lax.ppermute(value, axis, [(i, (i - k) % 4) for i in range(4)])  8.77 us
    ppermute x8, starting transfers between devices, ahead(): return lax.ppermute(value, axis, [(i, (i - k) % 4) for i in range(4)])  8.4 us
    pallas_call x2, Pallas kernels, call_stats(): pl.pallas_call(functools.partial(stats_kernel, far), out_shape=jax.ShapeD...  7.75 us
    pallas_call x1, Pallas kernels, call_pack(): pl.pallas_call(pack_kernel, out_shape=(jax.ShapeDtypeStruct((PIECE, DH),...  1.94 us
  transfers between devices with their start and end apart: 23, of which 13 were waited for; matrix products, arithmetic and copies ran while one was open for 1% of the time, Pallas kernels for 17%

profile of v8, /device:TPU:0, one launch (start us, length us, event | category | flops | bytes accessed | tf_op | source)
XLA Modules:
  0.0 84.4 jit_solution(1600505565667927909)
XLA Ops:
  0.6 1.9 %pack.1 = (bf16[1024,128]{1,0:T(8,128)(2,1)}, bf16[1024,128]{1,0:T(8,128)(2,1)}) custom-call(bf16[512,128]{1,0:T(8,128)(2,1)} %queries_ref.1, bf16[512,128]{1,0:T(8,128)(2,1)} %keys_ref.1, bf16[512,128]{1,0:T(8,128)(2,1)} %values_ref.1, bf16[512,128]{1,0:T(8,128)(2,1)} %grads_ref.1), custom_call_target="tpu_custom_call" | custom-call | tf_op jit(solution)/shard_map/pack/pallas_call | solution.py:349
  2.6 4.2 %collective-permute-start.4 = (bf16[1024,128]{1,0:T(8,128)(2,1)}, bf16[1024,128]{1,0:T(8,128)(2,1)S(1)}, u32[]{:S(2)}, u32[]{:S(2)}) collective-permute-start(bf16[1024,128]{1,0:T(8,128)(2,1)} %get-tuple-element.34.refs_0_.refs_7_), channel_id=1, source_target_pairs={{0,96},{32,0},{64,32},{96,64},{1,97},{33,1},{65,33},{97,65},{2,98}... | collective-permute-start | bytes 786440 | tf_op jit(solution)/shard_map/ppermute | solution.py:361
  6.8 3.0 %collective-permute-start.2 = (bf16[1024,128]{1,0:T(8,128)(2,1)}, bf16[1024,128]{1,0:T(8,128)(2,1)S(1)}, u32[]{:S(2)}, u32[]{:S(2)}) collective-permute-start(bf16[1024,128]{1,0:T(8,128)(2,1)} %get-tuple-element.32), channel_id=1, source_target_pairs={{0,24},{8,0},{16,8},{24,16},{1,25},{9,1},{17,9},{25,17},{2,26},{10... | collective-permute-start | bytes 786440 | tf_op jit(solution)/shard_map/ppermute | solution.py:361
  10.4 1.0 %collective-permute-start = (bf16[1024,128]{1,0:T(8,128)(2,1)}, bf16[1024,128]{1,0:T(8,128)(2,1)S(1)}, u32[]{:S(2)}, u32[]{:S(2)}) collective-permute-start(bf16[1024,128]{1,0:T(8,128)(2,1)} %get-tuple-element.32), channel_id=1, source_target_pairs={{0,8},{8,16},{16,24},{24,0},{1,9},{9,17},{17,25},{25,1},{2,10},{10... | collective-permute-start | bytes 786440 | tf_op jit(solution)/shard_map/ppermute | solution.py:361
  11.4 1.3 %collective-permute-done.4.refs_3_.refs_8_ = bf16[1024,128]{1,0:T(8,128)(2,1)S(1)} collective-permute-done((bf16[1024,128]{1,0:T(8,128)(2,1)}, bf16[1024,128]{1,0:T(8,128)(2,1)S(1)}, u32[]{:S(2)}, u32[]{:S(2)}) %collective-permute-start.4) | collective-permute-done | bytes 262176 | tf_op jit(solution)/shard_map/ppermute | solution.py:361
  12.7 3.3 %collective-permute-done.3.refs_1_.refs_7_ = bf16[1024,128]{1,0:T(8,128)(2,1)S(1)} collective-permute-done((bf16[1024,128]{1,0:T(8,128)(2,1)}, bf16[1024,128]{1,0:T(8,128)(2,1)S(1)}, u32[]{:S(2)}, u32[]{:S(2)}) %collective-permute-start.3) | collective-permute-done | bytes 262176 | tf_op jit(solution)/shard_map/ppermute | solution.py:361
  17.0 4.1 %collective-permute-done.2 = bf16[1024,128]{1,0:T(8,128)(2,1)S(1)} collective-permute-done((bf16[1024,128]{1,0:T(8,128)(2,1)}, bf16[1024,128]{1,0:T(8,128)(2,1)S(1)}, u32[]{:S(2)}, u32[]{:S(2)}) %collective-permute-start.2) | collective-permute-done | bytes 262176 | tf_op jit(solution)/shard_map/ppermute | solution.py:361
  21.0 3.6 %collective-permute-done = bf16[1024,128]{1,0:T(8,128)(2,1)S(1)} collective-permute-done((bf16[1024,128]{1,0:T(8,128)(2,1)}, bf16[1024,128]{1,0:T(8,128)(2,1)S(1)}, u32[]{:S(2)}, u32[]{:S(2)}) %collective-permute-start) | collective-permute-done | bytes 262176 | tf_op jit(solution)/shard_map/ppermute | solution.py:361
  25.0 3.9 %stats.2.refs_4_ = f32[2,16,256]{2,1,0:T(8,128)S(1)} custom-call(s32[32,2]{1,0:T(8,128)S(1)} %copy.12.order_ref.refs_0_, bf16[4,1024,128]{2,1,0:T(8,128)(2,1)S(1)} %bitcast.2, bf16[1024,128]{1,0:T(8,128)(2,1)S(1)} %copy-done, bf16[1024,128]{1,0:T(8,128)(2,1)S(1)} %collective-permute-done.3.refs_1_.refs_7_, ...), custom_call_target="tpu_custom_call" | custom-call | flops 1073741824 | bytes 2097152 | tf_op jit(solution)/shard_map/stats/pallas_call | solution.py:283
  28.9 3.8 %stats.3 = f32[2,16,256]{2,1,0:T(8,128)S(1)} custom-call(s32[32,2]{1,0:T(8,128)S(1)} %copy.12.order_ref.refs_0_, bf16[4,1024,128]{2,1,0:T(8,128)(2,1)S(1)} %bitcast.6, bf16[1024,128]{1,0:T(8,128)(2,1)S(1)} %copy-done, bf16[1024,128]{1,0:T(8,128)(2,1)S(1)} %collective-permute-done.3.refs_1_.refs_7_, ...), custom_call_target="tpu_custom_call" | custom-call | flops 1073741824 | bytes 2097152 | tf_op jit(solution)/shard_map/stats/pallas_call | solution.py:283
  34.2 3.0 %collective-permute-start.10 = (f32[2,16,256]{2,1,0:T(8,128)S(1)}, f32[2,16,256]{2,1,0:T(8,128)S(1)}, u32[]{:S(2)}, u32[]{:S(2)}) collective-permute-start(f32[2,16,256]{2,1,0:T(8,128)S(1)} %pad_maximum_fusion.refs_1_), channel_id=1, source_target_pairs={{0,24},{8,0},{16,8},{24,16},{1,25},{9,1},{17,9},{25,17},{2,26},{10... | collective-permute-start | bytes 98312 | tf_op jit(solution)/shard_map/ppermute | solution.py:361
  38.8 3.8 %collective-permute-done.9.refs_3_ = f32[2,16,256]{2,1,0:T(8,128)S(1)} collective-permute-done((f32[2,16,256]{2,1,0:T(8,128)S(1)}, f32[2,16,256]{2,1,0:T(8,128)S(1)}, u32[]{:S(2)}, u32[]{:S(2)}) %collective-permute-start.9) | collective-permute-done | bytes 32800 | tf_op jit(solution)/shard_map/ppermute | solution.py:361
  43.0 3.7 %grads.3 = (bf16[512,128]{1,0:T(8,128)(2,1)S(1)}, bf16[512,128]{1,0:T(8,128)(2,1)S(1)}, f32[16,128,256]{2,1,0:T(8,128)S(1)}) custom-call(s32[32,2]{1,0:T(8,128)S(1)} %copy.12.order_ref.refs_0_, f32[2,16,256]{2,1,0:T(8,128)S(1)} %pad_maximum_fusion.refs_1_, f32[2,16,256]{2,1,0:T(8,128)S(1)} %collective-permute-done.8.refs_2_, ...), custom_call_target="tpu_custom_call" | custom-call | flops 1342177280 | bytes 4194304 | tf_op jit(solution)/shard_map/grads/pallas_call | solution.py:312
  47.6 1.2 %collective-permute-start.12 = (bf16[512,128]{1,0:T(8,128)(2,1)S(1)}, bf16[512,128]{1,0:T(8,128)(2,1)S(1)}, u32[]{:S(2)}, u32[]{:S(2)}) collective-permute-start(bf16[512,128]{1,0:T(8,128)(2,1)S(1)} %get-tuple-element.48), channel_id=1, source_target_pairs={{0,32},{32,64},{64,96},{96,0},{1,33},{33,65},{65,97},{97,1},{2,34}... | collective-permute-start | bytes 393224 | tf_op jit(solution)/shard_map/ppermute | solution.py:365
  48.8 6.2 %grads.4 = (f32[1024,128]{1,0:T(8,128)S(1)}, f32[1024,128]{1,0:T(8,128)S(1)}, f32[16,128,256]{2,1,0:T(8,128)S(1)}) custom-call(s32[32,2]{1,0:T(8,128)S(1)} %copy.12.order_ref.refs_0_, f32[2,16,256]{2,1,0:T(8,128)S(1)} %pad_maximum_fusion.refs_1_, f32[2,16,256]{2,1,0:T(8,128)S(1)} %collective-permute-done.8.refs_2_, ...), custom_call_target="tpu_custom_call" | custom-call | flops 2684354560 | bytes 4194304 | tf_op jit(solution)/shard_map/grads/pallas_call | solution.py:312
  55.0 2.1 %collective-permute-start.13 = (bf16[1024,128]{1,0:T(8,128)(2,1)S(1)}, bf16[1024,128]{1,0:T(8,128)(2,1)S(1)}, u32[]{:S(2)}, u32[]{:S(2)}) collective-permute-start(bf16[1024,128]{1,0:T(8,128)(2,1)S(1)} %get-tuple-element.49), channel_id=1, source_target_pairs={{0,96},{32,0},{64,32},{96,64},{1,97},{33,1},{65,33},{97,65},{2,98}... | collective-permute-start | bytes 786440 | tf_op jit(solution)/shard_map/ppermute | solution.py:365
  57.2 4.3 %grads.5 = (f32[1024,128]{1,0:T(8,128)S(1)}, f32[8,128,256]{2,1,0:T(8,128)S(1)}, bf16[8,128,256]{2,1,0:T(8,128)(2,1)S(1)}) custom-call(s32[32,2]{1,0:T(8,128)S(1)} %copy.12.order_ref.refs_0_, f32[2,16,256]{2,1,0:T(8,128)S(1)} %pad_maximum_fusion.refs_1_, f32[2,16,256]{2,1,0:T(8,128)S(1)} %collective-permute-done.8.refs_2_, ...), custom_call_target="tpu_custom_call" | custom-call | flops 1342177280 | bytes 4194304 | tf_op jit(solution)/shard_map/grads/pallas_call | solution.py:312
  61.7 3.3 %collective-permute-done.14.z3_ref = bf16[1024,128]{1,0:T(8,128)(2,1)S(1)} collective-permute-done((bf16[1024,128]{1,0:T(8,128)(2,1)S(1)}, bf16[1024,128]{1,0:T(8,128)(2,1)S(1)}, u32[]{:S(2)}, u32[]{:S(2)}) %collective-permute-start.14) | collective-permute-done | bytes 262176 | tf_op jit(solution)/shard_map/ppermute | solution.py:365
  65.1 2.8 %collective-permute-start.17 = (bf16[1024,128]{1,0:T(8,128)(2,1)S(1)}, bf16[1024,128]{1,0:T(8,128)(2,1)S(1)}, u32[]{:S(2)}, u32[]{:S(2)}) collective-permute-start(bf16[1024,128]{1,0:T(8,128)(2,1)S(1)} %middle.1.sum_ref), channel_id=1, source_target_pairs={{0,3},{1,0},{2,1},{3,2},{4,7},{5,4},{6,5},{7,6},{8,11},{9,8},{10,9... | collective-permute-start | bytes 786440 | tf_op jit(solution)/shard_map/ppermute | solution.py:361
  69.8 1.9 %collective-permute-start.19 = (bf16[128,256]{1,0:T(8,128)(2,1)S(1)}, bf16[128,256]{1,0:T(8,128)(2,1)S(1)}, u32[]{:S(2)}, u32[]{:S(2)}) collective-permute-start(bf16[128,256]{1,0:T(8,128)(2,1)S(1)} %get-tuple-element.57), channel_id=1, source_target_pairs={{0,24},{8,0},{16,8},{24,16},{1,25},{9,1},{17,9},{25,17},{2,26},{10... | collective-permute-start | bytes 196616 | tf_op jit(solution)/shard_map/ppermute | solution.py:365
  71.8 2.2 %collective-permute-done.19.first_ref = bf16[128,256]{1,0:T(8,128)(2,1)S(1)} collective-permute-done((bf16[128,256]{1,0:T(8,128)(2,1)S(1)}, bf16[128,256]{1,0:T(8,128)(2,1)S(1)}, u32[]{:S(2)}, u32[]{:S(2)}) %collective-permute-start.19) | collective-permute-done | bytes 65568 | tf_op jit(solution)/shard_map/ppermute | solution.py:365
  74.1 3.0 %collective-permute-done.20.second_ref = bf16[128,256]{1,0:T(8,128)(2,1)S(1)} collective-permute-done((bf16[128,256]{1,0:T(8,128)(2,1)S(1)}, bf16[128,256]{1,0:T(8,128)(2,1)S(1)}, u32[]{:S(2)}, u32[]{:S(2)}) %collective-permute-start.20) | collective-permute-done | bytes 65568 | tf_op jit(solution)/shard_map/ppermute | solution.py:365
  77.2 2.0 %collective-permute-start.22 = (bf16[2,128,256]{2,1,0:T(8,128)(2,1)S(1)}, bf16[2,128,256]{2,1,0:T(8,128)(2,1)S(1)}, u32[]{:S(2)}, u32[]{:S(2)}) collective-permute-start(bf16[2,128,256]{2,1,0:T(8,128)(2,1)S(1)} %get-tuple-element.60), channel_id=1, source_target_pairs={{0,8},{8,16},{16,24},{24,0},{1,9},{9,17},{17,25},{25,1},{2,10},{10... | collective-permute-start | bytes 393224 | tf_op jit(solution)/shard_map/ppermute | solution.py:365
  79.8 3.7 %collective-permute-done.15.x1_ref = bf16[1024,128]{1,0:T(8,128)(2,1)S(1)} collective-permute-done((bf16[1024,128]{1,0:T(8,128)(2,1)S(1)}, bf16[1024,128]{1,0:T(8,128)(2,1)S(1)}, u32[]{:S(2)}, u32[]{:S(2)}) %collective-permute-start.15) | collective-permute-done | bytes 262176 | tf_op jit(solution)/shard_map/ppermute | solution.py:361
  (44 shorter events, 10.3 us)
Async XLA Ops:
  0.6 24.2 %copy-start.1 = (s32[32,2]{0,1:T(2,128)S(1)}, s32[32,2]{0,1:T(2,128)}, u32[]{:S(2)}) copy-start(s32[32,2]{0,1:T(2,128)} %param.5) | copy-start | bytes 772
  2.6 10.1 %collective-permute-start.4 = (bf16[1024,128]{1,0:T(8,128)(2,1)}, bf16[1024,128]{1,0:T(8,128)(2,1)S(1)}, u32[]{:S(2)}, u32[]{:S(2)}) collective-permute-start(bf16[1024,128]{1,0:T(8,128)(2,1)} %get-tuple-element.34.refs_0_.refs_7_), channel_id=1, source_target_pairs={{0,96},{32,0},{64,32},{96,64},{1,97},{33,1},{65,33},{97,65},{2,98}... | collective-permute-start | bytes 786440 | tf_op jit(solution)/shard_map/ppermute | solution.py:361
  6.8 9.2 %collective-permute-start.3 = (bf16[1024,128]{1,0:T(8,128)(2,1)}, bf16[1024,128]{1,0:T(8,128)(2,1)S(1)}, u32[]{:S(2)}, u32[]{:S(2)}) collective-permute-start(bf16[1024,128]{1,0:T(8,128)(2,1)} %get-tuple-element.34.refs_0_.refs_7_), channel_id=1, source_target_pairs={{0,32},{32,64},{64,96},{96,0},{1,33},{33,65},{65,97},{97,1},{2,34}... | collective-permute-start | bytes 786440 | tf_op jit(solution)/shard_map/ppermute | solution.py:361
  6.8 14.2 %collective-permute-start.2 = (bf16[1024,128]{1,0:T(8,128)(2,1)}, bf16[1024,128]{1,0:T(8,128)(2,1)S(1)}, u32[]{:S(2)}, u32[]{:S(2)}) collective-permute-start(bf16[1024,128]{1,0:T(8,128)(2,1)} %get-tuple-element.32), channel_id=1, source_target_pairs={{0,24},{8,0},{16,8},{24,16},{1,25},{9,1},{17,9},{25,17},{2,26},{10... | collective-permute-start | bytes 786440 | tf_op jit(solution)/shard_map/ppermute | solution.py:361
  9.8 11.2 %collective-permute-start.1 = (bf16[1024,128]{1,0:T(8,128)(2,1)}, bf16[1024,128]{1,0:T(8,128)(2,1)S(1)}, u32[]{:S(2)}, u32[]{:S(2)}) collective-permute-start(bf16[1024,128]{1,0:T(8,128)(2,1)} %get-tuple-element.32), channel_id=1, source_target_pairs={{0,16},{8,24},{16,0},{24,8},{1,17},{9,25},{17,1},{25,9},{2,18},{10... | collective-permute-start | bytes 786440 | tf_op jit(solution)/shard_map/ppermute | solution.py:361
  10.4 14.2 %collective-permute-start = (bf16[1024,128]{1,0:T(8,128)(2,1)}, bf16[1024,128]{1,0:T(8,128)(2,1)S(1)}, u32[]{:S(2)}, u32[]{:S(2)}) collective-permute-start(bf16[1024,128]{1,0:T(8,128)(2,1)} %get-tuple-element.32), channel_id=1, source_target_pairs={{0,8},{8,16},{16,24},{24,0},{1,9},{9,17},{17,25},{25,1},{2,10},{10... | collective-permute-start | bytes 786440 | tf_op jit(solution)/shard_map/ppermute | solution.py:361
  16.0 8.7 %collective-permute-start.5 = (bf16[1024,128]{1,0:T(8,128)(2,1)}, bf16[1024,128]{1,0:T(8,128)(2,1)S(1)}, u32[]{:S(2)}, u32[]{:S(2)}) collective-permute-start(bf16[1024,128]{1,0:T(8,128)(2,1)} %get-tuple-element.34.refs_0_.refs_7_), channel_id=1, source_target_pairs={{0,64},{32,96},{64,0},{96,32},{1,65},{33,97},{65,1},{97,33},{2,66}... | collective-permute-start | bytes 786440 | tf_op jit(solution)/shard_map/ppermute | solution.py:361
  24.8 4.1 %collective-permute-start.6 = (bf16[4096,128]{1,0:T(8,128)(2,1)S(1)}, bf16[4096,128]{1,0:T(8,128)(2,1)S(1)}, u32[]{:S(2)}, u32[]{:S(2)}) collective-permute-start(bf16[4096,128]{1,0:T(8,128)(2,1)S(1)} %constant_dynamic-update-slice_fusion), channel_id=1, source_target_pairs={{0,4},{4,0},{1,5},{5,1},{2,6},{6,2},{3,7},{7,3},{8,12},{12,8},{9,1... | collective-permute-start | bytes 3145736 | tf_op jit(solution)/shard_map/ppermute | solution.py:369
  32.7 1.4 %collective-permute-start.7 = (f32[2,16,256]{2,1,0:T(8,128)S(1)}, f32[2,16,256]{2,1,0:T(8,128)S(1)}, u32[]{:S(2)}, u32[]{:S(2)}) collective-permute-start(f32[2,16,256]{2,1,0:T(8,128)S(1)} %stats.3), channel_id=1, source_target_pairs={{0,4},{4,0},{1,5},{5,1},{2,6},{6,2},{3,7},{7,3},{8,12},{12,8},{9,1... | collective-permute-start | bytes 98312 | tf_op jit(solution)/shard_map/ppermute | solution.py:369
  34.2 4.6 %collective-permute-start.10 = (f32[2,16,256]{2,1,0:T(8,128)S(1)}, f32[2,16,256]{2,1,0:T(8,128)S(1)}, u32[]{:S(2)}, u32[]{:S(2)}) collective-permute-start(f32[2,16,256]{2,1,0:T(8,128)S(1)} %pad_maximum_fusion.refs_1_), channel_id=1, source_target_pairs={{0,24},{8,0},{16,8},{24,16},{1,25},{9,1},{17,9},{25,17},{2,26},{10... | collective-permute-start | bytes 98312 | tf_op jit(solution)/shard_map/ppermute | solution.py:361
  37.2 5.4 %collective-permute-start.9 = (f32[2,16,256]{2,1,0:T(8,128)S(1)}, f32[2,16,256]{2,1,0:T(8,128)S(1)}, u32[]{:S(2)}, u32[]{:S(2)}) collective-permute-start(f32[2,16,256]{2,1,0:T(8,128)S(1)} %pad_maximum_fusion.refs_1_), channel_id=1, source_target_pairs={{0,16},{8,24},{16,0},{24,8},{1,17},{9,25},{17,1},{25,9},{2,18},{10... | collective-permute-start | bytes 98312 | tf_op jit(solution)/shard_map/ppermute | solution.py:361
  37.8 5.1 %collective-permute-start.8 = (f32[2,16,256]{2,1,0:T(8,128)S(1)}, f32[2,16,256]{2,1,0:T(8,128)S(1)}, u32[]{:S(2)}, u32[]{:S(2)}) collective-permute-start(f32[2,16,256]{2,1,0:T(8,128)S(1)} %pad_maximum_fusion.refs_1_), channel_id=1, source_target_pairs={{0,8},{8,16},{16,24},{24,0},{1,9},{9,17},{17,25},{25,1},{2,10},{10... | collective-permute-start | bytes 98312 | tf_op jit(solution)/shard_map/ppermute | solution.py:361
  46.7 8.3 %collective-permute-start.11 = (bf16[512,128]{1,0:T(8,128)(2,1)S(1)}, bf16[512,128]{1,0:T(8,128)(2,1)S(1)}, u32[]{:S(2)}, u32[]{:S(2)}) collective-permute-start(bf16[512,128]{1,0:T(8,128)(2,1)S(1)} %get-tuple-element.47), channel_id=1, source_target_pairs={{0,96},{32,0},{64,32},{96,64},{1,97},{33,1},{65,33},{97,65},{2,98}... | collective-permute-start | bytes 393224 | tf_op jit(solution)/shard_map/ppermute | solution.py:365
  47.6 7.4 %collective-permute-start.12 = (bf16[512,128]{1,0:T(8,128)(2,1)S(1)}, bf16[512,128]{1,0:T(8,128)(2,1)S(1)}, u32[]{:S(2)}, u32[]{:S(2)}) collective-permute-start(bf16[512,128]{1,0:T(8,128)(2,1)S(1)} %get-tuple-element.48), channel_id=1, source_target_pairs={{0,32},{32,64},{64,96},{96,0},{1,33},{33,65},{65,97},{97,1},{2,34}... | collective-permute-start | bytes 393224 | tf_op jit(solution)/shard_map/ppermute | solution.py:365
  55.0 6.6 %collective-permute-start.13 = (bf16[1024,128]{1,0:T(8,128)(2,1)S(1)}, bf16[1024,128]{1,0:T(8,128)(2,1)S(1)}, u32[]{:S(2)}, u32[]{:S(2)}) collective-permute-start(bf16[1024,128]{1,0:T(8,128)(2,1)S(1)} %get-tuple-element.49), channel_id=1, source_target_pairs={{0,96},{32,0},{64,32},{96,64},{1,97},{33,1},{65,33},{97,65},{2,98}... | collective-permute-start | bytes 786440 | tf_op jit(solution)/shard_map/ppermute | solution.py:365
  57.1 7.8 %collective-permute-start.14 = (bf16[1024,128]{1,0:T(8,128)(2,1)S(1)}, bf16[1024,128]{1,0:T(8,128)(2,1)S(1)}, u32[]{:S(2)}, u32[]{:S(2)}) collective-permute-start(bf16[1024,128]{1,0:T(8,128)(2,1)S(1)} %get-tuple-element.50), channel_id=1, source_target_pairs={{0,32},{32,64},{64,96},{96,0},{1,33},{33,65},{65,97},{97,1},{2,34}... | collective-permute-start | bytes 786440 | tf_op jit(solution)/shard_map/ppermute | solution.py:365
  65.1 4.6 %collective-permute-start.18 = (bf16[8,128,256]{2,1,0:T(8,128)(2,1)S(1)}, bf16[8,128,256]{2,1,0:T(8,128)(2,1)S(1)}, u32[]{:S(2)}, u32[]{:S(2)}) collective-permute-start(bf16[8,128,256]{2,1,0:T(8,128)(2,1)S(1)} %get-tuple-element.53), channel_id=1, source_target_pairs={{0,4},{4,0},{1,5},{5,1},{2,6},{6,2},{3,7},{7,3},{8,12},{12,8},{9,1... | collective-permute-start | bytes 1572872 | tf_op jit(solution)/shard_map/ppermute | solution.py:369
  65.1 14.7 %collective-permute-start.17 = (bf16[1024,128]{1,0:T(8,128)(2,1)S(1)}, bf16[1024,128]{1,0:T(8,128)(2,1)S(1)}, u32[]{:S(2)}, u32[]{:S(2)}) collective-permute-start(bf16[1024,128]{1,0:T(8,128)(2,1)S(1)} %middle.1.sum_ref), channel_id=1, source_target_pairs={{0,3},{1,0},{2,1},{3,2},{4,7},{5,4},{6,5},{7,6},{8,11},{9,8},{10,9... | collective-permute-start | bytes 786440 | tf_op jit(solution)/shard_map/ppermute | solution.py:361
  68.0 11.8 %collective-permute-start.16 = (bf16[1024,128]{1,0:T(8,128)(2,1)S(1)}, bf16[1024,128]{1,0:T(8,128)(2,1)S(1)}, u32[]{:S(2)}, u32[]{:S(2)}) collective-permute-start(bf16[1024,128]{1,0:T(8,128)(2,1)S(1)} %middle.1.sum_ref), channel_id=1, source_target_pairs={{0,2},{1,3},{2,0},{3,1},{4,6},{5,7},{6,4},{7,5},{8,10},{9,11},{10,... | collective-permute-start | bytes 786440 | tf_op jit(solution)/shard_map/ppermute | solution.py:361
  68.8 14.7 %collective-permute-start.15 = (bf16[1024,128]{1,0:T(8,128)(2,1)S(1)}, bf16[1024,128]{1,0:T(8,128)(2,1)S(1)}, u32[]{:S(2)}, u32[]{:S(2)}) collective-permute-start(bf16[1024,128]{1,0:T(8,128)(2,1)S(1)} %middle.1.sum_ref), channel_id=1, source_target_pairs={{0,1},{1,2},{2,3},{3,0},{4,5},{5,6},{6,7},{7,4},{8,9},{9,10},{10,1... | collective-permute-start | bytes 786440 | tf_op jit(solution)/shard_map/ppermute | solution.py:361
  69.8 4.3 %collective-permute-start.19 = (bf16[128,256]{1,0:T(8,128)(2,1)S(1)}, bf16[128,256]{1,0:T(8,128)(2,1)S(1)}, u32[]{:S(2)}, u32[]{:S(2)}) collective-permute-start(bf16[128,256]{1,0:T(8,128)(2,1)S(1)} %get-tuple-element.57), channel_id=1, source_target_pairs={{0,24},{8,0},{16,8},{24,16},{1,25},{9,1},{17,9},{25,17},{2,26},{10... | collective-permute-start | bytes 196616 | tf_op jit(solution)/shard_map/ppermute | solution.py:365
  71.6 5.5 %collective-permute-start.20 = (bf16[128,256]{1,0:T(8,128)(2,1)S(1)}, bf16[128,256]{1,0:T(8,128)(2,1)S(1)}, u32[]{:S(2)}, u32[]{:S(2)}) collective-permute-start(bf16[128,256]{1,0:T(8,128)(2,1)S(1)} %get-tuple-element.58), channel_id=1, source_target_pairs={{0,8},{8,16},{16,24},{24,0},{1,9},{9,17},{17,25},{25,1},{2,10},{10... | collective-permute-start | bytes 196616 | tf_op jit(solution)/shard_map/ppermute | solution.py:365
  77.1 6.3 %collective-permute-start.21 = (bf16[2,128,256]{2,1,0:T(8,128)(2,1)S(1)}, bf16[2,128,256]{2,1,0:T(8,128)(2,1)S(1)}, u32[]{:S(2)}, u32[]{:S(2)}) collective-permute-start(bf16[2,128,256]{2,1,0:T(8,128)(2,1)S(1)} %get-tuple-element.59), channel_id=1, source_target_pairs={{0,24},{8,0},{16,8},{24,16},{1,25},{9,1},{17,9},{25,17},{2,26},{10... | collective-permute-start | bytes 393224 | tf_op jit(solution)/shard_map/ppermute | solution.py:365
  77.2 6.2 %collective-permute-start.22 = (bf16[2,128,256]{2,1,0:T(8,128)(2,1)S(1)}, bf16[2,128,256]{2,1,0:T(8,128)(2,1)S(1)}, u32[]{:S(2)}, u32[]{:S(2)}) collective-permute-start(bf16[2,128,256]{2,1,0:T(8,128)(2,1)S(1)} %get-tuple-element.60), channel_id=1, source_target_pairs={{0,8},{8,16},{16,24},{24,0},{1,9},{9,17},{17,25},{25,1},{2,10},{10... | collective-permute-start | bytes 393224 | tf_op jit(solution)/shard_map/ppermute | solution.py:365
  (1 other events, 22.4 us)
